TPU v7x, 32 devices: a whole 2x2x4 slice. The times are simulated.
32 devices in a mesh: dp: 4 (over x, core), mp: 8 (over z, y).
Axes of the slice: x: 2, y: 2, z: 4, core: 2. Of those that a mesh axis runs over, the one named last changes fastest.
Arguments:
- queries: bfloat16 [2048, 1024], P('dp', 'mp'), may hold values from -6 to 6
- keys: bfloat16 [2048, 1024], P('dp', 'mp'), may hold values from -6 to 6
- values: bfloat16 [2048, 1024], P('dp', 'mp'), may hold values from -6 to 6
- w_out: bfloat16 [1024, 6144], P('mp', 'dp'), may hold values from -0.1875 to 0.1875
- cotangent: bfloat16 [2048, 6144], P(('dp', 'mp')), may hold values from -6 to 6
Outputs:
- grad_queries: bfloat16 [2048, 1024], P('dp', 'mp')
- grad_keys: bfloat16 [2048, 1024], P('dp', 'mp')
- grad_values: bfloat16 [2048, 1024], P('dp', 'mp')
- grad_weight: bfloat16 [1024, 6144], P('mp', 'dp')
All inputs are finite; a program needn't handle non-finite values.
Results may differ from a plain program's by a relative error of at most 0.022.
Values may be sent and summed in bfloat16 or wider, within the bound.
No kernel may reach another device: no remote copies, remote signals or barrier semaphores. Data moves between devices by JAX's collectives and lax.ppermute only.
A program may use at most 64 MiB of HBM per device.

v0:
```python
import jax
import jax.numpy as jnp
from jax import lax
from jax.sharding import PartitionSpec as P

HD = 128
PATCH = 256


def forward_attention(queries, keys, values):
    images = queries.shape[0] // PATCH
    heads_here = queries.shape[1] // HD
    shape_four = (images, PATCH, heads_here, HD)
    scale = HD ** (-0.5)
    query_four = queries.reshape(shape_four)
    key_four = keys.reshape(shape_four)
    value_four = values.reshape(shape_four)
    scores = (
        jnp.einsum("iqhd,ikhd->ihqk", query_four, key_four, preferred_element_type=jnp.float32)
        * scale
    )
    attention = jax.nn.softmax(scores, axis=-1)
    rounded = attention.astype(jnp.bfloat16)
    attended = jnp.einsum(
        "ihqk,ikhd->iqhd", rounded, value_four, preferred_element_type=jnp.float32
    ).astype(jnp.bfloat16)
    return (attended.reshape(queries.shape), attention, rounded)


def backward_attention(queries, keys, values, d_att, attention, rounded):
    images = queries.shape[0] // PATCH
    heads_here = queries.shape[1] // HD
    shape_four = (images, PATCH, heads_here, HD)
    scale = HD ** (-0.5)
    query_four = queries.reshape(shape_four)
    key_four = keys.reshape(shape_four)
    value_four = values.reshape(shape_four)
    grad_four = d_att.reshape(shape_four)
    dprob = jnp.einsum("iqhd,ikhd->ihqk", grad_four, value_four, preferred_element_type=jnp.float32)
    delta = jnp.sum(attention * dprob, axis=-1, keepdims=True)
    dscore = (attention * (dprob - delta) * scale).astype(jnp.bfloat16)
    grad_q = jnp.einsum(
        "ihqk,ikhd->iqhd", dscore, key_four, preferred_element_type=jnp.float32
    ).astype(jnp.bfloat16)
    grad_k = jnp.einsum(
        "ihqk,iqhd->ikhd", dscore, query_four, preferred_element_type=jnp.float32
    ).astype(jnp.bfloat16)
    grad_v = jnp.einsum(
        "ihqk,iqhd->ikhd", rounded, grad_four, preferred_element_type=jnp.float32
    ).astype(jnp.bfloat16)
    return (
        grad_q.reshape(queries.shape),
        grad_k.reshape(queries.shape),
        grad_v.reshape(queries.shape),
    )


def on_device(queries, keys, values, w_out, cotangent):
    attended, attention, rounded = forward_attention(queries, keys, values)
    cot_full = lax.all_gather(cotangent, "mp", axis=0, tiled=True)
    d_full = lax.dot_general(
        cot_full,
        lax.all_gather(w_out, "dp", axis=1, tiled=True),
        (((1,), (1,)), ((), ())),
        preferred_element_type=jnp.float32,
    )
    grad_part = lax.dot_general(
        attended, cot_full, (((0,), (0,)), ((), ())), preferred_element_type=jnp.float32
    )
    d_att = d_full.astype(jnp.bfloat16)
    grad_q, grad_k, grad_v = backward_attention(queries, keys, values, d_att, attention, rounded)
    grad_weight = lax.psum_scatter(
        grad_part.astype(jnp.bfloat16), "dp", scatter_dimension=1, tiled=True
    )
    return (grad_q, grad_k, grad_v, grad_weight)


def solution(mesh):
    in_specs = (P("dp", "mp"), P("dp", "mp"), P("dp", "mp"), P("mp", "dp"), P(("dp", "mp"), None))
    out_specs = (P("dp", "mp"), P("dp", "mp"), P("dp", "mp"), P("mp", "dp"))
    return jax.shard_map(
        on_device, mesh=mesh, in_specs=in_specs, out_specs=out_specs, check_vma=False
    )
```

profile of v0, /device:TPU:0, one launch (start us, length us, event | category | flops | bytes accessed | tf_op | source)
XLA Modules:
  0.0 169.2 jit_solution(6927843350712538059)
XLA Ops:
  7.2 0.0 copy-start
  7.2 0.0 all-gather.3.cloned.1.call-start
  7.2 0.7 all-gather.3.cloned.1.call-update
  7.9 0.0 all-gather.5.cloned.1.call-start
  8.0 0.7 all-gather.5.cloned.1.call-update
  8.7 0.0 reduce-scatter.2.cloned.1.call-start
  8.7 0.0 copy-done
  8.7 1.3 fusion.23
  10.0 1.5 convolution_convert_fusion.1
  11.5 100.4 %all-gather.3.cloned.1.call-done = bf16[512,6144]{1,0:T(8,128)(2,1)} async-done(((bf16[64,6144]{1,0:T(8,128)(2,1)}), bf16[512,6144]{1,0:T(8,128)(2,1)}) %all-gather.3.cloned.1.call-update) | async-done | bytes 6291472 | tf_op jit(solution)/shard_map/all_gather | solution.py:60
  112.0 5.0 %convolution_convert_fusion = bf16[128,6144]{1,0:T(8,128)(2,1)} fusion(bf16[512,128]{1,0:T(8,128)(2,1)S(1)} %bitcast.50, bf16[512,6144]{1,0:T(8,128)(2,1)} %all-gather.3.cloned.1.call-done), kind=kOutput, calls=%fused_computation.2 | convolution fusion | flops 806092800 | bytes 7995392 | tf_op jit(solution)/shard_map/dot_general | solution.py:67
  117.0 0.0 copy-start.2
  117.0 0.0 copy-start.1
  117.0 0.0 reduce-scatter.2.cloned.1.call-update
  117.0 14.4 %all-gather.5.cloned.1.call-done = bf16[128,6144]{1,0:T(8,128)(2,1)} async-done(((bf16[128,1536]{1,0:T(8,128)(2,1)}), bf16[128,6144]{1,0:T(8,128)(2,1)}) %all-gather.5.cloned.1.call-update) | async-done | bytes 1572880 | tf_op jit(solution)/shard_map/all_gather | solution.py:63
  131.4 5.0 %convolution_convert_fusion.5 = bf16[512,128]{1,0:T(8,128)(2,1)S(1)} fusion(bf16[512,6144]{1,0:T(8,128)(2,1)} %all-gather.3.cloned.1.call-done, bf16[128,6144]{1,0:T(8,128)(2,1)} %all-gather.5.cloned.1.call-done), kind=kOutput, calls=%fused_computation.14 | convolution fusion | flops 805371904 | bytes 7995392 | tf_op jit(solution)/shard_map/dot_general | solution.py:61
  136.4 0.0 copy-done.2
  136.4 0.5 fusion.8
  137.0 0.8 copy.16
  137.7 0.0 copy-done.1
  137.7 0.2 fusion.24
  138.0 1.0 convolution_convert_fusion.3
  138.9 1.0 convolution_convert_fusion.4
  139.9 22.7 %reduce-scatter.2.cloned.1.call-done = bf16[128,1536]{1,0:T(8,128)(2,1)} async-done(((bf16[128,6144]{1,0:T(8,128)(2,1)}), bf16[128,1536]{1,0:T(8,128)(2,1)}) %reduce-scatter.2.cloned.1.call-update) | async-done | bytes 393232 | tf_op jit(solution)/shard_map/reduce_scatter | solution.py:72
Async XLA Ops:
  7.2 1.5 copy-start
  7.2 104.8 %all-gather.3.cloned.1.call-start = ((), (), s32[]{:S(2)}) async-start(), calls=%async_computation.1 | async-start | bytes 7077888 | tf_op jit(solution)/shard_map/all_gather | solution.py:60
  7.9 123.5 %all-gather.5.cloned.1.call-start = ((), (), s32[]{:S(2)}) async-start(), calls=%async_computation.2 | async-start | bytes 1966080 | tf_op jit(solution)/shard_map/all_gather | solution.py:63
  8.7 154.0 %reduce-scatter.2.cloned.1.call-start = ((), (), s32[]{:S(2)}) async-start(), calls=%async_computation.3 | async-start | bytes 1966080 | tf_op jit(solution)/shard_map/reduce_scatter | solution.py:72
  117.0 19.4 %copy-start.2 = (bf16[512,128]{1,0:T(8,128)(2,1)S(1)}, bf16[512,128]{1,0:T(8,128)(2,1)}, u32[]{:S(2)}) copy-start(bf16[512,128]{1,0:T(8,128)(2,1)} %param.6) | copy-start | bytes 393220
  117.0 20.7 %copy-start.1 = (bf16[512,128]{1,0:T(8,128)(2,1)S(1)}, bf16[512,128]{1,0:T(8,128)(2,1)}, u32[]{:S(2)}) copy-start(bf16[512,128]{1,0:T(8,128)(2,1)} %param.7) | copy-start | bytes 393220
Sparse Core Ops, SparseCore 0:
  10.2 101.7 all-gather.2
  113.5 17.8 all-gather.4
  134.5 28.1 reduce-scatter.1
where the time goes:
time: 169 us
  waiting for transfers between devices  139 us (82%)
  matrix products  15.6 us (9%)
  between operations  13.8 us (8%)
    all_gather x1, waiting for transfers between devices, on_device(): cot_full = lax.all_gather(cotangent, 'mp', axis=0, tiled=True)  100 us
    reduce_scatter x1, waiting for transfers between devices, on_device(): lax.psum_scatter(grad_part.astype(jnp.bfloat16), 'dp', scatter_dimension=...  22.7 us
    all_gather x1, waiting for transfers between devices, on_device(): lax.all_gather(w_out, 'dp', axis=1, tiled=True)  14.4 us
    dot_general x1, matrix products, on_device(): lax.dot_general(attended, cot_full, (((0,), (0,)), ((), ())), preferred_e...  5.04 us
    dot_general x1, matrix products, on_device(): lax.dot_general(cot_full, lax.all_gather(w_out, 'dp', axis=1, tiled=True)...  5.01 us
  transfers between devices with their start and end apart: 3, of which 3 were waited for; matrix products, arithmetic and copies ran while one was open for 10% of the time, Pallas kernels for 0%

commit v1 on v0

--- a/solution.py
+++ b/solution.py
@@ -1,10 +1,19 @@
+import functools
+
 import jax
 import jax.numpy as jnp
 from jax import lax
+from jax.experimental import pallas as pl
+from jax.experimental.pallas import tpu as pltpu
 from jax.sharding import PartitionSpec as P
 
 HD = 128
 PATCH = 256
+AXES = ("dp", "mp")
+ANY = pl.BlockSpec(memory_space=pl.ANY)
+VMEM = pl.BlockSpec(memory_space=pltpu.VMEM)
+F32 = jnp.float32
+BF16 = jnp.bfloat16
 
 
 def forward_attention(queries, keys, values):
@@ -75,9 +84,258 @@
     return (grad_q, grad_k, grad_v, grad_weight)
 
 
+def flip(x=0, c=0, z1=0, z0=0, y=0):
+    mask = (x * 2 + c) * 8 + z1 * 4 + z0 * 2 + y
+    return [(i, i ^ mask) for i in range(32)]
+
+
+def send(value, **bits):
+    return lax.ppermute(value, AXES, flip(**bits))
+
+
+def place():
+    dp, mp = lax.axis_index("dp"), lax.axis_index("mp")
+    return {"x": dp // 2, "c": dp % 2, "z1": mp // 4, "z0": (mp // 2) % 2, "y": mp % 2}
+
+
+def aligned(index, unit):
+    return pl.multiple_of(index * unit, unit)
+
+
+def pack_kernel(cuts, cot, *rest):
+    outs, sems = rest[:-1], rest[-1]
+    x = place()["x"]
+    quarter = cot.shape[1] // 4
+    copies = []
+    for n, (low, high) in enumerate(cuts):
+        for other in range(2):
+            half = 1 - x if other else x
+            for c in range(2):
+                start = pl.multiple_of(half * (2 * quarter) + (c * quarter + low), 128)
+                width = high - low
+                copies.append(
+                    pltpu.make_async_copy(
+                        cot.at[:, pl.ds(start, width)],
+                        outs[2 * n + other].at[:, pl.ds(c * width, width)],
+                        sems.at[len(copies)],
+                    )
+                )
+    for copy in copies:
+        copy.start()
+    for copy in copies:
+        copy.wait()
+
+
+def pack(cot, cuts):
+    shapes = []
+    for low, high in cuts:
+        shapes += [jax.ShapeDtypeStruct((cot.shape[0], 2 * (high - low)), cot.dtype)] * 2
+    return pl.pallas_call(
+        functools.partial(pack_kernel, cuts),
+        out_shape=shapes,
+        in_specs=[ANY],
+        out_specs=[ANY] * len(shapes),
+        scratch_shapes=[pltpu.SemaphoreType.DMA((4 * len(cuts),))],
+        cost_estimate=pl.CostEstimate(flops=0, bytes_accessed=2 * cot.size * 2, transcendentals=0),
+        name="pack",
+    )(cot)
+
+
+def dot(a, b, over):
+    return lax.dot_general(a, b, ((over[0], over[1]), ((), ())), preferred_element_type=F32)
+
+
+def forward_kernel(q, k, v, probs, mine, others, held):
+    z0 = place()["z0"]
+    half = PATCH // 2
+    for i in range(q.shape[0] // PATCH):
+        rows = pl.ds(i * PATCH, PATCH)
+        scores = dot(k[rows], q[rows], ((1,), (1,))) * (HD**-0.5)
+        top = jnp.max(scores, axis=0, keepdims=True)
+        raised = jnp.exp(scores - top)
+        attention = raised / jnp.sum(raised, axis=0, keepdims=True)
+        probs[i] = attention
+        held[...] = dot(attention.astype(BF16), v[rows], ((0,), (0,))).astype(BF16)
+        mine[pl.ds(i * half, half)] = held[pl.ds(aligned(z0, half), half)]
+        others[pl.ds(i * half, half)] = held[pl.ds(aligned(1 - z0, half), half)]
+
+
+def forward(q, k, v):
+    images = q.shape[0] // PATCH
+    half = jax.ShapeDtypeStruct((q.shape[0] // 2, HD), BF16)
+    return pl.pallas_call(
+        forward_kernel,
+        out_shape=[jax.ShapeDtypeStruct((images, PATCH, PATCH), F32), half, half],
+        in_specs=[VMEM] * 3,
+        out_specs=[VMEM] * 3,
+        scratch_shapes=[pltpu.VMEM((PATCH, HD), BF16)],
+        cost_estimate=pl.CostEstimate(
+            flops=4 * images * PATCH * PATCH * HD,
+            bytes_accessed=1 << 20,
+            transcendentals=images * PATCH * PATCH,
+        ),
+        name="forward",
+    )(q, k, v)
+
+
+def backward_kernel(q, k, v, probs, own, from_x, from_z, from_xz, gq, gk, gv, held):
+    z0 = place()["z0"]
+    half = PATCH // 2
+    mine = (own[...] + from_x[...].astype(F32)).astype(BF16)
+    others = (from_z[...].astype(F32) + from_xz[...].astype(F32)).astype(BF16)
+    for i in range(q.shape[0] // PATCH):
+        held[i, pl.ds(aligned(z0, half), half)] = mine[i * half : (i + 1) * half]
+        held[i, pl.ds(aligned(1 - z0, half), half)] = others[i * half : (i + 1) * half]
+    for i in range(q.shape[0] // PATCH):
+        rows = pl.ds(i * PATCH, PATCH)
+        attention, d_att = probs[i], held[i]
+        dprob = dot(v[rows], d_att, ((1,), (1,)))
+        delta = jnp.sum(attention * dprob, axis=0, keepdims=True)
+        dscore = (attention * (dprob - delta) * (HD**-0.5)).astype(BF16)
+        gv[rows] = dot(attention.astype(BF16), d_att, ((1,), (0,))).astype(BF16)
+        gk[rows] = dot(dscore, q[rows], ((1,), (0,))).astype(BF16)
+        gq[rows] = dot(dscore, k[rows], ((0,), (0,))).astype(BF16)
+
+
+def backward(q, k, v, probs, own, from_x, from_z, from_xz):
+    images = q.shape[0] // PATCH
+    return pl.pallas_call(
+        backward_kernel,
+        out_shape=[jax.ShapeDtypeStruct(q.shape, BF16)] * 3,
+        in_specs=[VMEM] * 8,
+        out_specs=[VMEM] * 3,
+        scratch_shapes=[pltpu.VMEM((images, PATCH, HD), BF16)],
+        cost_estimate=pl.CostEstimate(
+            flops=8 * images * PATCH * PATCH * HD, bytes_accessed=2 << 20, transcendentals=0
+        ),
+        name="backward",
+    )(q, k, v, probs, own, from_x, from_z, from_xz)
+
+
+def products_kernel(low, high, first, last, *refs):
+    refs = list(refs)
+    blocks = [refs.pop(0) for _ in range(8)]
+    w_refs = [refs.pop(0) for _ in range(4)]
+    att = [refs.pop(0) for _ in range(4)]
+    before = None if first else refs.pop(0)
+    keep, give = refs.pop(0), refs.pop(0)
+    d_refs = [refs.pop(0) for _ in range(4 if last else 1)]
+    c_held, w_held, g_held, sems = refs
+    at = place()
+    width = high - low
+    copies = []
+    for n, block in enumerate(blocks):
+        group, z1, y = n // 4, (n // 2) % 2, n % 2
+        z1 = 1 - at["z1"] if z1 else at["z1"]
+        y = 1 - at["y"] if y else at["y"]
+        row = pl.multiple_of(group * 256 + z1 * 128 + y * 64, 64)
+        copies.append(pltpu.make_async_copy(block, c_held.at[pl.ds(row, 64)], sems.at[n]))
+    for n, w in enumerate(w_refs):
+        c = 1 - at["c"] if n // 2 else at["c"]
+        copies.append(
+            pltpu.make_async_copy(
+                w.at[:, pl.ds(low, width)],
+                w_held.at[pl.ds((n % 2) * HD, HD), pl.ds(pl.multiple_of(c * width, 128), width)],
+                sems.at[8 + n],
+            )
+        )
+    for copy in copies:
+        copy.start()
+    attended = jnp.concatenate(
+        [
+            jnp.concatenate([att[0][...], att[2][...]], axis=1),
+            jnp.concatenate([att[1][...], att[3][...]], axis=1),
+        ],
+        axis=0,
+    )
+    for copy in copies:
+        copy.wait()
+    g_held[...] = dot(attended, c_held[...], ((0,), (0,)))
+    keep[...] = g_held[:, pl.ds(pl.multiple_of(at["c"] * width, 128), width)]
+    give[...] = g_held[:, pl.ds(pl.multiple_of((1 - at["c"]) * width, 128), width)].astype(BF16)
+    d = dot(c_held[...], w_held[...], ((1,), (1,)))
+    if not first:
+        d = d + before[...]
+    if not last:
+        d_refs[0][...] = d
+    else:
+        d_refs[0][...] = d[:256, :HD]
+        d_refs[1][...] = d[256:, :HD].astype(BF16)
+        d_refs[2][...] = d[:256, HD:].astype(BF16)
+        d_refs[3][...] = d[256:, HD:].astype(BF16)
+
+
+def products(low, high, blocks, w_all, att, before, last):
+    width = high - low
+    first = before is None
+    out = [
+        jax.ShapeDtypeStruct((2 * HD, width), F32),
+        jax.ShapeDtypeStruct((2 * HD, width), BF16),
+    ]
+    if last:
+        out.append(jax.ShapeDtypeStruct((256, HD), F32))
+        out += [jax.ShapeDtypeStruct((256, HD), BF16)] * 3
+    else:
+        out.append(jax.ShapeDtypeStruct((512, 2 * HD), F32))
+    extra = [] if first else [before]
+    return pl.pallas_call(
+        functools.partial(products_kernel, low, high, first, last),
+        out_shape=out,
+        in_specs=[ANY] * 12 + [VMEM] * (4 + len(extra)),
+        out_specs=[VMEM] * len(out),
+        scratch_shapes=[
+            pltpu.VMEM((512, 2 * width), BF16),
+            pltpu.VMEM((2 * HD, 2 * width), BF16),
+            pltpu.VMEM((2 * HD, 2 * width), F32),
+            pltpu.SemaphoreType.DMA((12,)),
+        ],
+        cost_estimate=pl.CostEstimate(
+            flops=4 * 512 * 2 * HD * 2 * width,
+            bytes_accessed=512 * 2 * width * 2 + 2 * HD * 2 * width * 6,
+            transcendentals=0,
+        ),
+        name="products",
+    )(*blocks, *w_all, *att, *extra)
+
+
+CUTS = ((0, 1024), (1024, 1536))
+
+
+def on_device_4x8(queries, keys, values, w_out, cotangent):
+    packed = pack(cotangent, CUTS)
+    gathered = []
+    for n in range(len(CUTS)):
+        m, o = packed[2 * n], packed[2 * n + 1]
+        za, zb = send(m, z1=1), send(o, x=1, z1=1)
+        ya, xo, yb = send(m, y=1), send(o, x=1), send(o, x=1, y=1)
+        gathered.append([m, ya, za, send(za, y=1), xo, yb, zb, send(zb, y=1)])
+    w_pair = send(w_out, z0=1)
+    w_all = [w_out, w_pair, send(w_out, c=1), send(w_pair, c=1)]
+    probs, mine, others = forward(queries, keys, values)
+    att = [mine, send(mine, x=1), send(others, z0=1), send(others, x=1, z0=1)]
+    before, parts = None, []
+    for n, (low, high) in enumerate(CUTS):
+        last = n == len(CUTS) - 1
+        keep, give, *d = products(low, high, gathered[n], w_all, att, before, last)
+        before = d[0]
+        total = keep + send(give, c=1).astype(F32)
+        pair = send(total[HD:].astype(BF16), z0=1)
+        parts.append((total[:HD] + pair.astype(F32)).astype(BF16))
+    own, to_x, to_z, to_xz = d
+    grad_q, grad_k, grad_v = backward(
+        queries, keys, values, probs, own, send(to_x, x=1), send(to_z, z0=1), send(to_xz, x=1, z0=1)
+    )
+    return grad_q, grad_k, grad_v, jnp.concatenate(parts, axis=1)
+
+
 def solution(mesh):
     in_specs = (P("dp", "mp"), P("dp", "mp"), P("dp", "mp"), P("mp", "dp"), P(("dp", "mp"), None))
     out_specs = (P("dp", "mp"), P("dp", "mp"), P("dp", "mp"), P("mp", "dp"))
+    small = mesh.shape["dp"] == 4 and mesh.shape["mp"] == 8
     return jax.shard_map(
-        on_device, mesh=mesh, in_specs=in_specs, out_specs=out_specs, check_vma=False
-    )
+        on_device_4x8 if small else on_device,
+        mesh=mesh,
+        in_specs=in_specs,
+        out_specs=out_specs,
+        check_vma=False,
+    )

time: 169 us -> 125 us (0.74)
  waiting for transfers between devices: 139 us -> 44.5 us
  Pallas kernels: 0 us -> 39.9 us
  starting transfers between devices: 0.11 us -> 35.4 us
  matrix products: 15.6 us -> 0 us
  between operations: 13.8 us -> 0.95 us
  other arithmetic: 0 us -> 2.15 us
    all_gather x2 -> x0, waiting for transfers between devices: 115 us -> none  [the longest x1 100 us: on_device(): cot_full = lax.all_gather(cotangent, 'mp', axis=0, tiled=True)]
    ppermute x0 -> x27, waiting for transfers between devices: none -> 44.5 us  [send(): return lax.ppermute(value, AXES, flip(**bits))]
    pallas_call x0 -> x5, Pallas kernels: none -> 39.9 us  [the longest x1 25 us: pack(): pl.pallas_call(functools.partial(pack_kernel, cuts), out_shape=shapes, in...]
    ppermute x0 -> x27, starting transfers between devices: none -> 35.4 us  [send(): return lax.ppermute(value, AXES, flip(**bits))]
    reduce_scatter x1 -> x0, waiting for transfers between devices: 22.7 us -> none  [on_device(): lax.psum_scatter(grad_part.astype(jnp.bfloat16), 'dp', scatter_dimension=...]
    dot_general x7 -> x0, matrix products: 14.3 us -> none  [the longest x1 5.04 us: on_device(): lax.dot_general(attended, cot_full, (((0,), (0,)), ((), ())), preferred_e...]
  transfers between devices with their start and end apart: 3 -> 27, of which waited for: 3 -> 11; matrix products, arithmetic and copies ran while one was open for 10% -> 1% of each run, Pallas kernels for 0% -> 32%
where the time goes in v1:
time: 125 us
  waiting for transfers between devices  44.5 us (36%)
  Pallas kernels  39.9 us (32%)
  starting transfers between devices  35.4 us (28%)
  other arithmetic  2.15 us (2%)
  local copies, waits for them, and re-layouts  1.68 us (1%)
    ppermute x27, waiting for transfers between devices, send(): return lax.ppermute(value, AXES, flip(**bits))  44.5 us
    ppermute x27, starting transfers between devices, send(): return lax.ppermute(value, AXES, flip(**bits))  35.4 us
    pallas_call x1, Pallas kernels, pack(): pl.pallas_call(functools.partial(pack_kernel, cuts), out_shape=shapes, in...  25 us
    pallas_call x2, Pallas kernels, products(): pl.pallas_call(functools.partial(products_kernel, low, high, first, last)...  9.61 us
    pallas_call x1, Pallas kernels, backward(): pl.pallas_call(backward_kernel, out_shape=[jax.ShapeDtypeStruct(q.shape,...  2.75 us
    pallas_call x1, Pallas kernels, forward(): pl.pallas_call(forward_kernel, out_shape=[jax.ShapeDtypeStruct((images, P...  2.59 us
  transfers between devices with their start and end apart: 27, of which 11 were waited for; matrix products, arithmetic and copies ran while one was open for 1% of the time, Pallas kernels for 32%

profile of v1, /device:TPU:0, one launch (start us, length us, event | category | flops | bytes accessed | tf_op | source)
XLA Modules:
  0.0 124.7 jit_solution(18272070062561585382)
XLA Ops:
  0.6 3.1 %collective-permute-start.7 = (bf16[128,1536]{1,0:T(8,128)(2,1)}, bf16[128,1536]{1,0:T(8,128)(2,1)S(1)}, u32[]{:S(2)}, u32[]{:S(2)}) collective-permute-start(bf16[128,1536]{1,0:T(8,128)(2,1)} %refs_8_.3), channel_id=1, source_target_pairs={{0,2},{1,3},{2,0},{3,1},{4,6},{5,7},{6,4},{7,5},{8,10},{9,11},{10,... | collective-permute-start | bytes 1179656 | tf_op jit(solution)/shard_map/ppermute | solution.py:93
  3.7 2.6 %forward.1 = (f32[2,256,256]{2,1,0:T(8,128)}, bf16[256,128]{1,0:T(8,128)(2,1)}, bf16[256,128]{1,0:T(8,128)(2,1)}) custom-call(bf16[512,128]{1,0:T(8,128)(2,1)} %q.3, bf16[512,128]{1,0:T(8,128)(2,1)} %k.3, bf16[512,128]{1,0:T(8,128)(2,1)} %v.3), custom_call_target="tpu_custom_call" | custom-call | flops 67108864 | bytes 1048576 | tf_op jit(solution)/shard_map/forward/pallas_call | solution.py:166
  8.3 25.0 %pack.1 = (bf16[64,2048]{1,0:T(8,128)(2,1)}, bf16[64,2048]{1,0:T(8,128)(2,1)}, bf16[64,1024]{1,0:T(8,128)(2,1)}, bf16[64,1024]{1,0:T(8,128)(2,1)}) custom-call(bf16[64,6144]{1,0:T(8,128)(2,1)} %cot.1), custom_call_target="tpu_custom_call" | custom-call | bytes 1572864 | tf_op jit(solution)/shard_map/pack/pallas_call | solution.py:133
  33.3 2.7 %collective-permute-start.14 = (bf16[64,2048]{1,0:T(8,128)(2,1)}, bf16[64,2048]{1,0:T(8,128)(2,1)S(1)}, u32[]{:S(2)}, u32[]{:S(2)}) collective-permute-start(bf16[64,2048]{1,0:T(8,128)(2,1)} %get-tuple-element.28.refs_0_), channel_id=1, source_target_pairs={{0,4},{1,5},{2,6},{3,7},{4,0},{5,1},{6,2},{7,3},{8,12},{9,13},{10,... | collective-permute-start | bytes 786440 | tf_op jit(solution)/shard_map/ppermute | solution.py:93
  36.3 2.6 %collective-permute-start.5 = (bf16[64,1024]{1,0:T(8,128)(2,1)}, bf16[64,1024]{1,0:T(8,128)(2,1)S(1)}, u32[]{:S(2)}, u32[]{:S(2)}) collective-permute-start(bf16[64,1024]{1,0:T(8,128)(2,1)} %get-tuple-element.25), channel_id=1, source_target_pairs={{0,20},{1,21},{2,22},{3,23},{4,16},{5,17},{6,18},{7,19},{8,28},{9,... | collective-permute-start | bytes 393224 | tf_op jit(solution)/shard_map/ppermute | solution.py:93
  38.8 2.6 %collective-permute-start.12 = (bf16[256,128]{1,0:T(8,128)(2,1)S(1)}, bf16[256,128]{1,0:T(8,128)(2,1)S(1)}, u32[]{:S(2)}, u32[]{:S(2)}) collective-permute-start(bf16[256,128]{1,0:T(8,128)(2,1)S(1)} %copy-done.24), channel_id=1, source_target_pairs={{0,18},{1,19},{2,16},{3,17},{4,22},{5,23},{6,20},{7,21},{8,26},{9,... | collective-permute-start | bytes 196616 | tf_op jit(solution)/shard_map/ppermute | solution.py:93
  41.4 6.5 %collective-permute-done.12.refs_15_ = bf16[256,128]{1,0:T(8,128)(2,1)S(1)} collective-permute-done((bf16[256,128]{1,0:T(8,128)(2,1)S(1)}, bf16[256,128]{1,0:T(8,128)(2,1)S(1)}, u32[]{:S(2)}, u32[]{:S(2)}) %collective-permute-start.12) | collective-permute-done | bytes 65568 | tf_op jit(solution)/shard_map/ppermute | solution.py:93
  47.9 4.0 %collective-permute-start.18 = (bf16[64,2048]{1,0:T(8,128)(2,1)}, bf16[64,2048]{1,0:T(8,128)(2,1)S(1)}, u32[]{:S(2)}, u32[]{:S(2)}) collective-permute-start(bf16[64,2048]{1,0:T(8,128)(2,1)} %get-tuple-element.29), channel_id=1, source_target_pairs={{0,20},{1,21},{2,22},{3,23},{4,16},{5,17},{6,18},{7,19},{8,28},{9,... | collective-permute-start | bytes 786440 | tf_op jit(solution)/shard_map/ppermute | solution.py:93
  51.9 10.6 %collective-permute-done.1.refs_2_ = bf16[64,1024]{1,0:T(8,128)(2,1)S(1)} collective-permute-done((bf16[64,1024]{1,0:T(8,128)(2,1)}, bf16[64,1024]{1,0:T(8,128)(2,1)S(1)}, u32[]{:S(2)}, u32[]{:S(2)}) %collective-permute-start.1) | collective-permute-done | bytes 131104 | tf_op jit(solution)/shard_map/ppermute | solution.py:93
  62.5 1.5 %collective-permute-start.13 = (bf16[64,2048]{1,0:T(8,128)(2,1)}, bf16[64,2048]{1,0:T(8,128)(2,1)S(1)}, u32[]{:S(2)}, u32[]{:S(2)}) collective-permute-start(bf16[64,2048]{1,0:T(8,128)(2,1)} %get-tuple-element.28.refs_0_), channel_id=1, source_target_pairs={{0,1},{1,0},{2,3},{3,2},{4,5},{5,4},{6,7},{7,6},{8,9},{9,8},{10,11... | collective-permute-start | bytes 786440 | tf_op jit(solution)/shard_map/ppermute | solution.py:93
  67.3 2.4 %collective-permute-done.18.refs_6_ = bf16[64,2048]{1,0:T(8,128)(2,1)S(1)} collective-permute-done((bf16[64,2048]{1,0:T(8,128)(2,1)}, bf16[64,2048]{1,0:T(8,128)(2,1)S(1)}, u32[]{:S(2)}, u32[]{:S(2)}) %collective-permute-start.18) | collective-permute-done | bytes 262176 | tf_op jit(solution)/shard_map/ppermute | solution.py:93
  69.8 2.5 %collective-permute-start.17 = (bf16[64,2048]{1,0:T(8,128)(2,1)}, bf16[64,2048]{1,0:T(8,128)(2,1)}, u32[]{:S(2)}, u32[]{:S(2)}) collective-permute-start(bf16[64,2048]{1,0:T(8,128)(2,1)} %get-tuple-element.29), channel_id=1, source_target_pairs={{0,17},{1,16},{2,19},{3,18},{4,21},{5,20},{6,23},{7,22},{8,25},{9,... | collective-permute-start | bytes 786440 | tf_op jit(solution)/shard_map/ppermute | solution.py:93
  72.8 2.6 %collective-permute-done.16.refs_4_ = bf16[64,2048]{1,0:T(8,128)(2,1)S(1)} collective-permute-done((bf16[64,2048]{1,0:T(8,128)(2,1)}, bf16[64,2048]{1,0:T(8,128)(2,1)S(1)}, u32[]{:S(2)}, u32[]{:S(2)}) %collective-permute-start.16) | collective-permute-done | bytes 262176 | tf_op jit(solution)/shard_map/ppermute | solution.py:93
  75.4 1.6 %collective-permute-start.19 = (bf16[64,2048]{1,0:T(8,128)(2,1)S(1)}, bf16[64,2048]{1,0:T(8,128)(2,1)S(1)}, u32[]{:S(2)}, u32[]{:S(2)}) collective-permute-start(bf16[64,2048]{1,0:T(8,128)(2,1)S(1)} %collective-permute-done.18.refs_6_), channel_id=1, source_target_pairs={{0,1},{1,0},{2,3},{3,2},{4,5},{5,4},{6,7},{7,6},{8,9},{9,8},{10,11... | collective-permute-start | bytes 786440 | tf_op jit(solution)/shard_map/ppermute | solution.py:93
  76.9 5.2 %collective-permute-done.17.refs_5_ = bf16[64,2048]{1,0:T(8,128)(2,1)} collective-permute-done((bf16[64,2048]{1,0:T(8,128)(2,1)}, bf16[64,2048]{1,0:T(8,128)(2,1)}, u32[]{:S(2)}, u32[]{:S(2)}) %collective-permute-start.17) | collective-permute-done | bytes 262176 | tf_op jit(solution)/shard_map/ppermute | solution.py:93
  82.6 1.5 %collective-permute-start.3 = (bf16[64,1024]{1,0:T(8,128)(2,1)}, bf16[64,1024]{1,0:T(8,128)(2,1)S(1)}, u32[]{:S(2)}, u32[]{:S(2)}) collective-permute-start(bf16[64,1024]{1,0:T(8,128)(2,1)} %get-tuple-element.25), channel_id=1, source_target_pairs={{0,16},{1,17},{2,18},{3,19},{4,20},{5,21},{6,22},{7,23},{8,24},{9,... | collective-permute-start | bytes 393224 | tf_op jit(solution)/shard_map/ppermute | solution.py:93
  84.1 3.0 %collective-permute-done.15.refs_3_ = bf16[64,2048]{1,0:T(8,128)(2,1)S(1)} collective-permute-done((bf16[64,2048]{1,0:T(8,128)(2,1)S(1)}, bf16[64,2048]{1,0:T(8,128)(2,1)S(1)}, u32[]{:S(2)}, u32[]{:S(2)}) %collective-permute-start.15) | collective-permute-done | bytes 262176 | tf_op jit(solution)/shard_map/ppermute | solution.py:93
  87.1 8.4 %collective-permute-done.19.refs_7_ = bf16[64,2048]{1,0:T(8,128)(2,1)S(1)} collective-permute-done((bf16[64,2048]{1,0:T(8,128)(2,1)S(1)}, bf16[64,2048]{1,0:T(8,128)(2,1)S(1)}, u32[]{:S(2)}, u32[]{:S(2)}) %collective-permute-start.19) | collective-permute-done | bytes 262176 | tf_op jit(solution)/shard_map/ppermute | solution.py:93
  97.7 5.2 %products.2 = (f32[256,1024]{1,0:T(8,128)}, bf16[256,1024]{1,0:T(8,128)(2,1)}, f32[512,256]{1,0:T(8,128)}) custom-call(bf16[64,2048]{1,0:T(8,128)(2,1)} %get-tuple-element.28.refs_0_, bf16[64,2048]{1,0:T(8,128)(2,1)} %copy-done.20, bf16[64,2048]{1,0:T(8,128)(2,1)} %copy-done.18, bf16[64,2048]{1,0:T(8,128)(2,1)} %copy-done.22, bf16[64,2048]{1,0:T(8,128)(2,1)} %copy-done.21, ...), custom_call_target="tpu_custom_call" | custom-call | flops 1073741824 | bytes 5242880 | tf_op jit(solution)/shard_map/products/pallas_call | solution.py:281
  103.9 4.4 %products.3 = (f32[256,512]{1,0:T(8,128)}, bf16[256,512]{1,0:T(8,128)(2,1)}, f32[256,128]{1,0:T(8,128)}, bf16[256,128]{1,0:T(8,128)(2,1)}, bf16[256,128]{1,0:T(8,128)(2,1)}, /*index=5*/bf16[256,128]{1,0:T(8,128)(2,1)}) custom-call(bf16[64,1024]{1,0:T(8,128)(2,1)} %get-tuple-element.24.refs_0_, bf16[64,1024]{1,0:T(8,128)(2,1)} %copy-done.7, ...), custom_call_target="tpu_custom_call" | custom-call | flops 536870912 | bytes 2621440 | tf_op jit(solution)/shard_map/products/pallas_call | solution.py:281
  108.9 3.5 %collective-permute-start.22 = (bf16[256,128]{1,0:T(8,128)(2,1)}, bf16[256,128]{1,0:T(8,128)(2,1)S(1)}, u32[]{:S(2)}, u32[]{:S(2)}) collective-permute-start(bf16[256,128]{1,0:T(8,128)(2,1)} %get-tuple-element.34), channel_id=1, source_target_pairs={{0,18},{1,19},{2,16},{3,17},{4,22},{5,23},{6,20},{7,21},{8,26},{9,... | collective-permute-start | bytes 196616 | tf_op jit(solution)/shard_map/ppermute | solution.py:93
  113.8 2.1 %collective-permute-start.24 = (bf16[128,1024]{1,0:T(8,128)(2,1)S(1)}, bf16[128,1024]{1,0:T(8,128)(2,1)S(1)}, u32[]{:S(2)}, u32[]{:S(2)}) collective-permute-start(bf16[128,1024]{1,0:T(8,128)(2,1)S(1)} %slice.30), channel_id=1, source_target_pairs={{0,2},{1,3},{2,0},{3,1},{4,6},{5,7},{6,4},{7,5},{8,10},{9,11},{10,... | collective-permute-start | bytes 786440 | tf_op jit(solution)/shard_map/ppermute | solution.py:93
  116.9 2.7 %backward.1 = (bf16[512,128]{1,0:T(8,128)(2,1)}, bf16[512,128]{1,0:T(8,128)(2,1)}, bf16[512,128]{1,0:T(8,128)(2,1)}) custom-call(bf16[512,128]{1,0:T(8,128)(2,1)} %q.3, bf16[512,128]{1,0:T(8,128)(2,1)} %k.3, bf16[512,128]{1,0:T(8,128)(2,1)} %v.3, f32[2,256,256]{2,1,0:T(8,128)} %get-tuple-element.23.probs, f32[256,128]{1,0:T(8,128)} %get-tuple-element.31.own, ...), custom_call_target="tpu_custom_call" | custom-call | flops 134217728 | bytes 2097152 | tf_op jit(solution)/shard_map/backward/pallas_call | solution.py:202
  120.0 3.8 %collective-permute-done.24 = bf16[128,1024]{1,0:T(8,128)(2,1)S(1)} collective-permute-done((bf16[128,1024]{1,0:T(8,128)(2,1)S(1)}, bf16[128,1024]{1,0:T(8,128)(2,1)S(1)}, u32[]{:S(2)}, u32[]{:S(2)}) %collective-permute-start.24) | collective-permute-done | bytes 262176 | tf_op jit(solution)/shard_map/ppermute | solution.py:93
  (92 shorter events, 13.8 us)
Async XLA Ops:
  0.6 66.2 %collective-permute-start.7 = (bf16[128,1536]{1,0:T(8,128)(2,1)}, bf16[128,1536]{1,0:T(8,128)(2,1)S(1)}, u32[]{:S(2)}, u32[]{:S(2)}) collective-permute-start(bf16[128,1536]{1,0:T(8,128)(2,1)} %refs_8_.3), channel_id=1, source_target_pairs={{0,2},{1,3},{2,0},{3,1},{4,6},{5,7},{6,4},{7,5},{8,10},{9,11},{10,... | collective-permute-start | bytes 1179656 | tf_op jit(solution)/shard_map/ppermute | solution.py:93
  6.3 29.9 %collective-permute-start.10 = (bf16[256,128]{1,0:T(8,128)(2,1)}, bf16[256,128]{1,0:T(8,128)(2,1)S(1)}, u32[]{:S(2)}, u32[]{:S(2)}) collective-permute-start(bf16[256,128]{1,0:T(8,128)(2,1)} %get-tuple-element.26.refs_12_), channel_id=1, source_target_pairs={{0,16},{1,17},{2,18},{3,19},{4,20},{5,21},{6,22},{7,23},{8,24},{9,... | collective-permute-start | bytes 196616 | tf_op jit(solution)/shard_map/ppermute | solution.py:93
  7.8 31.0 %collective-permute-start.11 = (bf16[256,128]{1,0:T(8,128)(2,1)}, bf16[256,128]{1,0:T(8,128)(2,1)S(1)}, u32[]{:S(2)}, u32[]{:S(2)}) collective-permute-start(bf16[256,128]{1,0:T(8,128)(2,1)} %get-tuple-element.27), channel_id=1, source_target_pairs={{0,2},{1,3},{2,0},{3,1},{4,6},{5,7},{6,4},{7,5},{8,10},{9,11},{10,... | collective-permute-start | bytes 196616 | tf_op jit(solution)/shard_map/ppermute | solution.py:93
  33.3 33.5 %collective-permute-start.14 = (bf16[64,2048]{1,0:T(8,128)(2,1)}, bf16[64,2048]{1,0:T(8,128)(2,1)S(1)}, u32[]{:S(2)}, u32[]{:S(2)}) collective-permute-start(bf16[64,2048]{1,0:T(8,128)(2,1)} %get-tuple-element.28.refs_0_), channel_id=1, source_target_pairs={{0,4},{1,5},{2,6},{3,7},{4,0},{5,1},{6,2},{7,3},{8,12},{9,13},{10,... | collective-permute-start | bytes 786440 | tf_op jit(solution)/shard_map/ppermute | solution.py:93
  35.9 26.6 %collective-permute-start.1 = (bf16[64,1024]{1,0:T(8,128)(2,1)}, bf16[64,1024]{1,0:T(8,128)(2,1)S(1)}, u32[]{:S(2)}, u32[]{:S(2)}) collective-permute-start(bf16[64,1024]{1,0:T(8,128)(2,1)} %get-tuple-element.24.refs_0_), channel_id=1, source_target_pairs={{0,4},{1,5},{2,6},{3,7},{4,0},{5,1},{6,2},{7,3},{8,12},{9,13},{10,... | collective-permute-start | bytes 393224 | tf_op jit(solution)/shard_map/ppermute | solution.py:93
  36.3 29.0 %collective-permute-start.5 = (bf16[64,1024]{1,0:T(8,128)(2,1)}, bf16[64,1024]{1,0:T(8,128)(2,1)S(1)}, u32[]{:S(2)}, u32[]{:S(2)}) collective-permute-start(bf16[64,1024]{1,0:T(8,128)(2,1)} %get-tuple-element.25), channel_id=1, source_target_pairs={{0,20},{1,21},{2,22},{3,23},{4,16},{5,17},{6,18},{7,19},{8,28},{9,... | collective-permute-start | bytes 393224 | tf_op jit(solution)/shard_map/ppermute | solution.py:93
  38.8 9.1 %collective-permute-start.12 = (bf16[256,128]{1,0:T(8,128)(2,1)S(1)}, bf16[256,128]{1,0:T(8,128)(2,1)S(1)}, u32[]{:S(2)}, u32[]{:S(2)}) collective-permute-start(bf16[256,128]{1,0:T(8,128)(2,1)S(1)} %copy-done.24), channel_id=1, source_target_pairs={{0,18},{1,19},{2,16},{3,17},{4,22},{5,23},{6,20},{7,21},{8,26},{9,... | collective-permute-start | bytes 196616 | tf_op jit(solution)/shard_map/ppermute | solution.py:93
  47.9 21.8 %collective-permute-start.18 = (bf16[64,2048]{1,0:T(8,128)(2,1)}, bf16[64,2048]{1,0:T(8,128)(2,1)S(1)}, u32[]{:S(2)}, u32[]{:S(2)}) collective-permute-start(bf16[64,2048]{1,0:T(8,128)(2,1)} %get-tuple-element.29), channel_id=1, source_target_pairs={{0,20},{1,21},{2,22},{3,23},{4,16},{5,17},{6,18},{7,19},{8,28},{9,... | collective-permute-start | bytes 786440 | tf_op jit(solution)/shard_map/ppermute | solution.py:93
  62.5 9.8 %collective-permute-start.13 = (bf16[64,2048]{1,0:T(8,128)(2,1)}, bf16[64,2048]{1,0:T(8,128)(2,1)S(1)}, u32[]{:S(2)}, u32[]{:S(2)}) collective-permute-start(bf16[64,2048]{1,0:T(8,128)(2,1)} %get-tuple-element.28.refs_0_), channel_id=1, source_target_pairs={{0,1},{1,0},{2,3},{3,2},{4,5},{5,4},{6,7},{7,6},{8,9},{9,8},{10,11... | collective-permute-start | bytes 786440 | tf_op jit(solution)/shard_map/ppermute | solution.py:93
  65.3 10.1 %collective-permute-start.16 = (bf16[64,2048]{1,0:T(8,128)(2,1)}, bf16[64,2048]{1,0:T(8,128)(2,1)S(1)}, u32[]{:S(2)}, u32[]{:S(2)}) collective-permute-start(bf16[64,2048]{1,0:T(8,128)(2,1)} %get-tuple-element.29), channel_id=1, source_target_pairs={{0,16},{1,17},{2,18},{3,19},{4,20},{5,21},{6,22},{7,23},{8,24},{9,... | collective-permute-start | bytes 786440 | tf_op jit(solution)/shard_map/ppermute | solution.py:93
  66.8 15.8 %collective-permute-start.8 = (bf16[128,1536]{1,0:T(8,128)(2,1)S(1)}, bf16[128,1536]{1,0:T(8,128)(2,1)S(1)}, u32[]{:S(2)}, u32[]{:S(2)}) collective-permute-start(bf16[128,1536]{1,0:T(8,128)(2,1)S(1)} %copy-done.1), channel_id=1, source_target_pairs={{0,8},{1,9},{2,10},{3,11},{4,12},{5,13},{6,14},{7,15},{8,0},{9,1},... | collective-permute-start | bytes 1179656 | tf_op jit(solution)/shard_map/ppermute | solution.py:93
  66.8 29.2 %collective-permute-start.9 = (bf16[128,1536]{1,0:T(8,128)(2,1)S(1)}, bf16[128,1536]{1,0:T(8,128)(2,1)S(1)}, u32[]{:S(2)}, u32[]{:S(2)}) collective-permute-start(bf16[128,1536]{1,0:T(8,128)(2,1)S(1)} %collective-permute-done.7.refs_9_), channel_id=1, source_target_pairs={{0,8},{1,9},{2,10},{3,11},{4,12},{5,13},{6,14},{7,15},{8,0},{9,1},... | collective-permute-start | bytes 1179656 | tf_op jit(solution)/shard_map/ppermute | solution.py:93
  69.8 12.3 %collective-permute-start.17 = (bf16[64,2048]{1,0:T(8,128)(2,1)}, bf16[64,2048]{1,0:T(8,128)(2,1)}, u32[]{:S(2)}, u32[]{:S(2)}) collective-permute-start(bf16[64,2048]{1,0:T(8,128)(2,1)} %get-tuple-element.29), channel_id=1, source_target_pairs={{0,17},{1,16},{2,19},{3,18},{4,21},{5,20},{6,23},{7,22},{8,25},{9,... | collective-permute-start | bytes 786440 | tf_op jit(solution)/shard_map/ppermute | solution.py:93
  72.3 14.9 %collective-permute-start.15 = (bf16[64,2048]{1,0:T(8,128)(2,1)S(1)}, bf16[64,2048]{1,0:T(8,128)(2,1)S(1)}, u32[]{:S(2)}, u32[]{:S(2)}) collective-permute-start(bf16[64,2048]{1,0:T(8,128)(2,1)S(1)} %collective-permute-done.14.refs_2_), channel_id=1, source_target_pairs={{0,1},{1,0},{2,3},{3,2},{4,5},{5,4},{6,7},{7,6},{8,9},{9,8},{10,11... | collective-permute-start | bytes 786440 | tf_op jit(solution)/shard_map/ppermute | solution.py:93
  75.4 20.2 %collective-permute-start.19 = (bf16[64,2048]{1,0:T(8,128)(2,1)S(1)}, bf16[64,2048]{1,0:T(8,128)(2,1)S(1)}, u32[]{:S(2)}, u32[]{:S(2)}) collective-permute-start(bf16[64,2048]{1,0:T(8,128)(2,1)S(1)} %collective-permute-done.18.refs_6_), channel_id=1, source_target_pairs={{0,1},{1,0},{2,3},{3,2},{4,5},{5,4},{6,7},{7,6},{8,9},{9,8},{10,11... | collective-permute-start | bytes 786440 | tf_op jit(solution)/shard_map/ppermute | solution.py:93
  82.1 20.9 %collective-permute-start = (bf16[64,1024]{1,0:T(8,128)(2,1)}, bf16[64,1024]{1,0:T(8,128)(2,1)S(1)}, u32[]{:S(2)}, u32[]{:S(2)}) collective-permute-start(bf16[64,1024]{1,0:T(8,128)(2,1)} %get-tuple-element.24.refs_0_), channel_id=1, source_target_pairs={{0,1},{1,0},{2,3},{3,2},{4,5},{5,4},{6,7},{7,6},{8,9},{9,8},{10,11... | collective-permute-start | bytes 393224 | tf_op jit(solution)/shard_map/ppermute | solution.py:93
  82.6 20.5 %collective-permute-start.3 = (bf16[64,1024]{1,0:T(8,128)(2,1)}, bf16[64,1024]{1,0:T(8,128)(2,1)S(1)}, u32[]{:S(2)}, u32[]{:S(2)}) collective-permute-start(bf16[64,1024]{1,0:T(8,128)(2,1)} %get-tuple-element.25), channel_id=1, source_target_pairs={{0,16},{1,17},{2,18},{3,19},{4,20},{5,21},{6,22},{7,23},{8,24},{9,... | collective-permute-start | bytes 393224 | tf_op jit(solution)/shard_map/ppermute | solution.py:93
  87.1 16.0 %collective-permute-start.4 = (bf16[64,1024]{1,0:T(8,128)(2,1)}, bf16[64,1024]{1,0:T(8,128)(2,1)S(1)}, u32[]{:S(2)}, u32[]{:S(2)}) collective-permute-start(bf16[64,1024]{1,0:T(8,128)(2,1)} %get-tuple-element.25), channel_id=1, source_target_pairs={{0,17},{1,16},{2,19},{3,18},{4,21},{5,20},{6,23},{7,22},{8,25},{9,... | collective-permute-start | bytes 393224 | tf_op jit(solution)/shard_map/ppermute | solution.py:93
  95.5 7.6 %collective-permute-start.2 = (bf16[64,1024]{1,0:T(8,128)(2,1)S(1)}, bf16[64,1024]{1,0:T(8,128)(2,1)S(1)}, u32[]{:S(2)}, u32[]{:S(2)}) collective-permute-start(bf16[64,1024]{1,0:T(8,128)(2,1)S(1)} %collective-permute-done.1.refs_2_), channel_id=1, source_target_pairs={{0,1},{1,0},{2,3},{3,2},{4,5},{5,4},{6,7},{7,6},{8,9},{9,8},{10,11... | collective-permute-start | bytes 393224 | tf_op jit(solution)/shard_map/ppermute | solution.py:93
  103.0 10.6 %collective-permute-start.23 = (bf16[256,1024]{1,0:T(8,128)(2,1)}, bf16[256,1024]{1,0:T(8,128)(2,1)S(1)}, u32[]{:S(2)}, u32[]{:S(2)}) collective-permute-start(bf16[256,1024]{1,0:T(8,128)(2,1)} %get-tuple-element.39), channel_id=1, source_target_pairs={{0,8},{1,9},{2,10},{3,11},{4,12},{5,13},{6,14},{7,15},{8,0},{9,1},... | collective-permute-start | bytes 1572872 | tf_op jit(solution)/shard_map/ppermute | solution.py:93
  108.9 7.0 %collective-permute-start.20 = (bf16[256,128]{1,0:T(8,128)(2,1)}, bf16[256,128]{1,0:T(8,128)(2,1)S(1)}, u32[]{:S(2)}, u32[]{:S(2)}) collective-permute-start(bf16[256,128]{1,0:T(8,128)(2,1)} %get-tuple-element.32), channel_id=1, source_target_pairs={{0,16},{1,17},{2,18},{3,19},{4,20},{5,21},{6,22},{7,23},{8,24},{9,... | collective-permute-start | bytes 196616 | tf_op jit(solution)/shard_map/ppermute | solution.py:93
  108.9 7.0 %collective-permute-start.21 = (bf16[256,128]{1,0:T(8,128)(2,1)}, bf16[256,128]{1,0:T(8,128)(2,1)S(1)}, u32[]{:S(2)}, u32[]{:S(2)}) collective-permute-start(bf16[256,128]{1,0:T(8,128)(2,1)} %get-tuple-element.33), channel_id=1, source_target_pairs={{0,2},{1,3},{2,0},{3,1},{4,6},{5,7},{6,4},{7,5},{8,10},{9,11},{10,... | collective-permute-start | bytes 196616 | tf_op jit(solution)/shard_map/ppermute | solution.py:93
  108.9 7.4 %collective-permute-start.22 = (bf16[256,128]{1,0:T(8,128)(2,1)}, bf16[256,128]{1,0:T(8,128)(2,1)S(1)}, u32[]{:S(2)}, u32[]{:S(2)}) collective-permute-start(bf16[256,128]{1,0:T(8,128)(2,1)} %get-tuple-element.34), channel_id=1, source_target_pairs={{0,18},{1,19},{2,16},{3,17},{4,22},{5,23},{6,20},{7,21},{8,26},{9,... | collective-permute-start | bytes 196616 | tf_op jit(solution)/shard_map/ppermute | solution.py:93
  113.8 10.0 %collective-permute-start.24 = (bf16[128,1024]{1,0:T(8,128)(2,1)S(1)}, bf16[128,1024]{1,0:T(8,128)(2,1)S(1)}, u32[]{:S(2)}, u32[]{:S(2)}) collective-permute-start(bf16[128,1024]{1,0:T(8,128)(2,1)S(1)} %slice.30), channel_id=1, source_target_pairs={{0,2},{1,3},{2,0},{3,1},{4,6},{5,7},{6,4},{7,5},{8,10},{9,11},{10,... | collective-permute-start | bytes 786440 | tf_op jit(solution)/shard_map/ppermute | solution.py:93
  (28 other events, 530.1 us)

commit v2 on v1

--- a/solution.py
+++ b/solution.py
@@ -102,28 +102,16 @@
     return pl.multiple_of(index * unit, unit)
 
 
-def pack_kernel(cuts, cot, *rest):
-    outs, sems = rest[:-1], rest[-1]
+def pack_kernel(cuts, cot, *outs):
     x = place()["x"]
     quarter = cot.shape[1] // 4
-    copies = []
     for n, (low, high) in enumerate(cuts):
+        width = high - low
         for other in range(2):
             half = 1 - x if other else x
             for c in range(2):
                 start = pl.multiple_of(half * (2 * quarter) + (c * quarter + low), 128)
-                width = high - low
-                copies.append(
-                    pltpu.make_async_copy(
-                        cot.at[:, pl.ds(start, width)],
-                        outs[2 * n + other].at[:, pl.ds(c * width, width)],
-                        sems.at[len(copies)],
-                    )
-                )
-    for copy in copies:
-        copy.start()
-    for copy in copies:
-        copy.wait()
+                outs[2 * n + other][:, c * width : (c + 1) * width] = cot[:, pl.ds(start, width)]
 
 
 def pack(cot, cuts):
@@ -133,9 +121,8 @@
     return pl.pallas_call(
         functools.partial(pack_kernel, cuts),
         out_shape=shapes,
-        in_specs=[ANY],
-        out_specs=[ANY] * len(shapes),
-        scratch_shapes=[pltpu.SemaphoreType.DMA((4 * len(cuts),))],
+        in_specs=[VMEM],
+        out_specs=[VMEM] * len(shapes),
         cost_estimate=pl.CostEstimate(flops=0, bytes_accessed=2 * cot.size * 2, transcendentals=0),
         name="pack",
     )(cot)
@@ -212,60 +199,58 @@
     )(q, k, v, probs, own, from_x, from_z, from_xz)
 
 
-def products_kernel(low, high, first, last, *refs):
+def products_kernel(low, high, first, last, pieces, *refs):
     refs = list(refs)
-    blocks = [refs.pop(0) for _ in range(8)]
-    w_refs = [refs.pop(0) for _ in range(4)]
-    att = [refs.pop(0) for _ in range(4)]
+    cots = [refs.pop(0) for _ in range(1 + max(ref for ref, _ in pieces))]
+    w_own, w_core = refs.pop(0), refs.pop(0)
+    att_own, att_x = refs.pop(0), refs.pop(0)
     before = None if first else refs.pop(0)
     keep, give = refs.pop(0), refs.pop(0)
-    d_refs = [refs.pop(0) for _ in range(4 if last else 1)]
-    c_held, w_held, g_held, sems = refs
+    d_refs = refs
     at = place()
     width = high - low
-    copies = []
-    for n, block in enumerate(blocks):
-        group, z1, y = n // 4, (n // 2) % 2, n % 2
-        z1 = 1 - at["z1"] if z1 else at["z1"]
-        y = 1 - at["y"] if y else at["y"]
-        row = pl.multiple_of(group * 256 + z1 * 128 + y * 64, 64)
-        copies.append(pltpu.make_async_copy(block, c_held.at[pl.ds(row, 64)], sems.at[n]))
-    for n, w in enumerate(w_refs):
-        c = 1 - at["c"] if n // 2 else at["c"]
-        copies.append(
-            pltpu.make_async_copy(
-                w.at[:, pl.ds(low, width)],
-                w_held.at[pl.ds((n % 2) * HD, HD), pl.ds(pl.multiple_of(c * width, 128), width)],
-                sems.at[8 + n],
-            )
-        )
-    for copy in copies:
-        copy.start()
+    tile = min(width, 512)
+    rows = []
+    for n in range(4):
+        z1 = 1 - at["z1"] if n // 2 else at["z1"]
+        y = 1 - at["y"] if n % 2 else at["y"]
+        rows.append(pl.multiple_of(z1 * 128 + y * 64, 64))
     attended = jnp.concatenate(
         [
-            jnp.concatenate([att[0][...], att[2][...]], axis=1),
-            jnp.concatenate([att[1][...], att[3][...]], axis=1),
+            jnp.concatenate([att[pl.ds(row, 64)], att[pl.ds(256 + row, 64)]], axis=1)
+            for att in (att_own, att_x)
+            for row in rows
         ],
         axis=0,
     )
-    for copy in copies:
-        copy.wait()
-    g_held[...] = dot(attended, c_held[...], ((0,), (0,)))
-    keep[...] = g_held[:, pl.ds(pl.multiple_of(at["c"] * width, 128), width)]
-    give[...] = g_held[:, pl.ds(pl.multiple_of((1 - at["c"]) * width, 128), width)].astype(BF16)
-    d = dot(c_held[...], w_held[...], ((1,), (1,)))
-    if not first:
-        d = d + before[...]
+    turned = attended.T
+    d = None if first else before[...]
+    for other in (1, 0):
+        c = 1 - at["c"] if other else at["c"]
+        w_ref = w_core if other else w_own
+        for start in range(0, width, tile):
+            columns = pl.ds(pl.multiple_of(c * width + start, 128), tile)
+            cot = jnp.concatenate(
+                [cots[ref][row : row + 64, columns] for ref, row in pieces], axis=0
+            )
+            share = dot(turned, cot, ((1,), (0,)))
+            if other:
+                give[:, start : start + tile] = share.astype(BF16)
+            else:
+                keep[:, start : start + tile] = share
+            part = dot(cot, w_ref[:, low + start : low + start + tile], ((1,), (1,)))
+            d = part if d is None else d + part
     if not last:
         d_refs[0][...] = d
     else:
-        d_refs[0][...] = d[:256, :HD]
-        d_refs[1][...] = d[256:, :HD].astype(BF16)
-        d_refs[2][...] = d[:256, HD:].astype(BF16)
-        d_refs[3][...] = d[256:, HD:].astype(BF16)
-
-
-def products(low, high, blocks, w_all, att, before, last):
+        for n, row in enumerate(rows):
+            for g in range(2):
+                share = d[(4 * g + n) * 64 : (4 * g + n + 1) * 64]
+                d_refs[g][pl.ds(row, 64)] = share[:, :HD].astype(d_refs[g].dtype)
+                d_refs[2 + g][pl.ds(row, 64)] = share[:, HD:].astype(BF16)
+
+
+def products(low, high, pieces, cots, w_all, att, before, last):
     width = high - low
     first = before is None
     out = [
@@ -279,51 +264,62 @@
         out.append(jax.ShapeDtypeStruct((512, 2 * HD), F32))
     extra = [] if first else [before]
     return pl.pallas_call(
-        functools.partial(products_kernel, low, high, first, last),
+        functools.partial(products_kernel, low, high, first, last, pieces),
         out_shape=out,
-        in_specs=[ANY] * 12 + [VMEM] * (4 + len(extra)),
+        in_specs=[VMEM] * (len(cots) + 4 + len(extra)),
         out_specs=[VMEM] * len(out),
-        scratch_shapes=[
-            pltpu.VMEM((512, 2 * width), BF16),
-            pltpu.VMEM((2 * HD, 2 * width), BF16),
-            pltpu.VMEM((2 * HD, 2 * width), F32),
-            pltpu.SemaphoreType.DMA((12,)),
-        ],
         cost_estimate=pl.CostEstimate(
             flops=4 * 512 * 2 * HD * 2 * width,
             bytes_accessed=512 * 2 * width * 2 + 2 * HD * 2 * width * 6,
             transcendentals=0,
         ),
         name="products",
-    )(*blocks, *w_all, *att, *extra)
+    )(*cots, *w_all, *att, *extra)
+
+
+def after(value, *others):
+    return lax.optimization_barrier((value, *others))[0]
 
 
 CUTS = ((0, 1024), (1024, 1536))
 
 
 def on_device_4x8(queries, keys, values, w_out, cotangent):
-    packed = pack(cotangent, CUTS)
-    gathered = []
-    for n in range(len(CUTS)):
-        m, o = packed[2 * n], packed[2 * n + 1]
-        za, zb = send(m, z1=1), send(o, x=1, z1=1)
-        ya, xo, yb = send(m, y=1), send(o, x=1), send(o, x=1, y=1)
-        gathered.append([m, ya, za, send(za, y=1), xo, yb, zb, send(zb, y=1)])
-    w_pair = send(w_out, z0=1)
-    w_all = [w_out, w_pair, send(w_out, c=1), send(w_pair, c=1)]
-    probs, mine, others = forward(queries, keys, values)
-    att = [mine, send(mine, x=1), send(others, z0=1), send(others, x=1, z0=1)]
+    m1, o1, m2, o2 = pack(cotangent, CUTS)
+    za1, x1 = send(m1, z1=1), send(o1, x=1)
+    w_z = send(w_out, z0=1)
+    zb1 = send(x1, z1=1)
+    y1 = send(jnp.concatenate([m1, x1]), y=1)
+    x2 = send(after(o2, x1), x=1)
+    sa1 = send(za1, y=1)
+    mx2 = jnp.concatenate([m2, x2])
+    z2 = send(after(mx2, za1), z1=1)
+    y2 = send(after(mx2, y1), y=1)
+    sb1 = send(zb1, y=1)
+    s2 = send(after(z2, y2), y=1)
+    w_own = jnp.concatenate([w_out, w_z])
+    w_all = [w_own, send(after(w_own, za1), c=1)]
+    q, k, v, _ = lax.optimization_barrier((queries, keys, values, x1))
+    probs, mine, others = forward(q, k, v)
+    att = jnp.concatenate([mine, send(after(others, y1), z0=1)])
+    att = [att, send(att, x=1)]
+    inputs = [
+        ([m1, x1, y1, za1, sa1, zb1, sb1], [(0, 0), (2, 0), (3, 0), (4, 0), (1, 0), (2, 64), (5, 0), (6, 0)]),
+        ([mx2, y2, z2, s2], [(0, 0), (1, 0), (2, 0), (3, 0), (0, 64), (1, 64), (2, 64), (3, 64)]),
+    ]
     before, parts = None, []
     for n, (low, high) in enumerate(CUTS):
         last = n == len(CUTS) - 1
-        keep, give, *d = products(low, high, gathered[n], w_all, att, before, last)
-        before = d[0]
+        cots, pieces = inputs[n]
+        keep, give, *d = products(low, high, pieces, cots, w_all, att, before, last)
         total = keep + send(give, c=1).astype(F32)
-        pair = send(total[HD:].astype(BF16), z0=1)
+        to_pair = total[HD:].astype(BF16)
+        pair = send(to_pair, z0=1)
+        before = after(d[0], to_pair)
         parts.append((total[:HD] + pair.astype(F32)).astype(BF16))
     own, to_x, to_z, to_xz = d
     grad_q, grad_k, grad_v = backward(
-        queries, keys, values, probs, own, send(to_x, x=1), send(to_z, z0=1), send(to_xz, x=1, z0=1)
+        q, k, v, probs, own, send(to_x, x=1), send(to_z, z0=1), send(to_xz, x=1, z0=1)
     )
     return grad_q, grad_k, grad_v, jnp.concatenate(parts, axis=1)
 

time: 125 us -> 106 us (0.85)
  Pallas kernels: 39.9 us -> 15.5 us
  waiting for transfers between devices: 44.5 us -> 61.9 us
  starting transfers between devices: 35.4 us -> 21.3 us
  local copies, waits for them, and re-layouts: 1.68 us -> 3.87 us
    pallas_call x1, Pallas kernels: 25 us -> 2.11 us  [pack(): pl.pallas_call(functools.partial(pack_kernel, cuts), out_shape=shapes, in...]
    ppermute x27 -> x21, waiting for transfers between devices: 44.5 us -> 61.9 us  [send(): return lax.ppermute(value, AXES, flip(**bits))]
    ppermute x27 -> x21, starting transfers between devices: 35.4 us -> 21.3 us  [send(): return lax.ppermute(value, AXES, flip(**bits))]
    unnamed x50 -> x45, local copies, waits for them, and re-layouts: 1.63 us -> 3.78 us
    pallas_call x2, Pallas kernels: 9.61 us -> 8.03 us  [products(): pl.pallas_call(functools.partial(products_kernel, low, high, first, last,...]
  transfers between devices with their start and end apart: 27 -> 21, of which waited for: 11 -> 13; matrix products, arithmetic and copies ran while one was open for 1% -> 2% of each run, Pallas kernels for 32% -> 5%
where the time goes in v2:
time: 106 us
  waiting for transfers between devices  61.9 us (58%)
  starting transfers between devices  21.3 us (20%)
  Pallas kernels  15.5 us (15%)
  local copies, waits for them, and re-layouts  3.87 us (4%)
  other arithmetic  2.33 us (2%)
    ppermute x21, waiting for transfers between devices, send(): return lax.ppermute(value, AXES, flip(**bits))  61.9 us
    ppermute x21, starting transfers between devices, send(): return lax.ppermute(value, AXES, flip(**bits))  21.3 us
    pallas_call x2, Pallas kernels, products(): pl.pallas_call(functools.partial(products_kernel, low, high, first, last,...  8.03 us
    unnamed x45, local copies, waits for them, and re-layouts  3.78 us
    pallas_call x1, Pallas kernels, backward(): pl.pallas_call(backward_kernel, out_shape=[jax.ShapeDtypeStruct(q.shape,...  2.8 us
    pallas_call x1, Pallas kernels, forward(): pl.pallas_call(forward_kernel, out_shape=[jax.ShapeDtypeStruct((images, P...  2.58 us
  transfers between devices with their start and end apart: 21, of which 13 were waited for; matrix products, arithmetic and copies ran while one was open for 2% of the time, Pallas kernels for 5%

profile of v2, /device:TPU:0, one launch (start us, length us, event | category | flops | bytes accessed | tf_op | source)
XLA Modules:
  0.0 105.8 jit_solution(3302476604319695379)
XLA Ops:
  0.6 2.1 %pack.1 = (bf16[64,2048]{1,0:T(8,128)(2,1)}, bf16[64,2048]{1,0:T(8,128)(2,1)}, bf16[64,1024]{1,0:T(8,128)(2,1)}, bf16[64,1024]{1,0:T(8,128)(2,1)}) custom-call(bf16[64,6144]{1,0:T(8,128)(2,1)} %cot.1), custom_call_target="tpu_custom_call" | custom-call | bytes 1572864 | tf_op jit(solution)/shard_map/pack/pallas_call | solution.py:121
  2.7 2.9 %collective-permute-start = (bf16[64,2048]{1,0:T(8,128)(2,1)}, bf16[64,2048]{1,0:T(8,128)(2,1)S(1)}, u32[]{:S(2)}, u32[]{:S(2)}) collective-permute-start(bf16[64,2048]{1,0:T(8,128)(2,1)} %get-tuple-element.33), channel_id=1, source_target_pairs={{0,16},{1,17},{2,18},{3,19},{4,20},{5,21},{6,22},{7,23},{8,24},{9,... | collective-permute-start | bytes 786440 | tf_op jit(solution)/shard_map/ppermute | solution.py:93
  5.7 2.6 %collective-permute-start.4 = (bf16[64,2048]{1,0:T(8,128)(2,1)}, bf16[64,2048]{1,0:T(8,128)(2,1)S(1)}, u32[]{:S(2)}, u32[]{:S(2)}) collective-permute-start(bf16[64,2048]{1,0:T(8,128)(2,1)} %get-tuple-element.41.refs_0_), channel_id=1, source_target_pairs={{0,4},{1,5},{2,6},{3,7},{4,0},{5,1},{6,2},{7,3},{8,12},{9,13},{10,... | collective-permute-start | bytes 786440 | tf_op jit(solution)/shard_map/ppermute | solution.py:93
  8.3 1.6 %collective-permute-start.7 = (bf16[128,1536]{1,0:T(8,128)(2,1)S(1)}, bf16[128,1536]{1,0:T(8,128)(2,1)S(1)}, u32[]{:S(2)}, u32[]{:S(2)}) collective-permute-start(bf16[128,1536]{1,0:T(8,128)(2,1)S(1)} %copy-done.4), channel_id=1, source_target_pairs={{0,2},{1,3},{2,0},{3,1},{4,6},{5,7},{6,4},{7,5},{8,10},{9,11},{10,... | collective-permute-start | bytes 1179656 | tf_op jit(solution)/shard_map/ppermute | solution.py:93
  9.9 2.3 %collective-permute-done.refs_1_ = bf16[64,2048]{1,0:T(8,128)(2,1)S(1)} collective-permute-done((bf16[64,2048]{1,0:T(8,128)(2,1)}, bf16[64,2048]{1,0:T(8,128)(2,1)S(1)}, u32[]{:S(2)}, u32[]{:S(2)}) %collective-permute-start) | collective-permute-done | bytes 262176 | tf_op jit(solution)/shard_map/ppermute | solution.py:93
  12.3 1.8 %collective-permute-start.2 = (bf16[128,2048]{1,0:T(8,128)(2,1)S(1)}, bf16[128,2048]{1,0:T(8,128)(2,1)}, u32[]{:S(2)}, u32[]{:S(2)}) collective-permute-start(bf16[128,2048]{1,0:T(8,128)(2,1)S(1)} %pad_maximum_fusion), channel_id=1, source_target_pairs={{0,1},{1,0},{2,3},{3,2},{4,5},{5,4},{6,7},{7,6},{8,9},{9,8},{10,11... | collective-permute-start | bytes 1572872 | tf_op jit(solution)/shard_map/ppermute | solution.py:93
  14.1 9.0 %collective-permute-done.7 = bf16[128,1536]{1,0:T(8,128)(2,1)S(1)} collective-permute-done((bf16[128,1536]{1,0:T(8,128)(2,1)S(1)}, bf16[128,1536]{1,0:T(8,128)(2,1)S(1)}, u32[]{:S(2)}, u32[]{:S(2)}) %collective-permute-start.7) | collective-permute-done | bytes 393248 | tf_op jit(solution)/shard_map/ppermute | solution.py:93
  23.2 1.6 %collective-permute-start.12 = (bf16[64,2048]{1,0:T(8,128)(2,1)S(1)}, bf16[64,2048]{1,0:T(8,128)(2,1)S(1)}, u32[]{:S(2)}, u32[]{:S(2)}) collective-permute-start(bf16[64,2048]{1,0:T(8,128)(2,1)S(1)} %collective-permute-done.refs_1_), channel_id=1, source_target_pairs={{0,4},{1,5},{2,6},{3,7},{4,0},{5,1},{6,2},{7,3},{8,12},{9,13},{10,... | collective-permute-start | bytes 786440 | tf_op jit(solution)/shard_map/ppermute | solution.py:93
  24.8 1.5 %collective-permute-start.11 = (bf16[64,2048]{1,0:T(8,128)(2,1)S(1)}, bf16[64,2048]{1,0:T(8,128)(2,1)S(1)}, u32[]{:S(2)}, u32[]{:S(2)}) collective-permute-start(bf16[64,2048]{1,0:T(8,128)(2,1)S(1)} %collective-permute-done.4.refs_3_), channel_id=1, source_target_pairs={{0,1},{1,0},{2,3},{3,2},{4,5},{5,4},{6,7},{7,6},{8,9},{9,8},{10,11... | collective-permute-start | bytes 786440 | tf_op jit(solution)/shard_map/ppermute | solution.py:93
  26.4 2.6 %forward.1 = (f32[2,256,256]{2,1,0:T(8,128)}, bf16[256,128]{1,0:T(8,128)(2,1)}, bf16[256,128]{1,0:T(8,128)(2,1)}) custom-call(bf16[512,128]{1,0:T(8,128)(2,1)} %q.1, bf16[512,128]{1,0:T(8,128)(2,1)} %k.1, bf16[512,128]{1,0:T(8,128)(2,1)} %v.1), custom_call_target="tpu_custom_call" | custom-call | flops 67108864 | bytes 1048576 | tf_op jit(solution)/shard_map/forward/pallas_call | solution.py:153
  28.9 9.5 %collective-permute-done.12.refs_5_ = bf16[64,2048]{1,0:T(8,128)(2,1)S(1)} collective-permute-done((bf16[64,2048]{1,0:T(8,128)(2,1)S(1)}, bf16[64,2048]{1,0:T(8,128)(2,1)S(1)}, u32[]{:S(2)}, u32[]{:S(2)}) %collective-permute-start.12) | collective-permute-done | bytes 262176 | tf_op jit(solution)/shard_map/ppermute | solution.py:93
  38.5 1.5 %collective-permute-start.13 = (bf16[64,2048]{1,0:T(8,128)(2,1)S(1)}, bf16[64,2048]{1,0:T(8,128)(2,1)S(1)}, u32[]{:S(2)}, u32[]{:S(2)}) collective-permute-start(bf16[64,2048]{1,0:T(8,128)(2,1)S(1)} %collective-permute-done.12.refs_5_), channel_id=1, source_target_pairs={{0,1},{1,0},{2,3},{3,2},{4,5},{5,4},{6,7},{7,6},{8,9},{9,8},{10,11... | collective-permute-start | bytes 786440 | tf_op jit(solution)/shard_map/ppermute | solution.py:93
  40.8 3.6 %collective-permute-done.9 = bf16[256,128]{1,0:T(8,128)(2,1)S(1)} collective-permute-done((bf16[256,128]{1,0:T(8,128)(2,1)}, bf16[256,128]{1,0:T(8,128)(2,1)S(1)}, u32[]{:S(2)}, u32[]{:S(2)}) %collective-permute-start.9) | collective-permute-done | bytes 65568 | tf_op jit(solution)/shard_map/ppermute | solution.py:93
  46.3 3.2 %collective-permute-done.10.refs_10_.refs_7_ = bf16[512,128]{1,0:T(8,128)(2,1)S(1)} collective-permute-done((bf16[512,128]{1,0:T(8,128)(2,1)S(1)}, bf16[512,128]{1,0:T(8,128)(2,1)S(1)}, u32[]{:S(2)}, u32[]{:S(2)}) %collective-permute-start.10) | collective-permute-done | bytes 131104 | tf_op jit(solution)/shard_map/ppermute | solution.py:93
  51.1 4.5 %products.2 = (f32[256,1024]{1,0:T(8,128)}, bf16[256,1024]{1,0:T(8,128)(2,1)}, f32[512,256]{1,0:T(8,128)}) custom-call(bf16[64,2048]{1,0:T(8,128)(2,1)} %get-tuple-element.41.refs_0_, bf16[64,2048]{1,0:T(8,128)(2,1)} %copy-done.7, bf16[128,2048]{1,0:T(8,128)(2,1)} %collective-permute-done.2.refs_2_, bf16[64,2048]{1,0:T(8,128)(2,1)} %copy-done.16, ...), custom_call_target="tpu_custom_call" | custom-call | flops 1073741824 | bytes 5242880 | tf_op jit(solution)/shard_map/products/pallas_call | solution.py:266
  56.3 5.3 %collective-permute-done.1 = bf16[64,1024]{1,0:T(8,128)(2,1)S(1)} collective-permute-done((bf16[64,1024]{1,0:T(8,128)(2,1)S(1)}, bf16[64,1024]{1,0:T(8,128)(2,1)S(1)}, u32[]{:S(2)}, u32[]{:S(2)}) %collective-permute-start.1) | collective-permute-done | bytes 131104 | tf_op jit(solution)/shard_map/ppermute | solution.py:93
  63.1 12.7 %collective-permute-done.5.refs_2_ = bf16[128,1024]{1,0:T(8,128)(2,1)S(1)} collective-permute-done((bf16[128,1024]{1,0:T(8,128)(2,1)S(1)}, bf16[128,1024]{1,0:T(8,128)(2,1)S(1)}, u32[]{:S(2)}, u32[]{:S(2)}) %collective-permute-start.5) | collective-permute-done | bytes 262176 | tf_op jit(solution)/shard_map/ppermute | solution.py:93
  76.4 1.4 %convert_add_fusion = f32[256,1024]{1,0:T(8,128)S(1)} fusion(f32[256,1024]{1,0:T(8,128)} %get-tuple-element.50, bf16[256,1024]{1,0:T(8,128)(2,1)S(1)} %collective-permute-done.14), kind=kLoop, calls=%fused_computation | loop fusion | flops 524288 | bytes 2621440 | tf_op jit(solution)/shard_map/add | solution.py:315
  77.8 6.3 %collective-permute-done.6.refs_3_ = bf16[128,1024]{1,0:T(8,128)(2,1)S(1)} collective-permute-done((bf16[128,1024]{1,0:T(8,128)(2,1)S(1)}, bf16[128,1024]{1,0:T(8,128)(2,1)S(1)}, u32[]{:S(2)}, u32[]{:S(2)}) %collective-permute-start.6) | collective-permute-done | bytes 262176 | tf_op jit(solution)/shard_map/ppermute | solution.py:93
  84.8 3.5 %products.3 = (f32[256,512]{1,0:T(8,128)}, bf16[256,512]{1,0:T(8,128)(2,1)}, f32[256,128]{1,0:T(8,128)}, bf16[256,128]{1,0:T(8,128)(2,1)}, bf16[256,128]{1,0:T(8,128)(2,1)}, /*index=5*/bf16[256,128]{1,0:T(8,128)(2,1)}) custom-call(bf16[128,1024]{1,0:T(8,128)(2,1)} %copy-done.2, bf16[128,1024]{1,0:T(8,128)(2,1)} %copy-done.9, bf16[128,1024]{1,0:T(8,128)(2,1)} %copy-done.8, ...), custom_call_target="tpu_custom_call" | custom-call | flops 536870912 | bytes 2621440 | tf_op jit(solution)/shard_map/products/pallas_call | solution.py:266
  88.9 2.9 %collective-permute-start.17 = (bf16[256,128]{1,0:T(8,128)(2,1)}, bf16[256,128]{1,0:T(8,128)(2,1)S(1)}, u32[]{:S(2)}, u32[]{:S(2)}) collective-permute-start(bf16[256,128]{1,0:T(8,128)(2,1)} %get-tuple-element.56), channel_id=1, source_target_pairs={{0,18},{1,19},{2,16},{3,17},{4,22},{5,23},{6,20},{7,21},{8,26},{9,... | collective-permute-start | bytes 196616 | tf_op jit(solution)/shard_map/ppermute | solution.py:93
  94.0 2.4 %collective-permute-done.17.from_xz = bf16[256,128]{1,0:T(8,128)(2,1)S(1)} collective-permute-done((bf16[256,128]{1,0:T(8,128)(2,1)}, bf16[256,128]{1,0:T(8,128)(2,1)S(1)}, u32[]{:S(2)}, u32[]{:S(2)}) %collective-permute-start.17) | collective-permute-done | bytes 65568 | tf_op jit(solution)/shard_map/ppermute | solution.py:93
  97.0 2.8 %backward.1 = (bf16[512,128]{1,0:T(8,128)(2,1)}, bf16[512,128]{1,0:T(8,128)(2,1)}, bf16[512,128]{1,0:T(8,128)(2,1)}) custom-call(bf16[512,128]{1,0:T(8,128)(2,1)} %q.1, bf16[512,128]{1,0:T(8,128)(2,1)} %k.1, bf16[512,128]{1,0:T(8,128)(2,1)} %v.1, f32[2,256,256]{2,1,0:T(8,128)} %get-tuple-element.37.probs, f32[256,128]{1,0:T(8,128)} %get-tuple-element.53.own, ...), custom_call_target="tpu_custom_call" | custom-call | flops 134217728 | bytes 2097152 | tf_op jit(solution)/shard_map/backward/pallas_call | solution.py:189
  100.7 4.3 %collective-permute-done.20 = bf16[128,512]{1,0:T(8,128)(2,1)S(1)} collective-permute-done((bf16[128,512]{1,0:T(8,128)(2,1)S(1)}, bf16[128,512]{1,0:T(8,128)(2,1)S(1)}, u32[]{:S(2)}, u32[]{:S(2)}) %collective-permute-start.20) | collective-permute-done | bytes 131104 | tf_op jit(solution)/shard_map/ppermute | solution.py:93
  (79 shorter events, 12.9 us)
Async XLA Ops:
  2.7 9.5 %collective-permute-start = (bf16[64,2048]{1,0:T(8,128)(2,1)}, bf16[64,2048]{1,0:T(8,128)(2,1)S(1)}, u32[]{:S(2)}, u32[]{:S(2)}) collective-permute-start(bf16[64,2048]{1,0:T(8,128)(2,1)} %get-tuple-element.33), channel_id=1, source_target_pairs={{0,16},{1,17},{2,18},{3,19},{4,20},{5,21},{6,22},{7,23},{8,24},{9,... | collective-permute-start | bytes 786440 | tf_op jit(solution)/shard_map/ppermute | solution.py:93
  5.7 17.4 %collective-permute-start.4 = (bf16[64,2048]{1,0:T(8,128)(2,1)}, bf16[64,2048]{1,0:T(8,128)(2,1)S(1)}, u32[]{:S(2)}, u32[]{:S(2)}) collective-permute-start(bf16[64,2048]{1,0:T(8,128)(2,1)} %get-tuple-element.41.refs_0_), channel_id=1, source_target_pairs={{0,4},{1,5},{2,6},{3,7},{4,0},{5,1},{6,2},{7,3},{8,12},{9,13},{10,... | collective-permute-start | bytes 786440 | tf_op jit(solution)/shard_map/ppermute | solution.py:93
  8.3 14.8 %collective-permute-start.7 = (bf16[128,1536]{1,0:T(8,128)(2,1)S(1)}, bf16[128,1536]{1,0:T(8,128)(2,1)S(1)}, u32[]{:S(2)}, u32[]{:S(2)}) collective-permute-start(bf16[128,1536]{1,0:T(8,128)(2,1)S(1)} %copy-done.4), channel_id=1, source_target_pairs={{0,2},{1,3},{2,0},{3,1},{4,6},{5,7},{6,4},{7,5},{8,10},{9,11},{10,... | collective-permute-start | bytes 1179656 | tf_op jit(solution)/shard_map/ppermute | solution.py:93
  12.3 27.7 %collective-permute-start.2 = (bf16[128,2048]{1,0:T(8,128)(2,1)S(1)}, bf16[128,2048]{1,0:T(8,128)(2,1)}, u32[]{:S(2)}, u32[]{:S(2)}) collective-permute-start(bf16[128,2048]{1,0:T(8,128)(2,1)S(1)} %pad_maximum_fusion), channel_id=1, source_target_pairs={{0,1},{1,0},{2,3},{3,2},{4,5},{5,4},{6,7},{7,6},{8,9},{9,8},{10,11... | collective-permute-start | bytes 1572872 | tf_op jit(solution)/shard_map/ppermute | solution.py:93
  23.1 26.4 %copy-start = (bf16[256,1536]{1,0:T(8,128)(2,1)}, bf16[256,1536]{1,0:T(8,128)(2,1)S(1)}, u32[]{:S(2)}) copy-start(bf16[256,1536]{1,0:T(8,128)(2,1)S(1)} %constant_dynamic-update-slice_fusion.2.refs_7_.refs_4_) | copy-start | bytes 2359300
  23.1 17.7 %copy-start.16 = (bf16[64,2048]{1,0:T(8,128)(2,1)}, bf16[64,2048]{1,0:T(8,128)(2,1)S(1)}, u32[]{:S(2)}) copy-start(bf16[64,2048]{1,0:T(8,128)(2,1)S(1)} %collective-permute-done.4.refs_3_) | copy-start | bytes 786436
  23.1 26.4 %collective-permute-start.8 = (bf16[256,1536]{1,0:T(8,128)(2,1)S(1)}, bf16[256,1536]{1,0:T(8,128)(2,1)S(1)}, u32[]{:S(2)}, u32[]{:S(2)}) collective-permute-start(bf16[256,1536]{1,0:T(8,128)(2,1)S(1)} %constant_dynamic-update-slice_fusion.2.refs_7_.refs_4_), channel_id=1, source_target_pairs={{0,8},{1,9},{2,10},{3,11},{4,12},{5,13},{6,14},{7,15},{8,0},{9,1},... | collective-permute-start | bytes 2359304 | tf_op jit(solution)/shard_map/ppermute | solution.py:93
  23.2 15.2 %collective-permute-start.12 = (bf16[64,2048]{1,0:T(8,128)(2,1)S(1)}, bf16[64,2048]{1,0:T(8,128)(2,1)S(1)}, u32[]{:S(2)}, u32[]{:S(2)}) collective-permute-start(bf16[64,2048]{1,0:T(8,128)(2,1)S(1)} %collective-permute-done.refs_1_), channel_id=1, source_target_pairs={{0,4},{1,5},{2,6},{3,7},{4,0},{5,1},{6,2},{7,3},{8,12},{9,13},{10,... | collective-permute-start | bytes 786440 | tf_op jit(solution)/shard_map/ppermute | solution.py:93
  24.8 20.3 %collective-permute-start.11 = (bf16[64,2048]{1,0:T(8,128)(2,1)S(1)}, bf16[64,2048]{1,0:T(8,128)(2,1)S(1)}, u32[]{:S(2)}, u32[]{:S(2)}) collective-permute-start(bf16[64,2048]{1,0:T(8,128)(2,1)S(1)} %collective-permute-done.4.refs_3_), channel_id=1, source_target_pairs={{0,1},{1,0},{2,3},{3,2},{4,5},{5,4},{6,7},{7,6},{8,9},{9,8},{10,11... | collective-permute-start | bytes 786440 | tf_op jit(solution)/shard_map/ppermute | solution.py:93
  38.5 7.9 %collective-permute-start.13 = (bf16[64,2048]{1,0:T(8,128)(2,1)S(1)}, bf16[64,2048]{1,0:T(8,128)(2,1)S(1)}, u32[]{:S(2)}, u32[]{:S(2)}) collective-permute-start(bf16[64,2048]{1,0:T(8,128)(2,1)S(1)} %collective-permute-done.12.refs_5_), channel_id=1, source_target_pairs={{0,1},{1,0},{2,3},{3,2},{4,5},{5,4},{6,7},{7,6},{8,9},{9,8},{10,11... | collective-permute-start | bytes 786440 | tf_op jit(solution)/shard_map/ppermute | solution.py:93
  40.0 4.5 %collective-permute-start.9 = (bf16[256,128]{1,0:T(8,128)(2,1)}, bf16[256,128]{1,0:T(8,128)(2,1)S(1)}, u32[]{:S(2)}, u32[]{:S(2)}) collective-permute-start(bf16[256,128]{1,0:T(8,128)(2,1)} %get-tuple-element.48), channel_id=1, source_target_pairs={{0,2},{1,3},{2,0},{3,1},{4,6},{5,7},{6,4},{7,5},{8,10},{9,11},{10,... | collective-permute-start | bytes 196616 | tf_op jit(solution)/shard_map/ppermute | solution.py:93
  44.5 5.0 %collective-permute-start.10 = (bf16[512,128]{1,0:T(8,128)(2,1)S(1)}, bf16[512,128]{1,0:T(8,128)(2,1)S(1)}, u32[]{:S(2)}, u32[]{:S(2)}) collective-permute-start(bf16[512,128]{1,0:T(8,128)(2,1)S(1)} %constant_dynamic-update-slice_fusion.4.refs_9_.refs_6_), channel_id=1, source_target_pairs={{0,16},{1,17},{2,18},{3,19},{4,20},{5,21},{6,22},{7,23},{8,24},{9,... | collective-permute-start | bytes 393224 | tf_op jit(solution)/shard_map/ppermute | solution.py:93
  55.6 20.8 %collective-permute-start.14 = (bf16[256,1024]{1,0:T(8,128)(2,1)}, bf16[256,1024]{1,0:T(8,128)(2,1)S(1)}, u32[]{:S(2)}, u32[]{:S(2)}) collective-permute-start(bf16[256,1024]{1,0:T(8,128)(2,1)} %get-tuple-element.51), channel_id=1, source_target_pairs={{0,8},{1,9},{2,10},{3,11},{4,12},{5,13},{6,14},{7,15},{8,0},{9,1},... | collective-permute-start | bytes 1572872 | tf_op jit(solution)/shard_map/ppermute | solution.py:93
  55.6 5.9 %collective-permute-start.1 = (bf16[64,1024]{1,0:T(8,128)(2,1)S(1)}, bf16[64,1024]{1,0:T(8,128)(2,1)S(1)}, u32[]{:S(2)}, u32[]{:S(2)}) collective-permute-start(bf16[64,1024]{1,0:T(8,128)(2,1)S(1)} %copy-done.20), channel_id=1, source_target_pairs={{0,16},{1,17},{2,18},{3,19},{4,20},{5,21},{6,22},{7,23},{8,24},{9,... | collective-permute-start | bytes 393224 | tf_op jit(solution)/shard_map/ppermute | solution.py:93
  61.6 16.2 %copy-start.2 = (bf16[128,1024]{1,0:T(8,128)(2,1)}, bf16[128,1024]{1,0:T(8,128)(2,1)S(1)}, u32[]{:S(2)}) copy-start(bf16[128,1024]{1,0:T(8,128)(2,1)S(1)} %constant_dynamic-update-slice_fusion.refs_0_) | copy-start | bytes 786436
  61.6 14.3 %collective-permute-start.5 = (bf16[128,1024]{1,0:T(8,128)(2,1)S(1)}, bf16[128,1024]{1,0:T(8,128)(2,1)S(1)}, u32[]{:S(2)}, u32[]{:S(2)}) collective-permute-start(bf16[128,1024]{1,0:T(8,128)(2,1)S(1)} %constant_dynamic-update-slice_fusion.refs_0_), channel_id=1, source_target_pairs={{0,4},{1,5},{2,6},{3,7},{4,0},{5,1},{6,2},{7,3},{8,12},{9,13},{10,... | collective-permute-start | bytes 786440 | tf_op jit(solution)/shard_map/ppermute | solution.py:93
  62.6 13.2 %collective-permute-start.3 = (bf16[128,1024]{1,0:T(8,128)(2,1)S(1)}, bf16[128,1024]{1,0:T(8,128)(2,1)S(1)}, u32[]{:S(2)}, u32[]{:S(2)}) collective-permute-start(bf16[128,1024]{1,0:T(8,128)(2,1)S(1)} %constant_dynamic-update-slice_fusion.refs_0_), channel_id=1, source_target_pairs={{0,1},{1,0},{2,3},{3,2},{4,5},{5,4},{6,7},{7,6},{8,9},{9,8},{10,11... | collective-permute-start | bytes 786440 | tf_op jit(solution)/shard_map/ppermute | solution.py:93
  75.8 8.3 %collective-permute-start.6 = (bf16[128,1024]{1,0:T(8,128)(2,1)S(1)}, bf16[128,1024]{1,0:T(8,128)(2,1)S(1)}, u32[]{:S(2)}, u32[]{:S(2)}) collective-permute-start(bf16[128,1024]{1,0:T(8,128)(2,1)S(1)} %collective-permute-done.5.refs_2_), channel_id=1, source_target_pairs={{0,1},{1,0},{2,3},{3,2},{4,5},{5,4},{6,7},{7,6},{8,9},{9,8},{10,11... | collective-permute-start | bytes 786440 | tf_op jit(solution)/shard_map/ppermute | solution.py:93
  88.3 11.5 %collective-permute-start.19 = (bf16[256,512]{1,0:T(8,128)(2,1)}, bf16[256,512]{1,0:T(8,128)(2,1)S(1)}, u32[]{:S(2)}, u32[]{:S(2)}) collective-permute-start(bf16[256,512]{1,0:T(8,128)(2,1)} %get-tuple-element.61), channel_id=1, source_target_pairs={{0,8},{1,9},{2,10},{3,11},{4,12},{5,13},{6,14},{7,15},{8,0},{9,1},... | collective-permute-start | bytes 786440 | tf_op jit(solution)/shard_map/ppermute | solution.py:93
  88.3 4.7 %collective-permute-start.15 = (bf16[256,128]{1,0:T(8,128)(2,1)}, bf16[256,128]{1,0:T(8,128)(2,1)S(1)}, u32[]{:S(2)}, u32[]{:S(2)}) collective-permute-start(bf16[256,128]{1,0:T(8,128)(2,1)} %get-tuple-element.54), channel_id=1, source_target_pairs={{0,16},{1,17},{2,18},{3,19},{4,20},{5,21},{6,22},{7,23},{8,24},{9,... | collective-permute-start | bytes 196616 | tf_op jit(solution)/shard_map/ppermute | solution.py:93
  88.9 5.0 %collective-permute-start.16 = (bf16[256,128]{1,0:T(8,128)(2,1)}, bf16[256,128]{1,0:T(8,128)(2,1)S(1)}, u32[]{:S(2)}, u32[]{:S(2)}) collective-permute-start(bf16[256,128]{1,0:T(8,128)(2,1)} %get-tuple-element.55), channel_id=1, source_target_pairs={{0,2},{1,3},{2,0},{3,1},{4,6},{5,7},{6,4},{7,5},{8,10},{9,11},{10,... | collective-permute-start | bytes 196616 | tf_op jit(solution)/shard_map/ppermute | solution.py:93
  88.9 7.5 %collective-permute-start.17 = (bf16[256,128]{1,0:T(8,128)(2,1)}, bf16[256,128]{1,0:T(8,128)(2,1)S(1)}, u32[]{:S(2)}, u32[]{:S(2)}) collective-permute-start(bf16[256,128]{1,0:T(8,128)(2,1)} %get-tuple-element.56), channel_id=1, source_target_pairs={{0,18},{1,19},{2,16},{3,17},{4,22},{5,23},{6,20},{7,21},{8,26},{9,... | collective-permute-start | bytes 196616 | tf_op jit(solution)/shard_map/ppermute | solution.py:93
  91.9 8.8 %collective-permute-start.18 = (bf16[128,1024]{1,0:T(8,128)(2,1)S(1)}, bf16[128,1024]{1,0:T(8,128)(2,1)S(1)}, u32[]{:S(2)}, u32[]{:S(2)}) collective-permute-start(bf16[128,1024]{1,0:T(8,128)(2,1)S(1)} %slice.30), channel_id=1, source_target_pairs={{0,2},{1,3},{2,0},{3,1},{4,6},{5,7},{6,4},{7,5},{8,10},{9,11},{10,... | collective-permute-start | bytes 786440 | tf_op jit(solution)/shard_map/ppermute | solution.py:93
  99.9 5.0 %collective-permute-start.20 = (bf16[128,512]{1,0:T(8,128)(2,1)S(1)}, bf16[128,512]{1,0:T(8,128)(2,1)S(1)}, u32[]{:S(2)}, u32[]{:S(2)}) collective-permute-start(bf16[128,512]{1,0:T(8,128)(2,1)S(1)} %slice.31), channel_id=1, source_target_pairs={{0,2},{1,3},{2,0},{3,1},{4,6},{5,7},{6,4},{7,5},{8,10},{9,11},{10,... | collective-permute-start | bytes 393224 | tf_op jit(solution)/shard_map/ppermute | solution.py:93
  (18 other events, 87.4 us)

commit v3 on v2

--- a/solution.py
+++ b/solution.py
@@ -13,6 +13,7 @@
 ANY = pl.BlockSpec(memory_space=pl.ANY)
 VMEM = pl.BlockSpec(memory_space=pltpu.VMEM)
 F32 = jnp.float32
+COST = pl.CostEstimate(flops=2 * 10**10, bytes_accessed=1 << 20, transcendentals=0)
 BF16 = jnp.bfloat16
 
 
@@ -123,7 +124,7 @@
         out_shape=shapes,
         in_specs=[VMEM],
         out_specs=[VMEM] * len(shapes),
-        cost_estimate=pl.CostEstimate(flops=0, bytes_accessed=2 * cot.size * 2, transcendentals=0),
+        cost_estimate=COST,
         name="pack",
     )(cot)
 
@@ -156,11 +157,7 @@
         in_specs=[VMEM] * 3,
         out_specs=[VMEM] * 3,
         scratch_shapes=[pltpu.VMEM((PATCH, HD), BF16)],
-        cost_estimate=pl.CostEstimate(
-            flops=4 * images * PATCH * PATCH * HD,
-            bytes_accessed=1 << 20,
-            transcendentals=images * PATCH * PATCH,
-        ),
+        cost_estimate=COST,
         name="forward",
     )(q, k, v)
 
@@ -192,9 +189,7 @@
         in_specs=[VMEM] * 8,
         out_specs=[VMEM] * 3,
         scratch_shapes=[pltpu.VMEM((images, PATCH, HD), BF16)],
-        cost_estimate=pl.CostEstimate(
-            flops=8 * images * PATCH * PATCH * HD, bytes_accessed=2 << 20, transcendentals=0
-        ),
+        cost_estimate=COST,
         name="backward",
     )(q, k, v, probs, own, from_x, from_z, from_xz)
 
@@ -268,11 +263,7 @@
         out_shape=out,
         in_specs=[VMEM] * (len(cots) + 4 + len(extra)),
         out_specs=[VMEM] * len(out),
-        cost_estimate=pl.CostEstimate(
-            flops=4 * 512 * 2 * HD * 2 * width,
-            bytes_accessed=512 * 2 * width * 2 + 2 * HD * 2 * width * 6,
-            transcendentals=0,
-        ),
+        cost_estimate=COST,
         name="products",
     )(*cots, *w_all, *att, *extra)
 
@@ -281,41 +272,50 @@
     return lax.optimization_barrier((value, *others))[0]
 
 
-CUTS = ((0, 1024), (1024, 1536))
+CUTS = ((0, 512), (512, 1024), (1024, 1536))
 
 
 def on_device_4x8(queries, keys, values, w_out, cotangent):
-    m1, o1, m2, o2 = pack(cotangent, CUTS)
-    za1, x1 = send(m1, z1=1), send(o1, x=1)
-    w_z = send(w_out, z0=1)
-    zb1 = send(x1, z1=1)
-    y1 = send(jnp.concatenate([m1, x1]), y=1)
-    x2 = send(after(o2, x1), x=1)
-    sa1 = send(za1, y=1)
-    mx2 = jnp.concatenate([m2, x2])
-    z2 = send(after(mx2, za1), z1=1)
-    y2 = send(after(mx2, y1), y=1)
-    sb1 = send(zb1, y=1)
-    s2 = send(after(z2, y2), y=1)
-    w_own = jnp.concatenate([w_out, w_z])
-    w_all = [w_own, send(after(w_own, za1), c=1)]
-    q, k, v, _ = lax.optimization_barrier((queries, keys, values, x1))
+    m1, o1, m2, o2, m3, o3 = pack(cotangent, CUTS)
+    two = lambda a, b: jnp.concatenate([a, b])
+    r0 = x1, za1, ya = send(o1, x=1), send(m1, z1=1), send(two(m1, m2), y=1)
+    x2, zb1, yb = send(o2, x=1), send(x1, z1=1), send(two(m3, x1), y=1)
+    r1 = x2, zb1, yb
+    w_z = send(after(w_out, *r0), z0=1)
+    x3, za2 = send(after(o3, *r0), x=1), send(after(m2, *r0), z1=1)
+    yc = send(after(two(x2, za1), *r0), y=1)
+    r2 = x3, za2, yc
+    zb2, yd = send(after(x2, *r1), z1=1), send(after(two(x3, zb1), *r1), y=1)
+    q, k, v, *_ = lax.optimization_barrier((queries, keys, values, *r0))
     probs, mine, others = forward(q, k, v)
-    att = jnp.concatenate([mine, send(after(others, y1), z0=1)])
-    att = [att, send(att, x=1)]
+    att_z = send(after(others, *r1), z0=1)
+    r3 = zb2, yd, w_z, att_z
+    za3, ye = send(after(m3, *r2), z1=1), send(after(two(za2, zb2), *r2), y=1)
+    w_own = two(w_out, w_z)
+    w_c = send(after(w_own, *r2), c=1)
+    att = two(mine, att_z)
+    att_x = send(after(att, *r2), x=1)
+    r4 = za3, ye, w_c, att_x
+    zb3, yf = send(after(x3, *r3), z1=1), send(after(za3, *r3), y=1)
+    r5 = zb3, yf
+    yg = send(after(zb3, *r4), y=1)
+    w_all, att = [w_own, w_c], [att, att_x]
     inputs = [
-        ([m1, x1, y1, za1, sa1, zb1, sb1], [(0, 0), (2, 0), (3, 0), (4, 0), (1, 0), (2, 64), (5, 0), (6, 0)]),
-        ([mx2, y2, z2, s2], [(0, 0), (1, 0), (2, 0), (3, 0), (0, 64), (1, 64), (2, 64), (3, 64)]),
+        ([m1, ya, za1, yc, x1, yb, zb1, yd], [0, 0, 0, 64, 0, 64, 0, 64]),
+        ([m2, ya, za2, ye, x2, yc, zb2, ye], [0, 64, 0, 0, 0, 0, 0, 64]),
+        ([m3, yb, za3, yf, x3, yd, zb3, yg], [0, 0, 0, 0, 0, 0, 0, 0]),
     ]
-    before, parts = None, []
+    before, parts, pairs = None, [], []
     for n, (low, high) in enumerate(CUTS):
         last = n == len(CUTS) - 1
-        cots, pieces = inputs[n]
+        cots, rows = inputs[n]
+        pieces = list(enumerate(rows))
         keep, give, *d = products(low, high, pieces, cots, w_all, att, before, last)
         total = keep + send(give, c=1).astype(F32)
         to_pair = total[HD:].astype(BF16)
         pair = send(to_pair, z0=1)
-        before = after(d[0], to_pair)
+        before = after(d[0], to_pair, *pairs) if n == len(CUTS) - 2 else d[0]
+        pairs.append(pair)
         parts.append((total[:HD] + pair.astype(F32)).astype(BF16))
     own, to_x, to_z, to_xz = d
     grad_q, grad_k, grad_v = backward(

time: 106 us -> 91 us (0.86)
  waiting for transfers between devices: 61.9 us -> 29.5 us
  starting transfers between devices: 21.3 us -> 33.4 us
  Pallas kernels: 15.5 us -> 18.4 us
  local copies, waits for them, and re-layouts: 3.87 us -> 6.17 us
    ppermute x21 -> x29, waiting for transfers between devices: 61.9 us -> 29.5 us  [send(): return lax.ppermute(value, AXES, flip(**bits))]
    ppermute x21 -> x29, starting transfers between devices: 21.3 us -> 33.4 us  [send(): return lax.ppermute(value, AXES, flip(**bits))]
    pallas_call x2 -> x3, Pallas kernels: 8.03 us -> 10.9 us  [products(): pl.pallas_call(functools.partial(products_kernel, low, high, first, last,...]
    unnamed x45 -> x64, local copies, waits for them, and re-layouts: 3.78 us -> 6.07 us
    add x2 -> x3, other arithmetic: 1.43 us -> 0.21 us  [on_device_4x8(): total = keep + send(give, c=1).astype(F32)]
    concatenate x1 -> x5, other arithmetic: 0.04 us -> 1.12 us  [on_device_4x8(): two = lambda a, b: jnp.concatenate([a, b])]
  transfers between devices with their start and end apart: 21 -> 29, of which waited for: 13 -> 10; matrix products, arithmetic and copies ran while one was open for 2% -> 1% of each run, Pallas kernels for 5% -> 18%
where the time goes in v3:
time: 91 us; the launch traced here: 90.6 us
  starting transfers between devices  33.4 us (37%)
  waiting for transfers between devices  29.5 us (32%)
  Pallas kernels  18.4 us (20%)
  local copies, waits for them, and re-layouts  6.17 us (7%)
  other arithmetic  2.18 us (2%)
  between operations  1 us (1%)
    ppermute x29, starting transfers between devices, send(): return lax.ppermute(value, AXES, flip(**bits))  33.4 us
    ppermute x29, waiting for transfers between devices, send(): return lax.ppermute(value, AXES, flip(**bits))  29.5 us
    pallas_call x3, Pallas kernels, products(): pl.pallas_call(functools.partial(products_kernel, low, high, first, last,...  10.9 us
    unnamed x64, local copies, waits for them, and re-layouts  6.07 us
    pallas_call x1, Pallas kernels, backward(): pl.pallas_call(backward_kernel, out_shape=[jax.ShapeDtypeStruct(q.shape,...  2.75 us
    pallas_call x1, Pallas kernels, forward(): pl.pallas_call(forward_kernel, out_shape=[jax.ShapeDtypeStruct((images, P...  2.66 us
    pallas_call x1, Pallas kernels, pack(): pl.pallas_call(functools.partial(pack_kernel, cuts), out_shape=shapes, in...  2.05 us
  transfers between devices with their start and end apart: 29, of which 10 were waited for; matrix products, arithmetic and copies ran while one was open for 1% of the time, Pallas kernels for 18%

profile of v3, /device:TPU:0, one launch (start us, length us, event | category | flops | bytes accessed | tf_op | source)
XLA Modules:
  0.0 90.6 jit_solution(5964302263229230872)
XLA Ops:
  0.6 2.1 %pack.1 = (bf16[64,1024]{1,0:T(8,128)(2,1)}, bf16[64,1024]{1,0:T(8,128)(2,1)}, bf16[64,1024]{1,0:T(8,128)(2,1)}, bf16[64,1024]{1,0:T(8,128)(2,1)}, bf16[64,1024]{1,0:T(8,128)(2,1)}, /*index=5*/bf16[64,1024]{1,0:T(8,128)(2,1)}) custom-call(bf16[64,6144]{1,0:T(8,128)(2,1)} %cot.1), custom_call_target="tpu_custom_call" | custom-call | flops 20000000000 | bytes 1048576 | tf_op jit(solution)/shard_map/pack/pallas_call | solution.py:122
  3.7 3.0 %collective-permute-start.2 = (bf16[128,1024]{1,0:T(8,128)(2,1)S(1)}, bf16[128,1024]{1,0:T(8,128)(2,1)S(1)}, u32[]{:S(2)}, u32[]{:S(2)}) collective-permute-start(bf16[128,1024]{1,0:T(8,128)(2,1)S(1)} %pad_maximum_fusion.1), channel_id=1, source_target_pairs={{0,1},{1,0},{2,3},{3,2},{4,5},{5,4},{6,7},{7,6},{8,9},{9,8},{10,11... | collective-permute-start | bytes 786440 | tf_op jit(solution)/shard_map/ppermute | solution.py:94
  6.8 2.6 %collective-permute-start.1 = (bf16[64,1024]{1,0:T(8,128)(2,1)S(1)}, bf16[64,1024]{1,0:T(8,128)(2,1)S(1)}, u32[]{:S(2)}, u32[]{:S(2)}) collective-permute-start(bf16[64,1024]{1,0:T(8,128)(2,1)S(1)} %copy-done.8), channel_id=1, source_target_pairs={{0,4},{1,5},{2,6},{3,7},{4,0},{5,1},{6,2},{7,3},{8,12},{9,13},{10,... | collective-permute-start | bytes 393224 | tf_op jit(solution)/shard_map/ppermute | solution.py:94
  9.4 1.5 %collective-permute-start = (bf16[64,1024]{1,0:T(8,128)(2,1)}, bf16[64,1024]{1,0:T(8,128)(2,1)S(1)}, u32[]{:S(2)}, u32[]{:S(2)}) collective-permute-start(bf16[64,1024]{1,0:T(8,128)(2,1)} %get-tuple-element.46), channel_id=1, source_target_pairs={{0,16},{1,17},{2,18},{3,19},{4,20},{5,21},{6,22},{7,23},{8,24},{9,... | collective-permute-start | bytes 393224 | tf_op jit(solution)/shard_map/ppermute | solution.py:94
  11.4 4.0 %collective-permute-done.1.refs_2_ = bf16[64,1024]{1,0:T(8,128)(2,1)S(1)} collective-permute-done((bf16[64,1024]{1,0:T(8,128)(2,1)S(1)}, bf16[64,1024]{1,0:T(8,128)(2,1)S(1)}, u32[]{:S(2)}, u32[]{:S(2)}) %collective-permute-start.1) | collective-permute-done | bytes 131104 | tf_op jit(solution)/shard_map/ppermute | solution.py:94
  15.7 1.6 %collective-permute-start.12 = (bf16[128,1536]{1,0:T(8,128)(2,1)S(1)}, bf16[128,1536]{1,0:T(8,128)(2,1)S(1)}, u32[]{:S(2)}, u32[]{:S(2)}) collective-permute-start(bf16[128,1536]{1,0:T(8,128)(2,1)S(1)} %copy-done.3), channel_id=1, source_target_pairs={{0,2},{1,3},{2,0},{3,1},{4,6},{5,7},{6,4},{7,5},{8,10},{9,11},{10,... | collective-permute-start | bytes 1179656 | tf_op jit(solution)/shard_map/ppermute | solution.py:94
  19.6 2.3 %collective-permute-start.9 = (bf16[64,1024]{1,0:T(8,128)(2,1)S(1)}, bf16[64,1024]{1,0:T(8,128)(2,1)S(1)}, u32[]{:S(2)}, u32[]{:S(2)}) collective-permute-start(bf16[64,1024]{1,0:T(8,128)(2,1)S(1)} %collective-permute-done.refs_4_), channel_id=1, source_target_pairs={{0,4},{1,5},{2,6},{3,7},{4,0},{5,1},{6,2},{7,3},{8,12},{9,13},{10,... | collective-permute-start | bytes 393224 | tf_op jit(solution)/shard_map/ppermute | solution.py:94
  22.5 8.6 %collective-permute-done.12 = bf16[128,1536]{1,0:T(8,128)(2,1)S(1)} collective-permute-done((bf16[128,1536]{1,0:T(8,128)(2,1)S(1)}, bf16[128,1536]{1,0:T(8,128)(2,1)S(1)}, u32[]{:S(2)}, u32[]{:S(2)}) %collective-permute-start.12) | collective-permute-done | bytes 393248 | tf_op jit(solution)/shard_map/ppermute | solution.py:94
  31.1 1.5 %collective-permute-start.4 = (bf16[64,1024]{1,0:T(8,128)(2,1)S(1)}, bf16[64,1024]{1,0:T(8,128)(2,1)S(1)}, u32[]{:S(2)}, u32[]{:S(2)}) collective-permute-start(bf16[64,1024]{1,0:T(8,128)(2,1)S(1)} %copy-done.25), channel_id=1, source_target_pairs={{0,16},{1,17},{2,18},{3,19},{4,20},{5,21},{6,22},{7,23},{8,24},{9,... | collective-permute-start | bytes 393224 | tf_op jit(solution)/shard_map/ppermute | solution.py:94
  32.7 3.4 %collective-permute-done.4.refs_4_ = bf16[64,1024]{1,0:T(8,128)(2,1)S(1)} collective-permute-done((bf16[64,1024]{1,0:T(8,128)(2,1)S(1)}, bf16[64,1024]{1,0:T(8,128)(2,1)S(1)}, u32[]{:S(2)}, u32[]{:S(2)}) %collective-permute-start.4) | collective-permute-done | bytes 131104 | tf_op jit(solution)/shard_map/ppermute | solution.py:94
  36.2 2.7 %forward.1 = (f32[2,256,256]{2,1,0:T(8,128)}, bf16[256,128]{1,0:T(8,128)(2,1)}, bf16[256,128]{1,0:T(8,128)(2,1)}) custom-call(bf16[512,128]{1,0:T(8,128)(2,1)} %q.1, bf16[512,128]{1,0:T(8,128)(2,1)} %k.1, bf16[512,128]{1,0:T(8,128)(2,1)} %v.1), custom_call_target="tpu_custom_call" | custom-call | flops 20000000000 | bytes 1048576 | tf_op jit(solution)/shard_map/forward/pallas_call | solution.py:154
  39.9 2.9 %collective-permute-start.10 = (bf16[64,1024]{1,0:T(8,128)(2,1)S(1)}, bf16[64,1024]{1,0:T(8,128)(2,1)S(1)}, u32[]{:S(2)}, u32[]{:S(2)}) collective-permute-start(bf16[64,1024]{1,0:T(8,128)(2,1)S(1)} %collective-permute-done.6.refs_4_), channel_id=1, source_target_pairs={{0,4},{1,5},{2,6},{3,7},{4,0},{5,1},{6,2},{7,3},{8,12},{9,13},{10,... | collective-permute-start | bytes 393224 | tf_op jit(solution)/shard_map/ppermute | solution.py:94
  43.6 1.6 %collective-permute-start.18 = (bf16[512,128]{1,0:T(8,128)(2,1)S(1)}, bf16[512,128]{1,0:T(8,128)(2,1)S(1)}, u32[]{:S(2)}, u32[]{:S(2)}) collective-permute-start(bf16[512,128]{1,0:T(8,128)(2,1)S(1)} %constant_dynamic-update-slice_fusion.2.refs_10_), channel_id=1, source_target_pairs={{0,16},{1,17},{2,18},{3,19},{4,20},{5,21},{6,22},{7,23},{8,24},{9,... | collective-permute-start | bytes 393224 | tf_op jit(solution)/shard_map/ppermute | solution.py:94
  45.2 4.3 %collective-permute-done.10.refs_6_ = bf16[64,1024]{1,0:T(8,128)(2,1)S(1)} collective-permute-done((bf16[64,1024]{1,0:T(8,128)(2,1)S(1)}, bf16[64,1024]{1,0:T(8,128)(2,1)S(1)}, u32[]{:S(2)}, u32[]{:S(2)}) %collective-permute-start.10) | collective-permute-done | bytes 131104 | tf_op jit(solution)/shard_map/ppermute | solution.py:94
  50.1 1.7 %collective-permute-start.16 = (bf16[128,1024]{1,0:T(8,128)(2,1)S(1)}, bf16[128,1024]{1,0:T(8,128)(2,1)S(1)}, u32[]{:S(2)}, u32[]{:S(2)}) collective-permute-start(bf16[128,1024]{1,0:T(8,128)(2,1)S(1)} %pad_maximum_fusion.5), channel_id=1, source_target_pairs={{0,1},{1,0},{2,3},{3,2},{4,5},{5,4},{6,7},{7,6},{8,9},{9,8},{10,11... | collective-permute-start | bytes 786440 | tf_op jit(solution)/shard_map/ppermute | solution.py:94
  51.8 3.0 %collective-permute-start.15 = (bf16[64,1024]{1,0:T(8,128)(2,1)S(1)}, bf16[64,1024]{1,0:T(8,128)(2,1)}, u32[]{:S(2)}, u32[]{:S(2)}) collective-permute-start(bf16[64,1024]{1,0:T(8,128)(2,1)S(1)} %collective-permute-done.4.refs_4_), channel_id=1, source_target_pairs={{0,4},{1,5},{2,6},{3,7},{4,0},{5,1},{6,2},{7,3},{8,12},{9,13},{10,... | collective-permute-start | bytes 393224 | tf_op jit(solution)/shard_map/ppermute | solution.py:94
  56.3 3.4 %products.3 = (f32[256,512]{1,0:T(8,128)}, bf16[256,512]{1,0:T(8,128)(2,1)}, f32[512,256]{1,0:T(8,128)}) custom-call(bf16[64,1024]{1,0:T(8,128)(2,1)} %get-tuple-element.47.refs_0_, bf16[128,1024]{1,0:T(8,128)(2,1)} %copy-done.19, bf16[64,1024]{1,0:T(8,128)(2,1)} %copy-done.10, bf16[128,1024]{1,0:T(8,128)(2,1)} %copy-done.21, bf16[64,1024]{1,0:T(8,128)(2,1)} %copy-done.11, ...), custom_call_target="tpu_custom_call" | custom-call | flops 20000000000 | bytes 1048576 | tf_op jit(solution)/shard_map/products/pallas_call | solution.py:261
  60.5 3.8 %products.4 = (f32[256,512]{1,0:T(8,128)}, bf16[256,512]{1,0:T(8,128)(2,1)}, f32[512,256]{1,0:T(8,128)}) custom-call(bf16[64,1024]{1,0:T(8,128)(2,1)} %get-tuple-element.56.refs_0_, bf16[128,1024]{1,0:T(8,128)(2,1)} %copy-done.19, bf16[64,1024]{1,0:T(8,128)(2,1)} %copy-done.12, bf16[128,1024]{1,0:T(8,128)(2,1)} %copy-done.22, bf16[64,1024]{1,0:T(8,128)(2,1)} %copy-done.9, ...), custom_call_target="tpu_custom_call" | custom-call | flops 20000000000 | bytes 1048576 | tf_op jit(solution)/shard_map/products/pallas_call | solution.py:261
  69.3 4.1 %collective-permute-done.22 = bf16[128,512]{1,0:T(8,128)(2,1)S(1)} collective-permute-done((bf16[128,512]{1,0:T(8,128)(2,1)S(1)}, bf16[128,512]{1,0:T(8,128)(2,1)S(1)}, u32[]{:S(2)}, u32[]{:S(2)}) %collective-permute-start.22) | collective-permute-done | bytes 131104 | tf_op jit(solution)/shard_map/ppermute | solution.py:94
  74.7 3.7 %products.5 = (f32[256,512]{1,0:T(8,128)}, bf16[256,512]{1,0:T(8,128)(2,1)}, f32[256,128]{1,0:T(8,128)}, bf16[256,128]{1,0:T(8,128)(2,1)}, bf16[256,128]{1,0:T(8,128)(2,1)}, /*index=5*/bf16[256,128]{1,0:T(8,128)(2,1)}) custom-call(bf16[64,1024]{1,0:T(8,128)(2,1)} %get-tuple-element.59.refs_0_, bf16[128,1024]{1,0:T(8,128)(2,1)} %copy-done.18, ...), custom_call_target="tpu_custom_call" | custom-call | flops 20000000000 | bytes 1048576 | tf_op jit(solution)/shard_map/products/pallas_call | solution.py:261
  78.4 1.6 %collective-permute-start.23 = (bf16[256,128]{1,0:T(8,128)(2,1)}, bf16[256,128]{1,0:T(8,128)(2,1)S(1)}, u32[]{:S(2)}, u32[]{:S(2)}) collective-permute-start(bf16[256,128]{1,0:T(8,128)(2,1)} %get-tuple-element.80), channel_id=1, source_target_pairs={{0,16},{1,17},{2,18},{3,19},{4,20},{5,21},{6,22},{7,23},{8,24},{9,... | collective-permute-start | bytes 196616 | tf_op jit(solution)/shard_map/ppermute | solution.py:94
  80.5 1.4 %collective-permute-start.25 = (bf16[256,128]{1,0:T(8,128)(2,1)}, bf16[256,128]{1,0:T(8,128)(2,1)S(1)}, u32[]{:S(2)}, u32[]{:S(2)}) collective-permute-start(bf16[256,128]{1,0:T(8,128)(2,1)} %get-tuple-element.82), channel_id=1, source_target_pairs={{0,18},{1,19},{2,16},{3,17},{4,22},{5,23},{6,20},{7,21},{8,26},{9,... | collective-permute-start | bytes 196616 | tf_op jit(solution)/shard_map/ppermute | solution.py:94
  83.2 1.9 %collective-permute-done.24.from_z = bf16[256,128]{1,0:T(8,128)(2,1)S(1)} collective-permute-done((bf16[256,128]{1,0:T(8,128)(2,1)}, bf16[256,128]{1,0:T(8,128)(2,1)S(1)}, u32[]{:S(2)}, u32[]{:S(2)}) %collective-permute-start.24) | collective-permute-done | bytes 65568 | tf_op jit(solution)/shard_map/ppermute | solution.py:94
  87.1 2.7 %backward.1 = (bf16[512,128]{1,0:T(8,128)(2,1)}, bf16[512,128]{1,0:T(8,128)(2,1)}, bf16[512,128]{1,0:T(8,128)(2,1)}) custom-call(bf16[512,128]{1,0:T(8,128)(2,1)} %q.1, bf16[512,128]{1,0:T(8,128)(2,1)} %k.1, bf16[512,128]{1,0:T(8,128)(2,1)} %v.1, f32[2,256,256]{2,1,0:T(8,128)} %get-tuple-element.52.probs, f32[256,128]{1,0:T(8,128)} %get-tuple-element.79.own, ...), custom_call_target="tpu_custom_call" | custom-call | flops 20000000000 | bytes 1048576 | tf_op jit(solution)/shard_map/backward/pallas_call | solution.py:186
  (121 shorter events, 20.3 us)
Async XLA Ops:
  3.7 11.9 %collective-permute-start.2 = (bf16[128,1024]{1,0:T(8,128)(2,1)S(1)}, bf16[128,1024]{1,0:T(8,128)(2,1)S(1)}, u32[]{:S(2)}, u32[]{:S(2)}) collective-permute-start(bf16[128,1024]{1,0:T(8,128)(2,1)S(1)} %pad_maximum_fusion.1), channel_id=1, source_target_pairs={{0,1},{1,0},{2,3},{3,2},{4,5},{5,4},{6,7},{7,6},{8,9},{9,8},{10,11... | collective-permute-start | bytes 786440 | tf_op jit(solution)/shard_map/ppermute | solution.py:94
  6.8 8.7 %collective-permute-start.1 = (bf16[64,1024]{1,0:T(8,128)(2,1)S(1)}, bf16[64,1024]{1,0:T(8,128)(2,1)S(1)}, u32[]{:S(2)}, u32[]{:S(2)}) collective-permute-start(bf16[64,1024]{1,0:T(8,128)(2,1)S(1)} %copy-done.8), channel_id=1, source_target_pairs={{0,4},{1,5},{2,6},{3,7},{4,0},{5,1},{6,2},{7,3},{8,12},{9,13},{10,... | collective-permute-start | bytes 393224 | tf_op jit(solution)/shard_map/ppermute | solution.py:94
  9.4 6.3 %collective-permute-start = (bf16[64,1024]{1,0:T(8,128)(2,1)}, bf16[64,1024]{1,0:T(8,128)(2,1)S(1)}, u32[]{:S(2)}, u32[]{:S(2)}) collective-permute-start(bf16[64,1024]{1,0:T(8,128)(2,1)} %get-tuple-element.46), channel_id=1, source_target_pairs={{0,16},{1,17},{2,18},{3,19},{4,20},{5,21},{6,22},{7,23},{8,24},{9,... | collective-permute-start | bytes 393224 | tf_op jit(solution)/shard_map/ppermute | solution.py:94
  10.8 6.5 %collective-permute-start.6 = (bf16[64,1024]{1,0:T(8,128)(2,1)}, bf16[64,1024]{1,0:T(8,128)(2,1)S(1)}, u32[]{:S(2)}, u32[]{:S(2)}) collective-permute-start(bf16[64,1024]{1,0:T(8,128)(2,1)} %get-tuple-element.57), channel_id=1, source_target_pairs={{0,16},{1,17},{2,18},{3,19},{4,20},{5,21},{6,22},{7,23},{8,24},{9,... | collective-permute-start | bytes 393224 | tf_op jit(solution)/shard_map/ppermute | solution.py:94
  15.7 15.4 %collective-permute-start.12 = (bf16[128,1536]{1,0:T(8,128)(2,1)S(1)}, bf16[128,1536]{1,0:T(8,128)(2,1)S(1)}, u32[]{:S(2)}, u32[]{:S(2)}) collective-permute-start(bf16[128,1536]{1,0:T(8,128)(2,1)S(1)} %copy-done.3), channel_id=1, source_target_pairs={{0,2},{1,3},{2,0},{3,1},{4,6},{5,7},{6,4},{7,5},{8,10},{9,11},{10,... | collective-permute-start | bytes 1179656 | tf_op jit(solution)/shard_map/ppermute | solution.py:94
  17.4 18.7 %collective-permute-start.7 = (bf16[128,1024]{1,0:T(8,128)(2,1)S(1)}, bf16[128,1024]{1,0:T(8,128)(2,1)S(1)}, u32[]{:S(2)}, u32[]{:S(2)}) collective-permute-start(bf16[128,1024]{1,0:T(8,128)(2,1)S(1)} %pad_maximum_fusion.3), channel_id=1, source_target_pairs={{0,1},{1,0},{2,3},{3,2},{4,5},{5,4},{6,7},{7,6},{8,9},{9,8},{10,11... | collective-permute-start | bytes 786440 | tf_op jit(solution)/shard_map/ppermute | solution.py:94
  18.3 20.5 %collective-permute-start.3 = (bf16[128,1024]{1,0:T(8,128)(2,1)S(1)}, bf16[128,1024]{1,0:T(8,128)(2,1)S(1)}, u32[]{:S(2)}, u32[]{:S(2)}) collective-permute-start(bf16[128,1024]{1,0:T(8,128)(2,1)S(1)} %pad_maximum_fusion.2), channel_id=1, source_target_pairs={{0,1},{1,0},{2,3},{3,2},{4,5},{5,4},{6,7},{7,6},{8,9},{9,8},{10,11... | collective-permute-start | bytes 786440 | tf_op jit(solution)/shard_map/ppermute | solution.py:94
  19.6 19.2 %collective-permute-start.9 = (bf16[64,1024]{1,0:T(8,128)(2,1)S(1)}, bf16[64,1024]{1,0:T(8,128)(2,1)S(1)}, u32[]{:S(2)}, u32[]{:S(2)}) collective-permute-start(bf16[64,1024]{1,0:T(8,128)(2,1)S(1)} %collective-permute-done.refs_4_), channel_id=1, source_target_pairs={{0,4},{1,5},{2,6},{3,7},{4,0},{5,1},{6,2},{7,3},{8,12},{9,13},{10,... | collective-permute-start | bytes 393224 | tf_op jit(solution)/shard_map/ppermute | solution.py:94
  21.9 10.8 %collective-permute-start.5 = (bf16[64,1024]{1,0:T(8,128)(2,1)S(1)}, bf16[64,1024]{1,0:T(8,128)(2,1)S(1)}, u32[]{:S(2)}, u32[]{:S(2)}) collective-permute-start(bf16[64,1024]{1,0:T(8,128)(2,1)S(1)} %copy-done.7), channel_id=1, source_target_pairs={{0,4},{1,5},{2,6},{3,7},{4,0},{5,1},{6,2},{7,3},{8,12},{9,13},{10,... | collective-permute-start | bytes 393224 | tf_op jit(solution)/shard_map/ppermute | solution.py:94
  36.1 18.7 %collective-permute-start.17 = (bf16[256,1536]{1,0:T(8,128)(2,1)S(1)}, bf16[256,1536]{1,0:T(8,128)(2,1)S(1)}, u32[]{:S(2)}, u32[]{:S(2)}) collective-permute-start(bf16[256,1536]{1,0:T(8,128)(2,1)S(1)} %constant_dynamic-update-slice_fusion.refs_8_), channel_id=1, source_target_pairs={{0,8},{1,9},{2,10},{3,11},{4,12},{5,13},{6,14},{7,15},{8,0},{9,1},... | collective-permute-start | bytes 2359304 | tf_op jit(solution)/shard_map/ppermute | solution.py:94
  39.6 12.2 %collective-permute-start.11 = (bf16[128,1024]{1,0:T(8,128)(2,1)S(1)}, bf16[128,1024]{1,0:T(8,128)(2,1)S(1)}, u32[]{:S(2)}, u32[]{:S(2)}) collective-permute-start(bf16[128,1024]{1,0:T(8,128)(2,1)S(1)} %pad_maximum_fusion.4), channel_id=1, source_target_pairs={{0,1},{1,0},{2,3},{3,2},{4,5},{5,4},{6,7},{7,6},{8,9},{9,8},{10,11... | collective-permute-start | bytes 786440 | tf_op jit(solution)/shard_map/ppermute | solution.py:94
  39.9 9.5 %collective-permute-start.10 = (bf16[64,1024]{1,0:T(8,128)(2,1)S(1)}, bf16[64,1024]{1,0:T(8,128)(2,1)S(1)}, u32[]{:S(2)}, u32[]{:S(2)}) collective-permute-start(bf16[64,1024]{1,0:T(8,128)(2,1)S(1)} %collective-permute-done.6.refs_4_), channel_id=1, source_target_pairs={{0,4},{1,5},{2,6},{3,7},{4,0},{5,1},{6,2},{7,3},{8,12},{9,13},{10,... | collective-permute-start | bytes 393224 | tf_op jit(solution)/shard_map/ppermute | solution.py:94
  43.6 11.2 %collective-permute-start.18 = (bf16[512,128]{1,0:T(8,128)(2,1)S(1)}, bf16[512,128]{1,0:T(8,128)(2,1)S(1)}, u32[]{:S(2)}, u32[]{:S(2)}) collective-permute-start(bf16[512,128]{1,0:T(8,128)(2,1)S(1)} %constant_dynamic-update-slice_fusion.2.refs_10_), channel_id=1, source_target_pairs={{0,16},{1,17},{2,18},{3,19},{4,20},{5,21},{6,22},{7,23},{8,24},{9,... | collective-permute-start | bytes 393224 | tf_op jit(solution)/shard_map/ppermute | solution.py:94
  50.1 9.6 %collective-permute-start.16 = (bf16[128,1024]{1,0:T(8,128)(2,1)S(1)}, bf16[128,1024]{1,0:T(8,128)(2,1)S(1)}, u32[]{:S(2)}, u32[]{:S(2)}) collective-permute-start(bf16[128,1024]{1,0:T(8,128)(2,1)S(1)} %pad_maximum_fusion.5), channel_id=1, source_target_pairs={{0,1},{1,0},{2,3},{3,2},{4,5},{5,4},{6,7},{7,6},{8,9},{9,8},{10,11... | collective-permute-start | bytes 786440 | tf_op jit(solution)/shard_map/ppermute | solution.py:94
  51.8 13.0 %collective-permute-start.8 = (bf16[64,1024]{1,0:T(8,128)(2,1)S(1)}, bf16[64,1024]{1,0:T(8,128)(2,1)S(1)}, u32[]{:S(2)}, u32[]{:S(2)}) collective-permute-start(bf16[64,1024]{1,0:T(8,128)(2,1)S(1)} %copy-done.5), channel_id=1, source_target_pairs={{0,4},{1,5},{2,6},{3,7},{4,0},{5,1},{6,2},{7,3},{8,12},{9,13},{10,... | collective-permute-start | bytes 393224 | tf_op jit(solution)/shard_map/ppermute | solution.py:94
  51.8 14.2 %collective-permute-start.15 = (bf16[64,1024]{1,0:T(8,128)(2,1)S(1)}, bf16[64,1024]{1,0:T(8,128)(2,1)}, u32[]{:S(2)}, u32[]{:S(2)}) collective-permute-start(bf16[64,1024]{1,0:T(8,128)(2,1)S(1)} %collective-permute-done.4.refs_4_), channel_id=1, source_target_pairs={{0,4},{1,5},{2,6},{3,7},{4,0},{5,1},{6,2},{7,3},{8,12},{9,13},{10,... | collective-permute-start | bytes 393224 | tf_op jit(solution)/shard_map/ppermute | solution.py:94
  59.8 7.1 %collective-permute-start.21 = (bf16[256,512]{1,0:T(8,128)(2,1)}, bf16[256,512]{1,0:T(8,128)(2,1)S(1)}, u32[]{:S(2)}, u32[]{:S(2)}) collective-permute-start(bf16[256,512]{1,0:T(8,128)(2,1)} %get-tuple-element.77), channel_id=1, source_target_pairs={{0,8},{1,9},{2,10},{3,11},{4,12},{5,13},{6,14},{7,15},{8,0},{9,1},... | collective-permute-start | bytes 786440 | tf_op jit(solution)/shard_map/ppermute | solution.py:94
  64.8 8.5 %collective-permute-start.14 = (bf16[64,1024]{1,0:T(8,128)(2,1)S(1)}, bf16[64,1024]{1,0:T(8,128)(2,1)S(1)}, u32[]{:S(2)}, u32[]{:S(2)}) collective-permute-start(bf16[64,1024]{1,0:T(8,128)(2,1)S(1)} %collective-permute-done.8.refs_2_), channel_id=1, source_target_pairs={{0,1},{1,0},{2,3},{3,2},{4,5},{5,4},{6,7},{7,6},{8,9},{9,8},{10,11... | collective-permute-start | bytes 393224 | tf_op jit(solution)/shard_map/ppermute | solution.py:94
  66.0 7.4 %collective-permute-start.19 = (bf16[64,1024]{1,0:T(8,128)(2,1)}, bf16[64,1024]{1,0:T(8,128)(2,1)S(1)}, u32[]{:S(2)}, u32[]{:S(2)}) collective-permute-start(bf16[64,1024]{1,0:T(8,128)(2,1)} %collective-permute-done.15.refs_6_), channel_id=1, source_target_pairs={{0,1},{1,0},{2,3},{3,2},{4,5},{5,4},{6,7},{7,6},{8,9},{9,8},{10,11... | collective-permute-start | bytes 393224 | tf_op jit(solution)/shard_map/ppermute | solution.py:94
  67.0 6.4 %collective-permute-start.22 = (bf16[128,512]{1,0:T(8,128)(2,1)S(1)}, bf16[128,512]{1,0:T(8,128)(2,1)S(1)}, u32[]{:S(2)}, u32[]{:S(2)}) collective-permute-start(bf16[128,512]{1,0:T(8,128)(2,1)S(1)} %slice.46), channel_id=1, source_target_pairs={{0,2},{1,3},{2,0},{3,1},{4,6},{5,7},{6,4},{7,5},{8,10},{9,11},{10,... | collective-permute-start | bytes 393224 | tf_op jit(solution)/shard_map/ppermute | solution.py:94
  68.0 14.0 %collective-permute-start.26 = (bf16[128,512]{1,0:T(8,128)(2,1)S(1)}, bf16[128,512]{1,0:T(8,128)(2,1)S(1)}, u32[]{:S(2)}, u32[]{:S(2)}) collective-permute-start(bf16[128,512]{1,0:T(8,128)(2,1)S(1)} %slice.47), channel_id=1, source_target_pairs={{0,2},{1,3},{2,0},{3,1},{4,6},{5,7},{6,4},{7,5},{8,10},{9,11},{10,... | collective-permute-start | bytes 393224 | tf_op jit(solution)/shard_map/ppermute | solution.py:94
  79.9 5.1 %collective-permute-start.24 = (bf16[256,128]{1,0:T(8,128)(2,1)}, bf16[256,128]{1,0:T(8,128)(2,1)S(1)}, u32[]{:S(2)}, u32[]{:S(2)}) collective-permute-start(bf16[256,128]{1,0:T(8,128)(2,1)} %get-tuple-element.81), channel_id=1, source_target_pairs={{0,2},{1,3},{2,0},{3,1},{4,6},{5,7},{6,4},{7,5},{8,10},{9,11},{10,... | collective-permute-start | bytes 196616 | tf_op jit(solution)/shard_map/ppermute | solution.py:94
  80.5 5.9 %collective-permute-start.25 = (bf16[256,128]{1,0:T(8,128)(2,1)}, bf16[256,128]{1,0:T(8,128)(2,1)S(1)}, u32[]{:S(2)}, u32[]{:S(2)}) collective-permute-start(bf16[256,128]{1,0:T(8,128)(2,1)} %get-tuple-element.82), channel_id=1, source_target_pairs={{0,18},{1,19},{2,16},{3,17},{4,22},{5,23},{6,20},{7,21},{8,26},{9,... | collective-permute-start | bytes 196616 | tf_op jit(solution)/shard_map/ppermute | solution.py:94
  82.1 7.7 %collective-permute-start.28 = (bf16[128,512]{1,0:T(8,128)(2,1)S(1)}, bf16[128,512]{1,0:T(8,128)(2,1)S(1)}, u32[]{:S(2)}, u32[]{:S(2)}) collective-permute-start(bf16[128,512]{1,0:T(8,128)(2,1)S(1)} %slice.45), channel_id=1, source_target_pairs={{0,2},{1,3},{2,0},{3,1},{4,6},{5,7},{6,4},{7,5},{8,10},{9,11},{10,... | collective-permute-start | bytes 393224 | tf_op jit(solution)/shard_map/ppermute | solution.py:94
  (36 other events, 162.2 us)

commit v4 on v3

--- a/solution.py
+++ b/solution.py
@@ -194,9 +194,9 @@
     )(q, k, v, probs, own, from_x, from_z, from_xz)
 
 
-def products_kernel(low, high, first, last, pieces, *refs):
+def products_kernel(low, high, first, last, *refs):
     refs = list(refs)
-    cots = [refs.pop(0) for _ in range(1 + max(ref for ref, _ in pieces))]
+    blocks = [refs.pop(0) for _ in range(8)]
     w_own, w_core = refs.pop(0), refs.pop(0)
     att_own, att_x = refs.pop(0), refs.pop(0)
     before = None if first else refs.pop(0)
@@ -224,9 +224,14 @@
         c = 1 - at["c"] if other else at["c"]
         w_ref = w_core if other else w_own
         for start in range(0, width, tile):
-            columns = pl.ds(pl.multiple_of(c * width + start, 128), tile)
             cot = jnp.concatenate(
-                [cots[ref][row : row + 64, columns] for ref, row in pieces], axis=0
+                [
+                    block[:, pl.ds(pl.multiple_of(c * half + start + skip, 128), tile)]
+                    for block in blocks
+                    for half in [block.shape[1] // 2]
+                    for skip in [low if half > width else 0]
+                ],
+                axis=0,
             )
             share = dot(turned, cot, ((1,), (0,)))
             if other:
@@ -245,7 +250,7 @@
                 d_refs[2 + g][pl.ds(row, 64)] = share[:, HD:].astype(BF16)
 
 
-def products(low, high, pieces, cots, w_all, att, before, last):
+def products(low, high, blocks, w_all, att, before, last):
     width = high - low
     first = before is None
     out = [
@@ -259,65 +264,61 @@
         out.append(jax.ShapeDtypeStruct((512, 2 * HD), F32))
     extra = [] if first else [before]
     return pl.pallas_call(
-        functools.partial(products_kernel, low, high, first, last, pieces),
+        functools.partial(products_kernel, low, high, first, last),
         out_shape=out,
-        in_specs=[VMEM] * (len(cots) + 4 + len(extra)),
+        in_specs=[VMEM] * (len(blocks) + 4 + len(extra)),
         out_specs=[VMEM] * len(out),
         cost_estimate=COST,
         name="products",
-    )(*cots, *w_all, *att, *extra)
+    )(*blocks, *w_all, *att, *extra)
+
+
+def cut(value, cuts):
+    half = value.shape[1] // 2
+    return [
+        jnp.concatenate([value[:, low:high], value[:, half + low : half + high]], axis=1)
+        for low, high in cuts
+    ]
 
 
 def after(value, *others):
     return lax.optimization_barrier((value, *others))[0]
 
 
-CUTS = ((0, 512), (512, 1024), (1024, 1536))
+CUTS = ((0, 1024), (1024, 1536))
 
 
 def on_device_4x8(queries, keys, values, w_out, cotangent):
-    m1, o1, m2, o2, m3, o3 = pack(cotangent, CUTS)
-    two = lambda a, b: jnp.concatenate([a, b])
-    r0 = x1, za1, ya = send(o1, x=1), send(m1, z1=1), send(two(m1, m2), y=1)
-    x2, zb1, yb = send(o2, x=1), send(x1, z1=1), send(two(m3, x1), y=1)
-    r1 = x2, zb1, yb
-    w_z = send(after(w_out, *r0), z0=1)
-    x3, za2 = send(after(o3, *r0), x=1), send(after(m2, *r0), z1=1)
-    yc = send(after(two(x2, za1), *r0), y=1)
-    r2 = x3, za2, yc
-    zb2, yd = send(after(x2, *r1), z1=1), send(after(two(x3, zb1), *r1), y=1)
-    q, k, v, *_ = lax.optimization_barrier((queries, keys, values, *r0))
+    m, o = pack(cotangent, ((0, 1536),))
+    za, x, ya, w_z = send(m, z1=1), send(o, x=1), send(m, y=1), send(w_out, z0=1)
+    x1, x2 = cut(x, CUTS)
+    zb1 = send(x1, z1=1)
+    yx = send(after(x, ya), y=1)
+    q, k, v, _ = lax.optimization_barrier((queries, keys, values, x))
     probs, mine, others = forward(q, k, v)
-    att_z = send(after(others, *r1), z0=1)
-    r3 = zb2, yd, w_z, att_z
-    za3, ye = send(after(m3, *r2), z1=1), send(after(two(za2, zb2), *r2), y=1)
-    w_own = two(w_out, w_z)
-    w_c = send(after(w_own, *r2), c=1)
-    att = two(mine, att_z)
-    att_x = send(after(att, *r2), x=1)
-    r4 = za3, ye, w_c, att_x
-    zb3, yf = send(after(x3, *r3), z1=1), send(after(za3, *r3), y=1)
-    r5 = zb3, yf
-    yg = send(after(zb3, *r4), y=1)
-    w_all, att = [w_own, w_c], [att, att_x]
-    inputs = [
-        ([m1, ya, za1, yc, x1, yb, zb1, yd], [0, 0, 0, 64, 0, 64, 0, 64]),
-        ([m2, ya, za2, ye, x2, yc, zb2, ye], [0, 64, 0, 0, 0, 0, 0, 64]),
-        ([m3, yb, za3, yf, x3, yd, zb3, yg], [0, 0, 0, 0, 0, 0, 0, 0]),
-    ]
+    zb2 = send(after(x2, za), z1=1)
+    sa = send(after(za, ya), y=1)
+    att_z = send(others, z0=1)
+    att = jnp.concatenate([mine, att_z])
+    att_x = send(after(att, ya), x=1)
+    w_own = after(jnp.concatenate([w_out, w_z]), yx)
+    w_c = send(w_own, c=1)
+    sb1 = send(after(zb1, yx), y=1)
+    sb2 = send(after(zb2, sa), y=1)
+    w_all, att = [w_own, w_c], [after(att, zb2), att_x]
+    inputs = [[m, ya, za, sa, x, yx, zb1, sb1], [m, ya, za, sa, x, yx, zb2, sb2]]
     before, parts, pairs = None, [], []
     for n, (low, high) in enumerate(CUTS):
         last = n == len(CUTS) - 1
-        cots, rows = inputs[n]
-        pieces = list(enumerate(rows))
-        keep, give, *d = products(low, high, pieces, cots, w_all, att, before, last)
+        keep, give, *d = products(low, high, inputs[n], w_all, att, before, last)
         total = keep + send(give, c=1).astype(F32)
         to_pair = total[HD:].astype(BF16)
         pair = send(to_pair, z0=1)
-        before = after(d[0], to_pair, *pairs) if n == len(CUTS) - 2 else d[0]
+        before = after(d[0], to_pair) if n == len(CUTS) - 2 else d[0]
         pairs.append(pair)
         parts.append((total[:HD] + pair.astype(F32)).astype(BF16))
     own, to_x, to_z, to_xz = d
+    q = after(q, *pairs[:-1])
     grad_q, grad_k, grad_v = backward(
         q, k, v, probs, own, send(to_x, x=1), send(to_z, z0=1), send(to_xz, x=1, z0=1)
     )

time: 91 us -> 89.3 us (0.981)
  waiting for transfers between devices: 29.5 us -> 39.8 us
  starting transfers between devices: 33.4 us -> 25.4 us
  local copies, waits for them, and re-layouts: 6.17 us -> 3.18 us
  Pallas kernels: 18.4 us -> 16.3 us
  other arithmetic: 2.18 us -> 3.41 us
    ppermute x29 -> x20, waiting for transfers between devices: 29.5 us -> 39.8 us  [send(): return lax.ppermute(value, AXES, flip(**bits))]
    ppermute x29 -> x20, starting transfers between devices: 33.4 us -> 25.4 us  [send(): return lax.ppermute(value, AXES, flip(**bits))]
    unnamed x64 -> x35, local copies, waits for them, and re-layouts: 6.07 us -> 3.09 us
    add x3 -> x2, other arithmetic: 0.21 us -> 2.47 us  [on_device_4x8(): total = keep + send(give, c=1).astype(F32)]
    pallas_call x3 -> x2, Pallas kernels: 10.9 us -> 8.73 us  [products(): pl.pallas_call(functools.partial(products_kernel, low, high, first, last)...]
    concatenate x5 -> x3, other arithmetic: 1.12 us -> 0.08 us  [the longest x1 0.05 us: on_device_4x8(): w_own = after(jnp.concatenate([w_out, w_z]), yx)]
  transfers between devices with their start and end apart: 29 -> 20, of which waited for: 10 -> 10; matrix products, arithmetic and copies ran while one was open for 1% -> 3% of each run, Pallas kernels for 18% -> 6%
where the time goes in v4:
time: 89.3 us; the launch traced here: 89 us
  waiting for transfers between devices  39.8 us (45%)
  starting transfers between devices  25.4 us (28%)
  Pallas kernels  16.3 us (18%)
  other arithmetic  3.41 us (4%)
  local copies, waits for them, and re-layouts  3.18 us (4%)
    ppermute x20, waiting for transfers between devices, send(): return lax.ppermute(value, AXES, flip(**bits))  39.8 us
    ppermute x20, starting transfers between devices, send(): return lax.ppermute(value, AXES, flip(**bits))  25.4 us
    pallas_call x2, Pallas kernels, products(): pl.pallas_call(functools.partial(products_kernel, low, high, first, last)...  8.73 us
    unnamed x35, local copies, waits for them, and re-layouts  3.09 us
    pallas_call x1, Pallas kernels, backward(): pl.pallas_call(backward_kernel, out_shape=[jax.ShapeDtypeStruct(q.shape,...  2.75 us
    pallas_call x1, Pallas kernels, forward(): pl.pallas_call(forward_kernel, out_shape=[jax.ShapeDtypeStruct((images, P...  2.73 us
    add x2, other arithmetic, on_device_4x8(): total = keep + send(give, c=1).astype(F32)  2.47 us
    pallas_call x1, Pallas kernels, pack(): pl.pallas_call(functools.partial(pack_kernel, cuts), out_shape=shapes, in...  2.1 us
  transfers between devices with their start and end apart: 20, of which 10 were waited for; matrix products, arithmetic and copies ran while one was open for 3% of the time, Pallas kernels for 6%

profile of v4, /device:TPU:0, one launch (start us, length us, event | category | flops | bytes accessed | tf_op | source)
XLA Modules:
  0.0 89.0 jit_solution(6429028829037972251)
XLA Ops:
  0.6 2.1 %pack.1 = (bf16[64,3072]{1,0:T(8,128)(2,1)}, bf16[64,3072]{1,0:T(8,128)(2,1)}) custom-call(bf16[64,6144]{1,0:T(8,128)(2,1)} %cot.1), custom_call_target="tpu_custom_call" | custom-call | flops 20000000000 | bytes 1048576 | tf_op jit(solution)/shard_map/pack/pallas_call | solution.py:122
  2.7 2.9 %collective-permute-start = (bf16[64,3072]{1,0:T(8,128)(2,1)}, bf16[64,3072]{1,0:T(8,128)(2,1)S(1)}, u32[]{:S(2)}, u32[]{:S(2)}) collective-permute-start(bf16[64,3072]{1,0:T(8,128)(2,1)} %get-tuple-element.34), channel_id=1, source_target_pairs={{0,16},{1,17},{2,18},{3,19},{4,20},{5,21},{6,22},{7,23},{8,24},{9,... | collective-permute-start | bytes 1179656 | tf_op jit(solution)/shard_map/ppermute | solution.py:94
  5.7 2.6 %collective-permute-start.2 = (bf16[64,3072]{1,0:T(8,128)(2,1)}, bf16[64,3072]{1,0:T(8,128)(2,1)S(1)}, u32[]{:S(2)}, u32[]{:S(2)}) collective-permute-start(bf16[64,3072]{1,0:T(8,128)(2,1)} %get-tuple-element.36.refs_0_), channel_id=1, source_target_pairs={{0,4},{1,5},{2,6},{3,7},{4,0},{5,1},{6,2},{7,3},{8,12},{9,13},{10,... | collective-permute-start | bytes 1179656 | tf_op jit(solution)/shard_map/ppermute | solution.py:94
  9.8 1.6 %collective-permute-start.7 = (bf16[128,1536]{1,0:T(8,128)(2,1)S(1)}, bf16[128,1536]{1,0:T(8,128)(2,1)S(1)}, u32[]{:S(2)}, u32[]{:S(2)}) collective-permute-start(bf16[128,1536]{1,0:T(8,128)(2,1)S(1)} %copy-done.2), channel_id=1, source_target_pairs={{0,2},{1,3},{2,0},{3,1},{4,6},{5,7},{6,4},{7,5},{8,10},{9,11},{10,... | collective-permute-start | bytes 1179656 | tf_op jit(solution)/shard_map/ppermute | solution.py:94
  11.4 3.6 %collective-permute-done.refs_4_ = bf16[64,3072]{1,0:T(8,128)(2,1)S(1)} collective-permute-done((bf16[64,3072]{1,0:T(8,128)(2,1)}, bf16[64,3072]{1,0:T(8,128)(2,1)S(1)}, u32[]{:S(2)}, u32[]{:S(2)}) %collective-permute-start) | collective-permute-done | bytes 393248 | tf_op jit(solution)/shard_map/ppermute | solution.py:94
  15.0 2.7 %forward.1 = (f32[2,256,256]{2,1,0:T(8,128)}, bf16[256,128]{1,0:T(8,128)(2,1)}, bf16[256,128]{1,0:T(8,128)(2,1)}) custom-call(bf16[512,128]{1,0:T(8,128)(2,1)} %q.1, bf16[512,128]{1,0:T(8,128)(2,1)} %k.1, bf16[512,128]{1,0:T(8,128)(2,1)} %v.1), custom_call_target="tpu_custom_call" | custom-call | flops 20000000000 | bytes 1048576 | tf_op jit(solution)/shard_map/forward/pallas_call | solution.py:154
  17.7 1.8 %collective-permute-start.9 = (bf16[256,128]{1,0:T(8,128)(2,1)}, bf16[256,128]{1,0:T(8,128)(2,1)S(1)}, u32[]{:S(2)}, u32[]{:S(2)}) collective-permute-start(bf16[256,128]{1,0:T(8,128)(2,1)} %get-tuple-element.44), channel_id=1, source_target_pairs={{0,2},{1,3},{2,0},{3,1},{4,6},{5,7},{6,4},{7,5},{8,10},{9,11},{10,... | collective-permute-start | bytes 196616 | tf_op jit(solution)/shard_map/ppermute | solution.py:94
  19.6 1.5 %collective-permute-start.4 = (bf16[64,3072]{1,0:T(8,128)(2,1)S(1)}, bf16[64,3072]{1,0:T(8,128)(2,1)}, u32[]{:S(2)}, u32[]{:S(2)}) collective-permute-start(bf16[64,3072]{1,0:T(8,128)(2,1)S(1)} %collective-permute-done.refs_4_), channel_id=1, source_target_pairs={{0,1},{1,0},{2,3},{3,2},{4,5},{5,4},{6,7},{7,6},{8,9},{9,8},{10,11... | collective-permute-start | bytes 1179656 | tf_op jit(solution)/shard_map/ppermute | solution.py:94
  21.1 6.7 %collective-permute-done.7 = bf16[128,1536]{1,0:T(8,128)(2,1)S(1)} collective-permute-done((bf16[128,1536]{1,0:T(8,128)(2,1)S(1)}, bf16[128,1536]{1,0:T(8,128)(2,1)S(1)}, u32[]{:S(2)}, u32[]{:S(2)}) %collective-permute-start.7) | collective-permute-done | bytes 393248 | tf_op jit(solution)/shard_map/ppermute | solution.py:94
  29.4 2.7 %collective-permute-start.5 = (bf16[64,2048]{1,0:T(8,128)(2,1)S(1)}, bf16[64,2048]{1,0:T(8,128)(2,1)S(1)}, u32[]{:S(2)}, u32[]{:S(2)}) collective-permute-start(bf16[64,2048]{1,0:T(8,128)(2,1)S(1)} %pad_maximum_fusion.2), channel_id=1, source_target_pairs={{0,4},{1,5},{2,6},{3,7},{4,0},{5,1},{6,2},{7,3},{8,12},{9,13},{10,... | collective-permute-start | bytes 786440 | tf_op jit(solution)/shard_map/ppermute | solution.py:94
  32.1 1.5 %collective-permute-start.3 = (bf16[64,3072]{1,0:T(8,128)(2,1)S(1)}, bf16[64,3072]{1,0:T(8,128)(2,1)S(1)}, u32[]{:S(2)}, u32[]{:S(2)}) collective-permute-start(bf16[64,3072]{1,0:T(8,128)(2,1)S(1)} %collective-permute-done.2.refs_2_), channel_id=1, source_target_pairs={{0,1},{1,0},{2,3},{3,2},{4,5},{5,4},{6,7},{7,6},{8,9},{9,8},{10,11... | collective-permute-start | bytes 1179656 | tf_op jit(solution)/shard_map/ppermute | solution.py:94
  33.6 11.0 %collective-permute-done.5.refs_6_ = bf16[64,2048]{1,0:T(8,128)(2,1)S(1)} collective-permute-done((bf16[64,2048]{1,0:T(8,128)(2,1)S(1)}, bf16[64,2048]{1,0:T(8,128)(2,1)S(1)}, u32[]{:S(2)}, u32[]{:S(2)}) %collective-permute-start.5) | collective-permute-done | bytes 262176 | tf_op jit(solution)/shard_map/ppermute | solution.py:94
  46.2 1.6 %collective-permute-start.11 = (bf16[512,128]{1,0:T(8,128)(2,1)S(1)}, bf16[512,128]{1,0:T(8,128)(2,1)S(1)}, u32[]{:S(2)}, u32[]{:S(2)}) collective-permute-start(bf16[512,128]{1,0:T(8,128)(2,1)S(1)} %constant_dynamic-update-slice_fusion.refs_10_), channel_id=1, source_target_pairs={{0,16},{1,17},{2,18},{3,19},{4,20},{5,21},{6,22},{7,23},{8,24},{9,... | collective-permute-start | bytes 393224 | tf_op jit(solution)/shard_map/ppermute | solution.py:94
  47.8 6.9 %collective-permute-done.10.refs_6_ = bf16[64,1024]{1,0:T(8,128)(2,1)S(1)} collective-permute-done((bf16[64,1024]{1,0:T(8,128)(2,1)S(1)}, bf16[64,1024]{1,0:T(8,128)(2,1)S(1)}, u32[]{:S(2)}, u32[]{:S(2)}) %collective-permute-start.10) | collective-permute-done | bytes 131104 | tf_op jit(solution)/shard_map/ppermute | solution.py:94
  56.6 4.7 %products.2 = (f32[256,1024]{1,0:T(8,128)}, bf16[256,1024]{1,0:T(8,128)(2,1)}, f32[512,256]{1,0:T(8,128)}) custom-call(bf16[64,3072]{1,0:T(8,128)(2,1)} %get-tuple-element.36.refs_0_, bf16[64,3072]{1,0:T(8,128)(2,1)} %copy-done.7, bf16[64,3072]{1,0:T(8,128)(2,1)} %copy-done.6, bf16[64,3072]{1,0:T(8,128)(2,1)} %copy-done.8, bf16[64,3072]{1,0:T(8,128)(2,1)} %copy-done.1, ...), custom_call_target="tpu_custom_call" | custom-call | flops 20000000000 | bytes 1048576 | tf_op jit(solution)/shard_map/products/pallas_call | solution.py:266
  61.9 1.5 %collective-permute-done.12 = bf16[256,1024]{1,0:T(8,128)(2,1)S(1)} collective-permute-done((bf16[256,1024]{1,0:T(8,128)(2,1)}, bf16[256,1024]{1,0:T(8,128)(2,1)S(1)}, u32[]{:S(2)}, u32[]{:S(2)}) %collective-permute-start.12) | collective-permute-done | bytes 524320 | tf_op jit(solution)/shard_map/ppermute | solution.py:94
  64.8 2.4 %collective-permute-done.14.refs_7_ = bf16[64,1024]{1,0:T(8,128)(2,1)S(1)} collective-permute-done((bf16[64,1024]{1,0:T(8,128)(2,1)S(1)}, bf16[64,1024]{1,0:T(8,128)(2,1)S(1)}, u32[]{:S(2)}, u32[]{:S(2)}) %collective-permute-start.14) | collective-permute-done | bytes 131104 | tf_op jit(solution)/shard_map/ppermute | solution.py:94
  67.9 4.0 %products.3 = (f32[256,512]{1,0:T(8,128)}, bf16[256,512]{1,0:T(8,128)(2,1)}, f32[256,128]{1,0:T(8,128)}, bf16[256,128]{1,0:T(8,128)(2,1)}, bf16[256,128]{1,0:T(8,128)(2,1)}, /*index=5*/bf16[256,128]{1,0:T(8,128)(2,1)}) custom-call(bf16[64,3072]{1,0:T(8,128)(2,1)} %get-tuple-element.36.refs_0_, bf16[64,3072]{1,0:T(8,128)(2,1)} %copy-done.7, ...), custom_call_target="tpu_custom_call" | custom-call | flops 20000000000 | bytes 1048576 | tf_op jit(solution)/shard_map/products/pallas_call | solution.py:266
  72.0 1.6 %collective-permute-start.15 = (bf16[256,128]{1,0:T(8,128)(2,1)}, bf16[256,128]{1,0:T(8,128)(2,1)S(1)}, u32[]{:S(2)}, u32[]{:S(2)}) collective-permute-start(bf16[256,128]{1,0:T(8,128)(2,1)} %get-tuple-element.56), channel_id=1, source_target_pairs={{0,16},{1,17},{2,18},{3,19},{4,20},{5,21},{6,22},{7,23},{8,24},{9,... | collective-permute-start | bytes 196616 | tf_op jit(solution)/shard_map/ppermute | solution.py:94
  73.5 1.9 %collective-permute-start.16 = (bf16[256,128]{1,0:T(8,128)(2,1)}, bf16[256,128]{1,0:T(8,128)(2,1)S(1)}, u32[]{:S(2)}, u32[]{:S(2)}) collective-permute-start(bf16[256,128]{1,0:T(8,128)(2,1)} %get-tuple-element.57), channel_id=1, source_target_pairs={{0,2},{1,3},{2,0},{3,1},{4,6},{5,7},{6,4},{7,5},{8,10},{9,11},{10,... | collective-permute-start | bytes 196616 | tf_op jit(solution)/shard_map/ppermute | solution.py:94
  76.7 2.0 %collective-permute-start.19 = (bf16[128,512]{1,0:T(8,128)(2,1)S(1)}, bf16[128,512]{1,0:T(8,128)(2,1)S(1)}, u32[]{:S(2)}, u32[]{:S(2)}) collective-permute-start(bf16[128,512]{1,0:T(8,128)(2,1)S(1)} %slice.51), channel_id=1, source_target_pairs={{0,2},{1,3},{2,0},{3,1},{4,6},{5,7},{6,4},{7,5},{8,10},{9,11},{10,... | collective-permute-start | bytes 393224 | tf_op jit(solution)/shard_map/ppermute | solution.py:94
  78.7 2.4 %collective-permute-done.13 = bf16[128,1024]{1,0:T(8,128)(2,1)S(1)} collective-permute-done((bf16[128,1024]{1,0:T(8,128)(2,1)S(1)}, bf16[128,1024]{1,0:T(8,128)(2,1)S(1)}, u32[]{:S(2)}, u32[]{:S(2)}) %collective-permute-start.13) | collective-permute-done | bytes 262176 | tf_op jit(solution)/shard_map/ppermute | solution.py:94
  82.5 2.3 %collective-permute-done.17.from_xz = bf16[256,128]{1,0:T(8,128)(2,1)S(1)} collective-permute-done((bf16[256,128]{1,0:T(8,128)(2,1)}, bf16[256,128]{1,0:T(8,128)(2,1)S(1)}, u32[]{:S(2)}, u32[]{:S(2)}) %collective-permute-start.17) | collective-permute-done | bytes 65568 | tf_op jit(solution)/shard_map/ppermute | solution.py:94
  85.4 2.7 %backward.1 = (bf16[512,128]{1,0:T(8,128)(2,1)}, bf16[512,128]{1,0:T(8,128)(2,1)}, bf16[512,128]{1,0:T(8,128)(2,1)}) custom-call(bf16[512,128]{1,0:T(8,128)(2,1)} %q.1, bf16[512,128]{1,0:T(8,128)(2,1)} %k.1, bf16[512,128]{1,0:T(8,128)(2,1)} %v.1, f32[2,256,256]{2,1,0:T(8,128)} %get-tuple-element.51.probs, f32[256,128]{1,0:T(8,128)} %get-tuple-element.55.own, ...), custom_call_target="tpu_custom_call" | custom-call | flops 20000000000 | bytes 1048576 | tf_op jit(solution)/shard_map/backward/pallas_call | solution.py:186
  (69 shorter events, 13.2 us)
Async XLA Ops:
  2.7 12.3 %collective-permute-start = (bf16[64,3072]{1,0:T(8,128)(2,1)}, bf16[64,3072]{1,0:T(8,128)(2,1)S(1)}, u32[]{:S(2)}, u32[]{:S(2)}) collective-permute-start(bf16[64,3072]{1,0:T(8,128)(2,1)} %get-tuple-element.34), channel_id=1, source_target_pairs={{0,16},{1,17},{2,18},{3,19},{4,20},{5,21},{6,22},{7,23},{8,24},{9,... | collective-permute-start | bytes 1179656 | tf_op jit(solution)/shard_map/ppermute | solution.py:94
  5.7 26.4 %collective-permute-start.2 = (bf16[64,3072]{1,0:T(8,128)(2,1)}, bf16[64,3072]{1,0:T(8,128)(2,1)S(1)}, u32[]{:S(2)}, u32[]{:S(2)}) collective-permute-start(bf16[64,3072]{1,0:T(8,128)(2,1)} %get-tuple-element.36.refs_0_), channel_id=1, source_target_pairs={{0,4},{1,5},{2,6},{3,7},{4,0},{5,1},{6,2},{7,3},{8,12},{9,13},{10,... | collective-permute-start | bytes 1179656 | tf_op jit(solution)/shard_map/ppermute | solution.py:94
  8.3 11.3 %collective-permute-start.1 = (bf16[64,3072]{1,0:T(8,128)(2,1)}, bf16[64,3072]{1,0:T(8,128)(2,1)S(1)}, u32[]{:S(2)}, u32[]{:S(2)}) collective-permute-start(bf16[64,3072]{1,0:T(8,128)(2,1)} %get-tuple-element.36.refs_0_), channel_id=1, source_target_pairs={{0,1},{1,0},{2,3},{3,2},{4,5},{5,4},{6,7},{7,6},{8,9},{9,8},{10,11... | collective-permute-start | bytes 1179656 | tf_op jit(solution)/shard_map/ppermute | solution.py:94
  9.8 18.0 %collective-permute-start.7 = (bf16[128,1536]{1,0:T(8,128)(2,1)S(1)}, bf16[128,1536]{1,0:T(8,128)(2,1)S(1)}, u32[]{:S(2)}, u32[]{:S(2)}) collective-permute-start(bf16[128,1536]{1,0:T(8,128)(2,1)S(1)} %copy-done.2), channel_id=1, source_target_pairs={{0,2},{1,3},{2,0},{3,1},{4,6},{5,7},{6,4},{7,5},{8,10},{9,11},{10,... | collective-permute-start | bytes 1179656 | tf_op jit(solution)/shard_map/ppermute | solution.py:94
  15.0 18.6 %copy-start.1 = (bf16[64,3072]{1,0:T(8,128)(2,1)}, bf16[64,3072]{1,0:T(8,128)(2,1)S(1)}, u32[]{:S(2)}) copy-start(bf16[64,3072]{1,0:T(8,128)(2,1)S(1)} %collective-permute-done.refs_4_) | copy-start | bytes 1179652
  17.7 28.5 %collective-permute-start.9 = (bf16[256,128]{1,0:T(8,128)(2,1)}, bf16[256,128]{1,0:T(8,128)(2,1)S(1)}, u32[]{:S(2)}, u32[]{:S(2)}) collective-permute-start(bf16[256,128]{1,0:T(8,128)(2,1)} %get-tuple-element.44), channel_id=1, source_target_pairs={{0,2},{1,3},{2,0},{3,1},{4,6},{5,7},{6,4},{7,5},{8,10},{9,11},{10,... | collective-permute-start | bytes 196616 | tf_op jit(solution)/shard_map/ppermute | solution.py:94
  19.6 9.8 %collective-permute-start.4 = (bf16[64,3072]{1,0:T(8,128)(2,1)S(1)}, bf16[64,3072]{1,0:T(8,128)(2,1)}, u32[]{:S(2)}, u32[]{:S(2)}) collective-permute-start(bf16[64,3072]{1,0:T(8,128)(2,1)S(1)} %collective-permute-done.refs_4_), channel_id=1, source_target_pairs={{0,1},{1,0},{2,3},{3,2},{4,5},{5,4},{6,7},{7,6},{8,9},{9,8},{10,11... | collective-permute-start | bytes 1179656 | tf_op jit(solution)/shard_map/ppermute | solution.py:94
  27.9 26.9 %copy-start = (bf16[256,1536]{1,0:T(8,128)(2,1)}, bf16[256,1536]{1,0:T(8,128)(2,1)S(1)}, u32[]{:S(2)}) copy-start(bf16[256,1536]{1,0:T(8,128)(2,1)S(1)} %pad_maximum_fusion.refs_8_) | copy-start | bytes 2359300
  27.9 18.2 %copy-start.3 = (bf16[256,128]{1,0:T(8,128)(2,1)S(1)}, bf16[256,128]{1,0:T(8,128)(2,1)}, u32[]{:S(2)}) copy-start(bf16[256,128]{1,0:T(8,128)(2,1)} %get-tuple-element.43) | copy-start | bytes 196612
  29.4 25.4 %collective-permute-start.8 = (bf16[256,1536]{1,0:T(8,128)(2,1)S(1)}, bf16[256,1536]{1,0:T(8,128)(2,1)S(1)}, u32[]{:S(2)}, u32[]{:S(2)}) collective-permute-start(bf16[256,1536]{1,0:T(8,128)(2,1)S(1)} %pad_maximum_fusion.refs_8_), channel_id=1, source_target_pairs={{0,8},{1,9},{2,10},{3,11},{4,12},{5,13},{6,14},{7,15},{8,0},{9,1},... | collective-permute-start | bytes 2359304 | tf_op jit(solution)/shard_map/ppermute | solution.py:94
  29.4 15.2 %collective-permute-start.5 = (bf16[64,2048]{1,0:T(8,128)(2,1)S(1)}, bf16[64,2048]{1,0:T(8,128)(2,1)S(1)}, u32[]{:S(2)}, u32[]{:S(2)}) collective-permute-start(bf16[64,2048]{1,0:T(8,128)(2,1)S(1)} %pad_maximum_fusion.2), channel_id=1, source_target_pairs={{0,4},{1,5},{2,6},{3,7},{4,0},{5,1},{6,2},{7,3},{8,12},{9,13},{10,... | collective-permute-start | bytes 786440 | tf_op jit(solution)/shard_map/ppermute | solution.py:94
  32.1 22.7 %copy-start.6 = (bf16[64,3072]{1,0:T(8,128)(2,1)}, bf16[64,3072]{1,0:T(8,128)(2,1)S(1)}, u32[]{:S(2)}) copy-start(bf16[64,3072]{1,0:T(8,128)(2,1)S(1)} %collective-permute-done.2.refs_2_) | copy-start | bytes 1179652
  32.1 22.6 %collective-permute-start.3 = (bf16[64,3072]{1,0:T(8,128)(2,1)S(1)}, bf16[64,3072]{1,0:T(8,128)(2,1)S(1)}, u32[]{:S(2)}, u32[]{:S(2)}) collective-permute-start(bf16[64,3072]{1,0:T(8,128)(2,1)S(1)} %collective-permute-done.2.refs_2_), channel_id=1, source_target_pairs={{0,1},{1,0},{2,3},{3,2},{4,5},{5,4},{6,7},{7,6},{8,9},{9,8},{10,11... | collective-permute-start | bytes 1179656 | tf_op jit(solution)/shard_map/ppermute | solution.py:94
  44.7 10.1 %collective-permute-start.6 = (bf16[64,2048]{1,0:T(8,128)(2,1)S(1)}, bf16[64,2048]{1,0:T(8,128)(2,1)S(1)}, u32[]{:S(2)}, u32[]{:S(2)}) collective-permute-start(bf16[64,2048]{1,0:T(8,128)(2,1)S(1)} %collective-permute-done.5.refs_6_), channel_id=1, source_target_pairs={{0,1},{1,0},{2,3},{3,2},{4,5},{5,4},{6,7},{7,6},{8,9},{9,8},{10,11... | collective-permute-start | bytes 786440 | tf_op jit(solution)/shard_map/ppermute | solution.py:94
  46.1 8.6 %collective-permute-start.10 = (bf16[64,1024]{1,0:T(8,128)(2,1)S(1)}, bf16[64,1024]{1,0:T(8,128)(2,1)S(1)}, u32[]{:S(2)}, u32[]{:S(2)}) collective-permute-start(bf16[64,1024]{1,0:T(8,128)(2,1)S(1)} %pad_maximum_fusion.3), channel_id=1, source_target_pairs={{0,4},{1,5},{2,6},{3,7},{4,0},{5,1},{6,2},{7,3},{8,12},{9,13},{10,... | collective-permute-start | bytes 393224 | tf_op jit(solution)/shard_map/ppermute | solution.py:94
  46.2 8.5 %collective-permute-start.11 = (bf16[512,128]{1,0:T(8,128)(2,1)S(1)}, bf16[512,128]{1,0:T(8,128)(2,1)S(1)}, u32[]{:S(2)}, u32[]{:S(2)}) collective-permute-start(bf16[512,128]{1,0:T(8,128)(2,1)S(1)} %constant_dynamic-update-slice_fusion.refs_10_), channel_id=1, source_target_pairs={{0,16},{1,17},{2,18},{3,19},{4,20},{5,21},{6,22},{7,23},{8,24},{9,... | collective-permute-start | bytes 393224 | tf_op jit(solution)/shard_map/ppermute | solution.py:94
  61.3 2.1 %collective-permute-start.12 = (bf16[256,1024]{1,0:T(8,128)(2,1)}, bf16[256,1024]{1,0:T(8,128)(2,1)S(1)}, u32[]{:S(2)}, u32[]{:S(2)}) collective-permute-start(bf16[256,1024]{1,0:T(8,128)(2,1)} %get-tuple-element.49), channel_id=1, source_target_pairs={{0,8},{1,9},{2,10},{3,11},{4,12},{5,13},{6,14},{7,15},{8,0},{9,1},... | collective-permute-start | bytes 1572872 | tf_op jit(solution)/shard_map/ppermute | solution.py:94
  61.3 5.9 %collective-permute-start.14 = (bf16[64,1024]{1,0:T(8,128)(2,1)S(1)}, bf16[64,1024]{1,0:T(8,128)(2,1)S(1)}, u32[]{:S(2)}, u32[]{:S(2)}) collective-permute-start(bf16[64,1024]{1,0:T(8,128)(2,1)S(1)} %collective-permute-done.10.refs_6_), channel_id=1, source_target_pairs={{0,1},{1,0},{2,3},{3,2},{4,5},{5,4},{6,7},{7,6},{8,9},{9,8},{10,11... | collective-permute-start | bytes 393224 | tf_op jit(solution)/shard_map/ppermute | solution.py:94
  71.9 3.7 %collective-permute-start.18 = (bf16[256,512]{1,0:T(8,128)(2,1)}, bf16[256,512]{1,0:T(8,128)(2,1)S(1)}, u32[]{:S(2)}, u32[]{:S(2)}) collective-permute-start(bf16[256,512]{1,0:T(8,128)(2,1)} %get-tuple-element.63), channel_id=1, source_target_pairs={{0,8},{1,9},{2,10},{3,11},{4,12},{5,13},{6,14},{7,15},{8,0},{9,1},... | collective-permute-start | bytes 786440 | tf_op jit(solution)/shard_map/ppermute | solution.py:94
  71.9 9.2 %collective-permute-start.13 = (bf16[128,1024]{1,0:T(8,128)(2,1)S(1)}, bf16[128,1024]{1,0:T(8,128)(2,1)S(1)}, u32[]{:S(2)}, u32[]{:S(2)}) collective-permute-start(bf16[128,1024]{1,0:T(8,128)(2,1)S(1)} %slice.50), channel_id=1, source_target_pairs={{0,2},{1,3},{2,0},{3,1},{4,6},{5,7},{6,4},{7,5},{8,10},{9,11},{10,... | collective-permute-start | bytes 786440 | tf_op jit(solution)/shard_map/ppermute | solution.py:94
  72.0 9.1 %collective-permute-start.15 = (bf16[256,128]{1,0:T(8,128)(2,1)}, bf16[256,128]{1,0:T(8,128)(2,1)S(1)}, u32[]{:S(2)}, u32[]{:S(2)}) collective-permute-start(bf16[256,128]{1,0:T(8,128)(2,1)} %get-tuple-element.56), channel_id=1, source_target_pairs={{0,16},{1,17},{2,18},{3,19},{4,20},{5,21},{6,22},{7,23},{8,24},{9,... | collective-permute-start | bytes 196616 | tf_op jit(solution)/shard_map/ppermute | solution.py:94
  73.5 8.9 %collective-permute-start.16 = (bf16[256,128]{1,0:T(8,128)(2,1)}, bf16[256,128]{1,0:T(8,128)(2,1)S(1)}, u32[]{:S(2)}, u32[]{:S(2)}) collective-permute-start(bf16[256,128]{1,0:T(8,128)(2,1)} %get-tuple-element.57), channel_id=1, source_target_pairs={{0,2},{1,3},{2,0},{3,1},{4,6},{5,7},{6,4},{7,5},{8,10},{9,11},{10,... | collective-permute-start | bytes 196616 | tf_op jit(solution)/shard_map/ppermute | solution.py:94
  75.5 9.3 %collective-permute-start.17 = (bf16[256,128]{1,0:T(8,128)(2,1)}, bf16[256,128]{1,0:T(8,128)(2,1)S(1)}, u32[]{:S(2)}, u32[]{:S(2)}) collective-permute-start(bf16[256,128]{1,0:T(8,128)(2,1)} %get-tuple-element.58), channel_id=1, source_target_pairs={{0,18},{1,19},{2,16},{3,17},{4,22},{5,23},{6,20},{7,21},{8,26},{9,... | collective-permute-start | bytes 196616 | tf_op jit(solution)/shard_map/ppermute | solution.py:94
  76.7 11.5 %collective-permute-start.19 = (bf16[128,512]{1,0:T(8,128)(2,1)S(1)}, bf16[128,512]{1,0:T(8,128)(2,1)S(1)}, u32[]{:S(2)}, u32[]{:S(2)}) collective-permute-start(bf16[128,512]{1,0:T(8,128)(2,1)S(1)} %slice.51), channel_id=1, source_target_pairs={{0,2},{1,3},{2,0},{3,1},{4,6},{5,7},{6,4},{7,5},{8,10},{9,11},{10,... | collective-permute-start | bytes 393224 | tf_op jit(solution)/shard_map/ppermute | solution.py:94
  (13 other events, 53.5 us)

commit v5 on v4

--- a/solution.py
+++ b/solution.py
@@ -13,7 +13,7 @@
 ANY = pl.BlockSpec(memory_space=pl.ANY)
 VMEM = pl.BlockSpec(memory_space=pltpu.VMEM)
 F32 = jnp.float32
-COST = pl.CostEstimate(flops=2 * 10**10, bytes_accessed=1 << 20, transcendentals=0)
+SMALL, LARGE = 10**9, 2 * 10**10
 BF16 = jnp.bfloat16
 
 
@@ -103,7 +103,22 @@
     return pl.multiple_of(index * unit, unit)
 
 
+def call(name, kernel, outs, ins, cost, scratch=()):
+    return pl.pallas_call(
+        kernel,
+        out_shape=[jax.ShapeDtypeStruct(shape, kind) for shape, kind in outs],
+        in_specs=[VMEM] * len(ins),
+        out_specs=[VMEM] * len(outs),
+        scratch_shapes=list(scratch),
+        cost_estimate=pl.CostEstimate(flops=cost, bytes_accessed=1 << 20, transcendentals=0),
+        compiler_params=pltpu.CompilerParams(vmem_limit_bytes=16 << 20),
+        name=name,
+    )(*(pltpu.with_memory_space_constraint(value, pltpu.VMEM) for value in ins))
+
+
 def pack_kernel(cuts, cot, *outs):
+    outs, token = outs[:-1], outs[-1]
+    token[...] = jnp.zeros_like(token)
     x = place()["x"]
     quarter = cot.shape[1] // 4
     for n, (low, high) in enumerate(cuts):
@@ -116,17 +131,11 @@
 
 
 def pack(cot, cuts):
-    shapes = []
+    outs = []
     for low, high in cuts:
-        shapes += [jax.ShapeDtypeStruct((cot.shape[0], 2 * (high - low)), cot.dtype)] * 2
-    return pl.pallas_call(
-        functools.partial(pack_kernel, cuts),
-        out_shape=shapes,
-        in_specs=[VMEM],
-        out_specs=[VMEM] * len(shapes),
-        cost_estimate=COST,
-        name="pack",
-    )(cot)
+        outs += [((cot.shape[0], 2 * (high - low)), BF16)] * 2
+    outs.append(((8, 128), F32))
+    return call("pack", functools.partial(pack_kernel, cuts), outs, [cot], SMALL)
 
 
 def dot(a, b, over):
@@ -150,19 +159,13 @@
 
 def forward(q, k, v):
     images = q.shape[0] // PATCH
-    half = jax.ShapeDtypeStruct((q.shape[0] // 2, HD), BF16)
-    return pl.pallas_call(
-        forward_kernel,
-        out_shape=[jax.ShapeDtypeStruct((images, PATCH, PATCH), F32), half, half],
-        in_specs=[VMEM] * 3,
-        out_specs=[VMEM] * 3,
-        scratch_shapes=[pltpu.VMEM((PATCH, HD), BF16)],
-        cost_estimate=COST,
-        name="forward",
-    )(q, k, v)
-
-
-def backward_kernel(q, k, v, probs, own, from_x, from_z, from_xz, gq, gk, gv, held):
+    half = ((q.shape[0] // 2, HD), BF16)
+    outs = [((images, PATCH, PATCH), F32), half, half]
+    return call("forward", forward_kernel, outs, [q, k, v], SMALL, [pltpu.VMEM((PATCH, HD), BF16)])
+
+
+def backward_kernel(at, q, k, v, probs, own, from_x, from_z, from_xz, gq, gk, gv, held):
+    del at
     z0 = place()["z0"]
     half = PATCH // 2
     mine = (own[...] + from_x[...].astype(F32)).astype(BF16)
@@ -181,24 +184,18 @@
         gq[rows] = dot(dscore, k[rows], ((0,), (0,))).astype(BF16)
 
 
-def backward(q, k, v, probs, own, from_x, from_z, from_xz):
+def backward(at, q, k, v, probs, own, from_x, from_z, from_xz):
     images = q.shape[0] // PATCH
-    return pl.pallas_call(
-        backward_kernel,
-        out_shape=[jax.ShapeDtypeStruct(q.shape, BF16)] * 3,
-        in_specs=[VMEM] * 8,
-        out_specs=[VMEM] * 3,
-        scratch_shapes=[pltpu.VMEM((images, PATCH, HD), BF16)],
-        cost_estimate=COST,
-        name="backward",
-    )(q, k, v, probs, own, from_x, from_z, from_xz)
+    ins = [at, q, k, v, probs, own, from_x, from_z, from_xz]
+    scratch = [pltpu.VMEM((images, PATCH, HD), BF16)]
+    return call("backward", backward_kernel, [(q.shape, BF16)] * 3, ins, LARGE, scratch)
 
 
 def products_kernel(low, high, first, last, *refs):
     refs = list(refs)
     blocks = [refs.pop(0) for _ in range(8)]
-    w_own, w_core = refs.pop(0), refs.pop(0)
-    att_own, att_x = refs.pop(0), refs.pop(0)
+    w_refs = [refs.pop(0) for _ in range(2)]
+    att = [refs.pop(0) for _ in range(2)]
     before = None if first else refs.pop(0)
     keep, give = refs.pop(0), refs.pop(0)
     d_refs = refs
@@ -212,8 +209,8 @@
         rows.append(pl.multiple_of(z1 * 128 + y * 64, 64))
     attended = jnp.concatenate(
         [
-            jnp.concatenate([att[pl.ds(row, 64)], att[pl.ds(256 + row, 64)]], axis=1)
-            for att in (att_own, att_x)
+            jnp.concatenate([att[g][pl.ds(row, 64)], att[g][pl.ds(256 + row, 64)]], axis=1)
+            for g in range(2)
             for row in rows
         ],
         axis=0,
@@ -222,7 +219,6 @@
     d = None if first else before[...]
     for other in (1, 0):
         c = 1 - at["c"] if other else at["c"]
-        w_ref = w_core if other else w_own
         for start in range(0, width, tile):
             cot = jnp.concatenate(
                 [
@@ -238,7 +234,7 @@
                 give[:, start : start + tile] = share.astype(BF16)
             else:
                 keep[:, start : start + tile] = share
-            part = dot(cot, w_ref[:, low + start : low + start + tile], ((1,), (1,)))
+            part = dot(cot, w_refs[other][:, low + start : low + start + tile], ((1,), (1,)))
             d = part if d is None else d + part
     if not last:
         d_refs[0][...] = d
@@ -252,25 +248,32 @@
 
 def products(low, high, blocks, w_all, att, before, last):
     width = high - low
+    outs = [((2 * HD, width), F32), ((2 * HD, width), BF16)]
+    if last:
+        outs += [((256, HD), F32)] + [((256, HD), BF16)] * 3
+    else:
+        outs += [((512, 2 * HD), F32)]
     first = before is None
-    out = [
-        jax.ShapeDtypeStruct((2 * HD, width), F32),
-        jax.ShapeDtypeStruct((2 * HD, width), BF16),
-    ]
-    if last:
-        out.append(jax.ShapeDtypeStruct((256, HD), F32))
-        out += [jax.ShapeDtypeStruct((256, HD), BF16)] * 3
-    else:
-        out.append(jax.ShapeDtypeStruct((512, 2 * HD), F32))
-    extra = [] if first else [before]
-    return pl.pallas_call(
-        functools.partial(products_kernel, low, high, first, last),
-        out_shape=out,
-        in_specs=[VMEM] * (len(blocks) + 4 + len(extra)),
-        out_specs=[VMEM] * len(out),
-        cost_estimate=COST,
-        name="products",
-    )(*blocks, *w_all, *att, *extra)
+    ins = [*blocks, *w_all, *att] + ([] if first else [before])
+    kernel = functools.partial(products_kernel, low, high, first, last)
+    return call("products", kernel, outs, ins, LARGE)
+
+
+def fence_kernel(token, out):
+    out[...] = token[...]
+
+
+def fence(token, *others):
+    token = after(token, *others)
+    return call("fence", fence_kernel, [(token.shape, token.dtype)], [token], LARGE)[0]
+
+
+def after(value, *others):
+    return lax.optimization_barrier((value, *others))[0]
+
+
+def two(a, b):
+    return jnp.concatenate([a, b])
 
 
 def cut(value, cuts):
@@ -289,38 +292,46 @@
 
 
 def on_device_4x8(queries, keys, values, w_out, cotangent):
-    m, o = pack(cotangent, ((0, 1536),))
-    za, x, ya, w_z = send(m, z1=1), send(o, x=1), send(m, y=1), send(w_out, z0=1)
+    m, o, at = pack(cotangent, ((0, 1536),))
+    za, x, ya = send(m, z1=1), send(o, x=1), send(m, y=1)
+    at = fence(at)
+    q, k, v, _ = lax.optimization_barrier((queries, keys, values, at))
+    probs, mine, others = forward(q, k, v)
+    att_z = send(others, z0=1)
     x1, x2 = cut(x, CUTS)
     zb1 = send(x1, z1=1)
-    yx = send(after(x, ya), y=1)
-    q, k, v, _ = lax.optimization_barrier((queries, keys, values, x))
-    probs, mine, others = forward(q, k, v)
-    zb2 = send(after(x2, za), z1=1)
-    sa = send(after(za, ya), y=1)
-    att_z = send(others, z0=1)
-    att = jnp.concatenate([mine, att_z])
-    att_x = send(after(att, ya), x=1)
-    w_own = after(jnp.concatenate([w_out, w_z]), yx)
+    at = fence(at, x, mine)
+    yx = send(after(x, ya, at), y=1)
+    att = two(mine, att_z)
+    att_x = send(after(att, at), x=1)
+    at = fence(at, ya, att_z)
+    w_z = send(after(w_out, at), z0=1)
+    zb2 = send(after(x2, za, at), z1=1)
+    sa = send(after(za, at), y=1)
+    at = fence(at, za, att_x)
+    w_own = after(two(w_out, w_z), at)
     w_c = send(w_own, c=1)
-    sb1 = send(after(zb1, yx), y=1)
-    sb2 = send(after(zb2, sa), y=1)
-    w_all, att = [w_own, w_c], [after(att, zb2), att_x]
+    at = fence(at, yx, w_z)
+    sb1 = send(after(zb1, at), y=1)
+    at = fence(at, zb1, w_c)
+    sb2 = send(after(zb2, at), y=1)
+    at = fence(at, zb2)
+    w_all, att = [w_own, w_c], [att, att_x]
     inputs = [[m, ya, za, sa, x, yx, zb1, sb1], [m, ya, za, sa, x, yx, zb2, sb2]]
     before, parts, pairs = None, [], []
     for n, (low, high) in enumerate(CUTS):
         last = n == len(CUTS) - 1
+        att[0] = after(att[0], at)
         keep, give, *d = products(low, high, inputs[n], w_all, att, before, last)
+        before = d[0]
         total = keep + send(give, c=1).astype(F32)
         to_pair = total[HD:].astype(BF16)
         pair = send(to_pair, z0=1)
-        before = after(d[0], to_pair) if n == len(CUTS) - 2 else d[0]
-        pairs.append(pair)
+        at = fence(at, to_pair)
         parts.append((total[:HD] + pair.astype(F32)).astype(BF16))
     own, to_x, to_z, to_xz = d
-    q = after(q, *pairs[:-1])
     grad_q, grad_k, grad_v = backward(
-        q, k, v, probs, own, send(to_x, x=1), send(to_z, z0=1), send(to_xz, x=1, z0=1)
+        at, q, k, v, probs, own, send(to_x, x=1), send(to_z, z0=1), send(to_xz, x=1, z0=1)
     )
     return grad_q, grad_k, grad_v, jnp.concatenate(parts, axis=1)
 

time: 89.3 us -> 70.7 us (0.79)
  Pallas kernels: 16.3 us -> 4.51 us
  starting transfers between devices: 25.4 us -> 20 us
  other arithmetic: 3.41 us -> 1.18 us
  waiting for transfers between devices: 39.8 us -> 41.8 us
  local copies, waits for them, and re-layouts: 3.18 us -> 2.26 us
    pallas_call x5 -> x14, Pallas kernels: 16.3 us -> 4.51 us  [call(): pl.pallas_call(kernel, out_shape=[jax.ShapeDtypeStruct(shape, kind) for s...]
    ppermute x20, starting transfers between devices: 25.4 us -> 20 us  [send(): return lax.ppermute(value, AXES, flip(**bits))]
    add x2, other arithmetic: 2.47 us -> 0.25 us  [on_device_4x8(): total = keep + send(give, c=1).astype(F32)]
    ppermute x20, waiting for transfers between devices: 39.8 us -> 41.8 us  [send(): return lax.ppermute(value, AXES, flip(**bits))]
    unnamed x35 -> x15, local copies, waits for them, and re-layouts: 3.09 us -> 2.17 us
  transfers between devices with their start and end apart: 20 -> 20, of which waited for: 10 -> 13; matrix products, arithmetic and copies ran while one was open for 3% -> 1% of each run, Pallas kernels for 6% -> 3%
where the time goes in v5:
time: 70.7 us; the launch traced here: 70.5 us
  waiting for transfers between devices  41.8 us (59%)
  starting transfers between devices  20 us (28%)
  Pallas kernels  4.51 us (6%)
  local copies, waits for them, and re-layouts  2.26 us (3%)
  other arithmetic  1.18 us (2%)
  between operations  0.81 us (1%)
    ppermute x20, waiting for transfers between devices, send(): return lax.ppermute(value, AXES, flip(**bits))  41.8 us
    ppermute x20, starting transfers between devices, send(): return lax.ppermute(value, AXES, flip(**bits))  20 us
    pallas_call x14, Pallas kernels, call(): pl.pallas_call(kernel, out_shape=[jax.ShapeDtypeStruct(shape, kind) for s...  4.51 us
    unnamed x15, local copies, waits for them, and re-layouts  2.17 us
  transfers between devices with their start and end apart: 20, of which 13 were waited for; matrix products, arithmetic and copies ran while one was open for 1% of the time, Pallas kernels for 3%

profile of v5, /device:TPU:0, one launch (start us, length us, event | category | flops | bytes accessed | tf_op | source)
XLA Modules:
  0.0 70.5 jit_solution(4660450083732778105)
XLA Ops:
  0.6 1.1 %copy-done = bf16[64,6144]{1,0:T(8,128)(2,1)S(1)} copy-done((bf16[64,6144]{1,0:T(8,128)(2,1)S(1)}, bf16[64,6144]{1,0:T(8,128)(2,1)}, u32[]{:S(2)}) %copy-start) | copy-done | bytes 786456
  1.8 3.0 %collective-permute-start.1 = (bf16[64,3072]{1,0:T(8,128)(2,1)S(1)}, bf16[64,3072]{1,0:T(8,128)(2,1)S(1)}, u32[]{:S(2)}, u32[]{:S(2)}) collective-permute-start(bf16[64,3072]{1,0:T(8,128)(2,1)S(1)} %get-tuple-element.50.refs_0_), channel_id=1, source_target_pairs={{0,1},{1,0},{2,3},{3,2},{4,5},{5,4},{6,7},{7,6},{8,9},{9,8},{10,11... | collective-permute-start | bytes 1179656 | tf_op jit(solution)/shard_map/ppermute | solution.py:94
  4.9 2.6 %collective-permute-start.3 = (bf16[64,3072]{1,0:T(8,128)(2,1)S(1)}, bf16[64,3072]{1,0:T(8,128)(2,1)S(1)}, u32[]{:S(2)}, u32[]{:S(2)}) collective-permute-start(bf16[64,3072]{1,0:T(8,128)(2,1)S(1)} %get-tuple-element.50.refs_0_), channel_id=1, source_target_pairs={{0,4},{1,5},{2,6},{3,7},{4,0},{5,1},{6,2},{7,3},{8,12},{9,13},{10,... | collective-permute-start | bytes 1179656 | tf_op jit(solution)/shard_map/ppermute | solution.py:94
  7.4 1.5 %collective-permute-start = (bf16[64,3072]{1,0:T(8,128)(2,1)S(1)}, bf16[64,3072]{1,0:T(8,128)(2,1)S(1)}, u32[]{:S(2)}, u32[]{:S(2)}) collective-permute-start(bf16[64,3072]{1,0:T(8,128)(2,1)S(1)} %get-tuple-element.44), channel_id=1, source_target_pairs={{0,16},{1,17},{2,18},{3,19},{4,20},{5,21},{6,22},{7,23},{8,24},{9,... | collective-permute-start | bytes 1179656 | tf_op jit(solution)/shard_map/ppermute | solution.py:94
  8.9 0.9 %copy-done.1 = bf16[512,128]{1,0:T(8,128)(2,1)S(1)} copy-done((bf16[512,128]{1,0:T(8,128)(2,1)S(1)}, bf16[512,128]{1,0:T(8,128)(2,1)}, u32[]{:S(2)}) %copy-start.1) | copy-done | bytes 131096
  10.0 0.9 %forward.1 = (f32[2,256,256]{2,1,0:T(8,128)S(1)}, bf16[256,128]{1,0:T(8,128)(2,1)S(1)}, bf16[256,128]{1,0:T(8,128)(2,1)S(1)}) custom-call(bf16[512,128]{1,0:T(8,128)(2,1)S(1)} %copy-done.1, bf16[512,128]{1,0:T(8,128)(2,1)S(1)} %copy-done.2, bf16[512,128]{1,0:T(8,128)(2,1)S(1)} %copy-done.4), custom_call_target="tpu_custom_call" | custom-call | flops 1000000000 | bytes 1048576 | tf_op jit(solution)/shard_map/forward/pallas_call | solution.py:107
  10.9 1.6 %collective-permute-start.2 = (bf16[256,128]{1,0:T(8,128)(2,1)S(1)}, bf16[256,128]{1,0:T(8,128)(2,1)S(1)}, u32[]{:S(2)}, u32[]{:S(2)}) collective-permute-start(bf16[256,128]{1,0:T(8,128)(2,1)S(1)} %get-tuple-element.51), channel_id=1, source_target_pairs={{0,2},{1,3},{2,0},{3,1},{4,6},{5,7},{6,4},{7,5},{8,10},{9,11},{10,... | collective-permute-start | bytes 196616 | tf_op jit(solution)/shard_map/ppermute | solution.py:94
  12.5 4.5 %collective-permute-done.2 = bf16[256,128]{1,0:T(8,128)(2,1)S(1)} collective-permute-done((bf16[256,128]{1,0:T(8,128)(2,1)S(1)}, bf16[256,128]{1,0:T(8,128)(2,1)S(1)}, u32[]{:S(2)}, u32[]{:S(2)}) %collective-permute-start.2) | collective-permute-done | bytes 65568 | tf_op jit(solution)/shard_map/ppermute | solution.py:94
  17.7 1.5 %collective-permute-start.4 = (bf16[512,128]{1,0:T(8,128)(2,1)S(1)}, bf16[512,128]{1,0:T(8,128)(2,1)S(1)}, u32[]{:S(2)}, u32[]{:S(2)}) collective-permute-start(bf16[512,128]{1,0:T(8,128)(2,1)S(1)} %constant_dynamic-update-slice_fusion.refs_10_), channel_id=1, source_target_pairs={{0,16},{1,17},{2,18},{3,19},{4,20},{5,21},{6,22},{7,23},{8,24},{9,... | collective-permute-start | bytes 393224 | tf_op jit(solution)/shard_map/ppermute | solution.py:94
  19.2 1.9 %collective-permute-start.6 = (bf16[128,1536]{1,0:T(8,128)(2,1)S(1)}, bf16[128,1536]{1,0:T(8,128)(2,1)S(1)}, u32[]{:S(2)}, u32[]{:S(2)}) collective-permute-start(bf16[128,1536]{1,0:T(8,128)(2,1)S(1)} %copy-done.6), channel_id=1, source_target_pairs={{0,2},{1,3},{2,0},{3,1},{4,6},{5,7},{6,4},{7,5},{8,10},{9,11},{10,... | collective-permute-start | bytes 1179656 | tf_op jit(solution)/shard_map/ppermute | solution.py:94
  21.9 4.1 %collective-permute-done.3.refs_2_ = bf16[64,3072]{1,0:T(8,128)(2,1)S(1)} collective-permute-done((bf16[64,3072]{1,0:T(8,128)(2,1)S(1)}, bf16[64,3072]{1,0:T(8,128)(2,1)S(1)}, u32[]{:S(2)}, u32[]{:S(2)}) %collective-permute-start.3) | collective-permute-done | bytes 393248 | tf_op jit(solution)/shard_map/ppermute | solution.py:94
  26.3 12.1 %collective-permute-done.6 = bf16[128,1536]{1,0:T(8,128)(2,1)S(1)} collective-permute-done((bf16[128,1536]{1,0:T(8,128)(2,1)S(1)}, bf16[128,1536]{1,0:T(8,128)(2,1)S(1)}, u32[]{:S(2)}, u32[]{:S(2)}) %collective-permute-start.6) | collective-permute-done | bytes 393248 | tf_op jit(solution)/shard_map/ppermute | solution.py:94
  38.5 1.7 %collective-permute-done.7.refs_6_ = bf16[64,2048]{1,0:T(8,128)(2,1)S(1)} collective-permute-done((bf16[64,2048]{1,0:T(8,128)(2,1)S(1)}, bf16[64,2048]{1,0:T(8,128)(2,1)S(1)}, u32[]{:S(2)}, u32[]{:S(2)}) %collective-permute-start.7) | collective-permute-done | bytes 262176 | tf_op jit(solution)/shard_map/ppermute | solution.py:94
  40.8 0.9 %collective-permute-done.9.refs_6_ = bf16[64,1024]{1,0:T(8,128)(2,1)S(1)} collective-permute-done((bf16[64,1024]{1,0:T(8,128)(2,1)S(1)}, bf16[64,1024]{1,0:T(8,128)(2,1)S(1)}, u32[]{:S(2)}, u32[]{:S(2)}) %collective-permute-start.9) | collective-permute-done | bytes 131104 | tf_op jit(solution)/shard_map/ppermute | solution.py:94
  41.7 5.6 %collective-permute-done.11.refs_7_ = bf16[64,2048]{1,0:T(8,128)(2,1)S(1)} collective-permute-done((bf16[64,2048]{1,0:T(8,128)(2,1)S(1)}, bf16[64,2048]{1,0:T(8,128)(2,1)S(1)}, u32[]{:S(2)}, u32[]{:S(2)}) %collective-permute-start.11) | collective-permute-done | bytes 262176 | tf_op jit(solution)/shard_map/ppermute | solution.py:94
  47.3 1.3 %products.2 = (f32[256,1024]{1,0:T(8,128)S(1)}, bf16[256,1024]{1,0:T(8,128)(2,1)S(1)}, f32[512,256]{1,0:T(8,128)S(1)}) custom-call(bf16[64,3072]{1,0:T(8,128)(2,1)S(1)} %get-tuple-element.50.refs_0_, bf16[64,3072]{1,0:T(8,128)(2,1)S(1)} %collective-permute-done.1.refs_1_, bf16[64,3072]{1,0:T(8,128)(2,1)S(1)} %collective-permute-done.3.refs_2_, ...), custom_call_target="tpu_custom_call" | custom-call | flops 20000000000 | bytes 1048576 | tf_op jit(solution)/shard_map/products/pallas_call | solution.py:107
  49.2 1.3 %collective-permute-done.12 = bf16[256,1024]{1,0:T(8,128)(2,1)S(1)} collective-permute-done((bf16[256,1024]{1,0:T(8,128)(2,1)S(1)}, bf16[256,1024]{1,0:T(8,128)(2,1)S(1)}, u32[]{:S(2)}, u32[]{:S(2)}) %collective-permute-start.12) | collective-permute-done | bytes 524320 | tf_op jit(solution)/shard_map/ppermute | solution.py:94
  50.8 3.8 %collective-permute-done.13.refs_7_ = bf16[64,1024]{1,0:T(8,128)(2,1)S(1)} collective-permute-done((bf16[64,1024]{1,0:T(8,128)(2,1)S(1)}, bf16[64,1024]{1,0:T(8,128)(2,1)S(1)}, u32[]{:S(2)}, u32[]{:S(2)}) %collective-permute-start.13) | collective-permute-done | bytes 131104 | tf_op jit(solution)/shard_map/ppermute | solution.py:94
  55.9 1.5 %collective-permute-start.15 = (bf16[256,128]{1,0:T(8,128)(2,1)S(1)}, bf16[256,128]{1,0:T(8,128)(2,1)S(1)}, u32[]{:S(2)}, u32[]{:S(2)}) collective-permute-start(bf16[256,128]{1,0:T(8,128)(2,1)S(1)} %get-tuple-element.76), channel_id=1, source_target_pairs={{0,16},{1,17},{2,18},{3,19},{4,20},{5,21},{6,22},{7,23},{8,24},{9,... | collective-permute-start | bytes 196616 | tf_op jit(solution)/shard_map/ppermute | solution.py:94
  57.4 1.2 %collective-permute-start.16 = (bf16[256,128]{1,0:T(8,128)(2,1)S(1)}, bf16[256,128]{1,0:T(8,128)(2,1)S(1)}, u32[]{:S(2)}, u32[]{:S(2)}) collective-permute-start(bf16[256,128]{1,0:T(8,128)(2,1)S(1)} %get-tuple-element.77), channel_id=1, source_target_pairs={{0,2},{1,3},{2,0},{3,1},{4,6},{5,7},{6,4},{7,5},{8,10},{9,11},{10,... | collective-permute-start | bytes 196616 | tf_op jit(solution)/shard_map/ppermute | solution.py:94
  59.5 1.6 %collective-permute-start.19 = (bf16[128,512]{1,0:T(8,128)(2,1)S(1)}, bf16[128,512]{1,0:T(8,128)(2,1)S(1)}, u32[]{:S(2)}, u32[]{:S(2)}) collective-permute-start(bf16[128,512]{1,0:T(8,128)(2,1)S(1)} %slice.51), channel_id=1, source_target_pairs={{0,2},{1,3},{2,0},{3,1},{4,6},{5,7},{6,4},{7,5},{8,10},{9,11},{10,... | collective-permute-start | bytes 393224 | tf_op jit(solution)/shard_map/ppermute | solution.py:94
  61.2 4.8 %collective-permute-done.16.from_z = bf16[256,128]{1,0:T(8,128)(2,1)S(1)} collective-permute-done((bf16[256,128]{1,0:T(8,128)(2,1)S(1)}, bf16[256,128]{1,0:T(8,128)(2,1)S(1)}, u32[]{:S(2)}, u32[]{:S(2)}) %collective-permute-start.16) | collective-permute-done | bytes 65568 | tf_op jit(solution)/shard_map/ppermute | solution.py:94
  66.0 2.0 %collective-permute-done.17.from_xz = bf16[256,128]{1,0:T(8,128)(2,1)S(1)} collective-permute-done((bf16[256,128]{1,0:T(8,128)(2,1)S(1)}, bf16[256,128]{1,0:T(8,128)(2,1)S(1)}, u32[]{:S(2)}, u32[]{:S(2)}) %collective-permute-start.17) | collective-permute-done | bytes 65568 | tf_op jit(solution)/shard_map/ppermute | solution.py:94
  68.0 1.5 %backward.1 = (bf16[512,128]{1,0:T(8,128)(2,1)}, bf16[512,128]{1,0:T(8,128)(2,1)}, bf16[512,128]{1,0:T(8,128)(2,1)}) custom-call(f32[8,128]{1,0:T(8,128)S(1)} %fence.17.at, bf16[512,128]{1,0:T(8,128)(2,1)S(1)} %copy-done.1, bf16[512,128]{1,0:T(8,128)(2,1)S(1)} %copy-done.3, bf16[512,128]{1,0:T(8,128)(2,1)S(1)} %copy-done.5, ...), custom_call_target="tpu_custom_call" | custom-call | flops 20000000000 | bytes 1048576 | tf_op jit(solution)/shard_map/backward/pallas_call | solution.py:107
  (58 shorter events, 6.8 us)
Async XLA Ops:
  0.6 1.1 %copy-start = (bf16[64,6144]{1,0:T(8,128)(2,1)S(1)}, bf16[64,6144]{1,0:T(8,128)(2,1)}, u32[]{:S(2)}) copy-start(bf16[64,6144]{1,0:T(8,128)(2,1)} %cot.1) | copy-start | bytes 2359300
  1.8 17.4 %collective-permute-start.1 = (bf16[64,3072]{1,0:T(8,128)(2,1)S(1)}, bf16[64,3072]{1,0:T(8,128)(2,1)S(1)}, u32[]{:S(2)}, u32[]{:S(2)}) collective-permute-start(bf16[64,3072]{1,0:T(8,128)(2,1)S(1)} %get-tuple-element.50.refs_0_), channel_id=1, source_target_pairs={{0,1},{1,0},{2,3},{3,2},{4,5},{5,4},{6,7},{7,6},{8,9},{9,8},{10,11... | collective-permute-start | bytes 1179656 | tf_op jit(solution)/shard_map/ppermute | solution.py:94
  4.9 21.2 %collective-permute-start.3 = (bf16[64,3072]{1,0:T(8,128)(2,1)S(1)}, bf16[64,3072]{1,0:T(8,128)(2,1)S(1)}, u32[]{:S(2)}, u32[]{:S(2)}) collective-permute-start(bf16[64,3072]{1,0:T(8,128)(2,1)S(1)} %get-tuple-element.50.refs_0_), channel_id=1, source_target_pairs={{0,4},{1,5},{2,6},{3,7},{4,0},{5,1},{6,2},{7,3},{8,12},{9,13},{10,... | collective-permute-start | bytes 1179656 | tf_op jit(solution)/shard_map/ppermute | solution.py:94
  7.4 10.3 %collective-permute-start = (bf16[64,3072]{1,0:T(8,128)(2,1)S(1)}, bf16[64,3072]{1,0:T(8,128)(2,1)S(1)}, u32[]{:S(2)}, u32[]{:S(2)}) collective-permute-start(bf16[64,3072]{1,0:T(8,128)(2,1)S(1)} %get-tuple-element.44), channel_id=1, source_target_pairs={{0,16},{1,17},{2,18},{3,19},{4,20},{5,21},{6,22},{7,23},{8,24},{9,... | collective-permute-start | bytes 1179656 | tf_op jit(solution)/shard_map/ppermute | solution.py:94
  10.9 6.1 %collective-permute-start.2 = (bf16[256,128]{1,0:T(8,128)(2,1)S(1)}, bf16[256,128]{1,0:T(8,128)(2,1)S(1)}, u32[]{:S(2)}, u32[]{:S(2)}) collective-permute-start(bf16[256,128]{1,0:T(8,128)(2,1)S(1)} %get-tuple-element.51), channel_id=1, source_target_pairs={{0,2},{1,3},{2,0},{3,1},{4,6},{5,7},{6,4},{7,5},{8,10},{9,11},{10,... | collective-permute-start | bytes 196616 | tf_op jit(solution)/shard_map/ppermute | solution.py:94
  17.7 1.5 %copy-start.6 = (bf16[128,1536]{1,0:T(8,128)(2,1)S(1)}, bf16[128,1536]{1,0:T(8,128)(2,1)}, u32[]{:S(2)}) copy-start(bf16[128,1536]{1,0:T(8,128)(2,1)} %param.8) | copy-start | bytes 1179652
  17.7 8.3 %collective-permute-start.4 = (bf16[512,128]{1,0:T(8,128)(2,1)S(1)}, bf16[512,128]{1,0:T(8,128)(2,1)S(1)}, u32[]{:S(2)}, u32[]{:S(2)}) collective-permute-start(bf16[512,128]{1,0:T(8,128)(2,1)S(1)} %constant_dynamic-update-slice_fusion.refs_10_), channel_id=1, source_target_pairs={{0,16},{1,17},{2,18},{3,19},{4,20},{5,21},{6,22},{7,23},{8,24},{9,... | collective-permute-start | bytes 393224 | tf_op jit(solution)/shard_map/ppermute | solution.py:94
  19.2 19.1 %collective-permute-start.6 = (bf16[128,1536]{1,0:T(8,128)(2,1)S(1)}, bf16[128,1536]{1,0:T(8,128)(2,1)S(1)}, u32[]{:S(2)}, u32[]{:S(2)}) collective-permute-start(bf16[128,1536]{1,0:T(8,128)(2,1)S(1)} %copy-done.6), channel_id=1, source_target_pairs={{0,2},{1,3},{2,0},{3,1},{4,6},{5,7},{6,4},{7,5},{8,10},{9,11},{10,... | collective-permute-start | bytes 1179656 | tf_op jit(solution)/shard_map/ppermute | solution.py:94
  21.1 17.4 %collective-permute-start.5 = (bf16[64,3072]{1,0:T(8,128)(2,1)S(1)}, bf16[64,3072]{1,0:T(8,128)(2,1)S(1)}, u32[]{:S(2)}, u32[]{:S(2)}) collective-permute-start(bf16[64,3072]{1,0:T(8,128)(2,1)S(1)} %collective-permute-done.refs_4_), channel_id=1, source_target_pairs={{0,1},{1,0},{2,3},{3,2},{4,5},{5,4},{6,7},{7,6},{8,9},{9,8},{10,11... | collective-permute-start | bytes 1179656 | tf_op jit(solution)/shard_map/ppermute | solution.py:94
  21.7 18.6 %collective-permute-start.7 = (bf16[64,2048]{1,0:T(8,128)(2,1)S(1)}, bf16[64,2048]{1,0:T(8,128)(2,1)S(1)}, u32[]{:S(2)}, u32[]{:S(2)}) collective-permute-start(bf16[64,2048]{1,0:T(8,128)(2,1)S(1)} %pad_maximum_fusion.2), channel_id=1, source_target_pairs={{0,4},{1,5},{2,6},{3,7},{4,0},{5,1},{6,2},{7,3},{8,12},{9,13},{10,... | collective-permute-start | bytes 786440 | tf_op jit(solution)/shard_map/ppermute | solution.py:94
  26.0 15.6 %collective-permute-start.9 = (bf16[64,1024]{1,0:T(8,128)(2,1)S(1)}, bf16[64,1024]{1,0:T(8,128)(2,1)S(1)}, u32[]{:S(2)}, u32[]{:S(2)}) collective-permute-start(bf16[64,1024]{1,0:T(8,128)(2,1)S(1)} %pad_maximum_fusion.3), channel_id=1, source_target_pairs={{0,4},{1,5},{2,6},{3,7},{4,0},{5,1},{6,2},{7,3},{8,12},{9,13},{10,... | collective-permute-start | bytes 393224 | tf_op jit(solution)/shard_map/ppermute | solution.py:94
  26.0 15.6 %collective-permute-start.10 = (bf16[64,3072]{1,0:T(8,128)(2,1)S(1)}, bf16[64,3072]{1,0:T(8,128)(2,1)S(1)}, u32[]{:S(2)}, u32[]{:S(2)}) collective-permute-start(bf16[64,3072]{1,0:T(8,128)(2,1)S(1)} %collective-permute-done.3.refs_2_), channel_id=1, source_target_pairs={{0,1},{1,0},{2,3},{3,2},{4,5},{5,4},{6,7},{7,6},{8,9},{9,8},{10,11... | collective-permute-start | bytes 1179656 | tf_op jit(solution)/shard_map/ppermute | solution.py:94
  38.4 2.4 %collective-permute-start.8 = (bf16[256,1536]{1,0:T(8,128)(2,1)S(1)}, bf16[256,1536]{1,0:T(8,128)(2,1)S(1)}, u32[]{:S(2)}, u32[]{:S(2)}) collective-permute-start(bf16[256,1536]{1,0:T(8,128)(2,1)S(1)} %pad_maximum_fusion.refs_8_), channel_id=1, source_target_pairs={{0,8},{1,9},{2,10},{3,11},{4,12},{5,13},{6,14},{7,15},{8,0},{9,1},... | collective-permute-start | bytes 2359304 | tf_op jit(solution)/shard_map/ppermute | solution.py:94
  40.2 7.0 %collective-permute-start.11 = (bf16[64,2048]{1,0:T(8,128)(2,1)S(1)}, bf16[64,2048]{1,0:T(8,128)(2,1)S(1)}, u32[]{:S(2)}, u32[]{:S(2)}) collective-permute-start(bf16[64,2048]{1,0:T(8,128)(2,1)S(1)} %collective-permute-done.7.refs_6_), channel_id=1, source_target_pairs={{0,1},{1,0},{2,3},{3,2},{4,5},{5,4},{6,7},{7,6},{8,9},{9,8},{10,11... | collective-permute-start | bytes 786440 | tf_op jit(solution)/shard_map/ppermute | solution.py:94
  48.6 2.0 %collective-permute-start.12 = (bf16[256,1024]{1,0:T(8,128)(2,1)S(1)}, bf16[256,1024]{1,0:T(8,128)(2,1)S(1)}, u32[]{:S(2)}, u32[]{:S(2)}) collective-permute-start(bf16[256,1024]{1,0:T(8,128)(2,1)S(1)} %get-tuple-element.66), channel_id=1, source_target_pairs={{0,8},{1,9},{2,10},{3,11},{4,12},{5,13},{6,14},{7,15},{8,0},{9,1},... | collective-permute-start | bytes 1572872 | tf_op jit(solution)/shard_map/ppermute | solution.py:94
  48.7 5.9 %collective-permute-start.13 = (bf16[64,1024]{1,0:T(8,128)(2,1)S(1)}, bf16[64,1024]{1,0:T(8,128)(2,1)S(1)}, u32[]{:S(2)}, u32[]{:S(2)}) collective-permute-start(bf16[64,1024]{1,0:T(8,128)(2,1)S(1)} %collective-permute-done.9.refs_6_), channel_id=1, source_target_pairs={{0,1},{1,0},{2,3},{3,2},{4,5},{5,4},{6,7},{7,6},{8,9},{9,8},{10,11... | collective-permute-start | bytes 393224 | tf_op jit(solution)/shard_map/ppermute | solution.py:94
  55.3 4.1 %collective-permute-start.14 = (bf16[256,512]{1,0:T(8,128)(2,1)S(1)}, bf16[256,512]{1,0:T(8,128)(2,1)S(1)}, u32[]{:S(2)}, u32[]{:S(2)}) collective-permute-start(bf16[256,512]{1,0:T(8,128)(2,1)S(1)} %get-tuple-element.72), channel_id=1, source_target_pairs={{0,8},{1,9},{2,10},{3,11},{4,12},{5,13},{6,14},{7,15},{8,0},{9,1},... | collective-permute-start | bytes 786440 | tf_op jit(solution)/shard_map/ppermute | solution.py:94
  55.4 14.1 %collective-permute-start.18 = (bf16[128,1024]{1,0:T(8,128)(2,1)S(1)}, bf16[128,1024]{1,0:T(8,128)(2,1)S(1)}, u32[]{:S(2)}, u32[]{:S(2)}) collective-permute-start(bf16[128,1024]{1,0:T(8,128)(2,1)S(1)} %slice.50), channel_id=1, source_target_pairs={{0,2},{1,3},{2,0},{3,1},{4,6},{5,7},{6,4},{7,5},{8,10},{9,11},{10,... | collective-permute-start | bytes 786440 | tf_op jit(solution)/shard_map/ppermute | solution.py:94
  55.9 5.3 %collective-permute-start.15 = (bf16[256,128]{1,0:T(8,128)(2,1)S(1)}, bf16[256,128]{1,0:T(8,128)(2,1)S(1)}, u32[]{:S(2)}, u32[]{:S(2)}) collective-permute-start(bf16[256,128]{1,0:T(8,128)(2,1)S(1)} %get-tuple-element.76), channel_id=1, source_target_pairs={{0,16},{1,17},{2,18},{3,19},{4,20},{5,21},{6,22},{7,23},{8,24},{9,... | collective-permute-start | bytes 196616 | tf_op jit(solution)/shard_map/ppermute | solution.py:94
  57.4 8.6 %collective-permute-start.16 = (bf16[256,128]{1,0:T(8,128)(2,1)S(1)}, bf16[256,128]{1,0:T(8,128)(2,1)S(1)}, u32[]{:S(2)}, u32[]{:S(2)}) collective-permute-start(bf16[256,128]{1,0:T(8,128)(2,1)S(1)} %get-tuple-element.77), channel_id=1, source_target_pairs={{0,2},{1,3},{2,0},{3,1},{4,6},{5,7},{6,4},{7,5},{8,10},{9,11},{10,... | collective-permute-start | bytes 196616 | tf_op jit(solution)/shard_map/ppermute | solution.py:94
  58.6 9.3 %collective-permute-start.17 = (bf16[256,128]{1,0:T(8,128)(2,1)S(1)}, bf16[256,128]{1,0:T(8,128)(2,1)S(1)}, u32[]{:S(2)}, u32[]{:S(2)}) collective-permute-start(bf16[256,128]{1,0:T(8,128)(2,1)S(1)} %get-tuple-element.78), channel_id=1, source_target_pairs={{0,18},{1,19},{2,16},{3,17},{4,22},{5,23},{6,20},{7,21},{8,26},{9,... | collective-permute-start | bytes 196616 | tf_op jit(solution)/shard_map/ppermute | solution.py:94
  59.5 8.4 %copy-start.3 = (bf16[512,128]{1,0:T(8,128)(2,1)S(1)}, bf16[512,128]{1,0:T(8,128)(2,1)}, u32[]{:S(2)}) copy-start(bf16[512,128]{1,0:T(8,128)(2,1)} %k.1) | copy-start | bytes 393220
  59.5 8.4 %copy-start.5 = (bf16[512,128]{1,0:T(8,128)(2,1)S(1)}, bf16[512,128]{1,0:T(8,128)(2,1)}, u32[]{:S(2)}) copy-start(bf16[512,128]{1,0:T(8,128)(2,1)} %v.1) | copy-start | bytes 393220
  59.5 10.2 %collective-permute-start.19 = (bf16[128,512]{1,0:T(8,128)(2,1)S(1)}, bf16[128,512]{1,0:T(8,128)(2,1)S(1)}, u32[]{:S(2)}, u32[]{:S(2)}) collective-permute-start(bf16[128,512]{1,0:T(8,128)(2,1)S(1)} %slice.51), channel_id=1, source_target_pairs={{0,2},{1,3},{2,0},{3,1},{4,6},{5,7},{6,4},{7,5},{8,10},{9,11},{10,... | collective-permute-start | bytes 393224 | tf_op jit(solution)/shard_map/ppermute | solution.py:94
  (3 other events, 2.9 us)

commit v6 on v5

--- a/solution.py
+++ b/solution.py
@@ -13,7 +13,7 @@
 ANY = pl.BlockSpec(memory_space=pl.ANY)
 VMEM = pl.BlockSpec(memory_space=pltpu.VMEM)
 F32 = jnp.float32
-SMALL, LARGE = 10**9, 2 * 10**10
+SMALL, LARGE = 1, 10000000000
 BF16 = jnp.bfloat16
 
 
@@ -191,9 +191,10 @@
     return call("backward", backward_kernel, [(q.shape, BF16)] * 3, ins, LARGE, scratch)
 
 
-def products_kernel(low, high, first, last, *refs):
-    refs = list(refs)
-    blocks = [refs.pop(0) for _ in range(8)]
+def products_kernel(low, high, first, last, places, *refs):
+    refs = list(refs[1:])
+    arrays = [refs.pop(0) for _ in range(1 + max(array for array, _ in places))]
+    blocks = [(arrays[array], row) for array, row in places]
     w_refs = [refs.pop(0) for _ in range(2)]
     att = [refs.pop(0) for _ in range(2)]
     before = None if first else refs.pop(0)
@@ -201,7 +202,7 @@
     d_refs = refs
     at = place()
     width = high - low
-    tile = min(width, 512)
+    tile = next(size for size in (512, 384, 256, 128) if width % size == 0)
     rows = []
     for n in range(4):
         z1 = 1 - at["z1"] if n // 2 else at["z1"]
@@ -222,8 +223,8 @@
         for start in range(0, width, tile):
             cot = jnp.concatenate(
                 [
-                    block[:, pl.ds(pl.multiple_of(c * half + start + skip, 128), tile)]
-                    for block in blocks
+                    block[row : row + 64, pl.ds(pl.multiple_of(c * half + start + skip, 128), tile)]
+                    for block, row in blocks
                     for half in [block.shape[1] // 2]
                     for skip in [low if half > width else 0]
                 ],
@@ -246,16 +247,22 @@
                 d_refs[2 + g][pl.ds(row, 64)] = share[:, HD:].astype(BF16)
 
 
-def products(low, high, blocks, w_all, att, before, last):
+def products(limits, blocks, w_all, att, token, before, last):
+    low, high = limits
     width = high - low
     outs = [((2 * HD, width), F32), ((2 * HD, width), BF16)]
     if last:
         outs += [((256, HD), F32)] + [((256, HD), BF16)] * 3
     else:
         outs += [((512, 2 * HD), F32)]
-    first = before is None
-    ins = [*blocks, *w_all, *att] + ([] if first else [before])
-    kernel = functools.partial(products_kernel, low, high, first, last)
+    arrays, places = [], []
+    for array, row in blocks:
+        known = [n for n, other in enumerate(arrays) if other is array]
+        places.append((known[0] if known else len(arrays), row))
+        if not known:
+            arrays.append(array)
+    ins = [token, *arrays, *w_all, *att] + ([] if before is None else [before])
+    kernel = functools.partial(products_kernel, low, high, before is None, last, places)
     return call("products", kernel, outs, ins, LARGE)
 
 
@@ -263,9 +270,9 @@
     out[...] = token[...]
 
 
-def fence(token, *others):
+def fence(token, *others, cost):
     token = after(token, *others)
-    return call("fence", fence_kernel, [(token.shape, token.dtype)], [token], LARGE)[0]
+    return call("fence", fence_kernel, [(token.shape, token.dtype)], [token], cost)[0]
 
 
 def after(value, *others):
@@ -288,52 +295,64 @@
     return lax.optimization_barrier((value, *others))[0]
 
 
-CUTS = ((0, 1024), (1024, 1536))
+CUTS = ((0, 896), (896, 1536))
 
 
 def on_device_4x8(queries, keys, values, w_out, cotangent):
-    m, o, at = pack(cotangent, ((0, 1536),))
-    za, x, ya = send(m, z1=1), send(o, x=1), send(m, y=1)
-    at = fence(at)
-    q, k, v, _ = lax.optimization_barrier((queries, keys, values, at))
-    probs, mine, others = forward(q, k, v)
-    att_z = send(others, z0=1)
+    m, o, m1, _, m2, _, token = pack(cotangent, ((0, CUTS[-1][1]), *CUTS))
+    at0 = fence(token, cost=1)
+    at1 = fence(at0, cost=10**10)
+    x = send(o, x=1)
+    at2 = fence(at1, x, cost=10**10)
+    za = send(m, z1=1)
+    probs, mine, others = forward(queries, keys, values)
+    ya = send(m, y=1)
+    att_z = send(after(others, at0, ya), z0=1)
+    att = two(mine, att_z)
+    att_x = send(att, x=1)
+    at3 = fence(at2, za, att_x, cost=10**10)
+    at4 = fence(at3, cost=10**10)
     x1, x2 = cut(x, CUTS)
+    zb2 = send(after(x2, at3), z1=1)
+    at5 = fence(at4, zb2, cost=10**10)
+    att_all = [att, att_x]
+    own_x = att_all[0]
+    sa = send(za, y=1)
+    yx = send(after(x, at2), y=1)
     zb1 = send(x1, z1=1)
-    at = fence(at, x, mine)
-    yx = send(after(x, ya, at), y=1)
-    att = two(mine, att_z)
-    att_x = send(after(att, at), x=1)
-    at = fence(at, ya, att_z)
-    w_z = send(after(w_out, at), z0=1)
-    zb2 = send(after(x2, za, at), z1=1)
-    sa = send(after(za, at), y=1)
-    at = fence(at, za, att_x)
-    w_own = after(two(w_out, w_z), at)
-    w_c = send(w_own, c=1)
-    at = fence(at, yx, w_z)
-    sb1 = send(after(zb1, at), y=1)
-    at = fence(at, zb1, w_c)
-    sb2 = send(after(zb2, at), y=1)
-    at = fence(at, zb2)
-    w_all, att = [w_own, w_c], [att, att_x]
-    inputs = [[m, ya, za, sa, x, yx, zb1, sb1], [m, ya, za, sa, x, yx, zb2, sb2]]
-    before, parts, pairs = None, [], []
-    for n, (low, high) in enumerate(CUTS):
-        last = n == len(CUTS) - 1
-        att[0] = after(att[0], at)
-        keep, give, *d = products(low, high, inputs[n], w_all, att, before, last)
-        before = d[0]
-        total = keep + send(give, c=1).astype(F32)
-        to_pair = total[HD:].astype(BF16)
-        pair = send(to_pair, z0=1)
-        at = fence(at, to_pair)
-        parts.append((total[:HD] + pair.astype(F32)).astype(BF16))
-    own, to_x, to_z, to_xz = d
-    grad_q, grad_k, grad_v = backward(
-        at, q, k, v, probs, own, send(to_x, x=1), send(to_z, z0=1), send(to_xz, x=1, z0=1)
-    )
-    return grad_q, grad_k, grad_v, jnp.concatenate(parts, axis=1)
+    sb1 = send(zb1, y=1)
+    w_z = send(after(w_out, x), z0=1)
+    w_own = two(w_out, w_z)
+    w_c = send(two(w_out, w_z), c=1)
+    w_all = [w_own, w_c]
+    blocks = [(m, 0), (ya, 0), (za, 0), (sa, 0), (x, 0), (yx, 0), (zb1, 0), (sb1, 0)]
+    keep1, give1, d = products(
+        CUTS[0], blocks, w_all, [own_x, att_all[1]], token, None, False
+    )
+    got1 = send(give1, c=1)
+    total1 = keep1 + got1.astype(F32)
+    to_pair1 = total1[HD:].astype(BF16)
+    own_x = after(att_all[0], at4, at2)
+    sb2 = send(after(zb2, at4), y=1)
+    blocks = [(m, 0), (ya, 0), (za, 0), (sa, 0), (x, 0), (yx, 0), (zb2, 0), (sb2, 0)]
+    keep2, give2, own, to_x, to_z, to_xz = products(
+        CUTS[1], blocks, w_all, [own_x, att_all[1]], token, d, True
+    )
+    got2 = send(give2, c=1)
+    pair1 = send(after(to_pair1, got2), z0=1)
+    queries = after(queries, pair1, at1)
+    from_x = send(after(to_x, at0), x=1)
+    from_z = send(to_z, z0=1)
+    from_xz = send(to_xz, x=1, z0=1)
+    grads = backward(at5, queries, keys, values, probs, own, from_x, from_z, from_xz)
+    rest1 = total1[:HD]
+    part1 = (rest1 + pair1.astype(F32)).astype(BF16)
+    total2 = keep2 + got2.astype(F32)
+    rest2 = total2[:HD]
+    to_pair2 = total2[HD:].astype(BF16)
+    pair2 = send(to_pair2, z0=1)
+    part2 = (rest2 + pair2.astype(F32)).astype(BF16)
+    return *grads, jnp.concatenate([part1, part2], axis=1)
 
 
 def solution(mesh):

time: 70.7 us -> 69.7 us (0.986)
  waiting for transfers between devices: 41.8 us -> 38.2 us
  Pallas kernels: 4.51 us -> 7.11 us
    ppermute x20, waiting for transfers between devices: 41.8 us -> 38.2 us  [send(): return lax.ppermute(value, AXES, flip(**bits))]
    pallas_call x14 -> x11, Pallas kernels: 4.51 us -> 7.11 us  [call(): pl.pallas_call(kernel, out_shape=[jax.ShapeDtypeStruct(shape, kind) for s...]
    unnamed x15 -> x12, local copies, waits for them, and re-layouts: 2.17 us -> 2.25 us
  transfers between devices with their start and end apart: 20 -> 20, of which waited for: 13 -> 8; matrix products, arithmetic and copies ran while one was open for 1% -> 2% of each run, Pallas kernels for 3% -> 7%
where the time goes in v6:
time: 69.7 us; the launch traced here: 69.5 us
  waiting for transfers between devices  38.2 us (55%)
  starting transfers between devices  20 us (29%)
  Pallas kernels  7.11 us (10%)
  local copies, waits for them, and re-layouts  2.38 us (3%)
  other arithmetic  1.03 us (1%)
  between operations  0.81 us (1%)
    ppermute x20, waiting for transfers between devices, send(): return lax.ppermute(value, AXES, flip(**bits))  38.2 us
    ppermute x20, starting transfers between devices, send(): return lax.ppermute(value, AXES, flip(**bits))  20 us
    pallas_call x11, Pallas kernels, call(): pl.pallas_call(kernel, out_shape=[jax.ShapeDtypeStruct(shape, kind) for s...  7.11 us
    unnamed x12, local copies, waits for them, and re-layouts  2.25 us
  transfers between devices with their start and end apart: 20, of which 8 were waited for; matrix products, arithmetic and copies ran while one was open for 2% of the time, Pallas kernels for 7%

profile of v6, /device:TPU:0, one launch (start us, length us, event | category | flops | bytes accessed | tf_op | source)
XLA Modules:
  0.0 69.5 jit_solution(12336128893847156465)
XLA Ops:
  0.6 1.1 %copy-done = bf16[64,6144]{1,0:T(8,128)(2,1)S(1)} copy-done((bf16[64,6144]{1,0:T(8,128)(2,1)S(1)}, bf16[64,6144]{1,0:T(8,128)(2,1)}, u32[]{:S(2)}) %copy-start) | copy-done | bytes 786456
  1.8 0.9 %pack.1 = (bf16[64,3072]{1,0:T(8,128)(2,1)S(1)}, bf16[64,3072]{1,0:T(8,128)(2,1)S(1)}, bf16[64,1792]{1,0:T(8,128)(2,1)}, bf16[64,1792]{1,0:T(8,128)(2,1)}, bf16[...) custom-call(bf16[64,6144]{1,0:T(8,128)(2,1)S(1)} %copy-done), custom_call_target="tpu_custom_call" | custom-call | flops 1 | bytes 1048576 | tf_op jit(solution)/shard_map/pack/pallas_call | solution.py:107
  2.7 4.0 %collective-permute-start.1 = (bf16[64,3072]{1,0:T(8,128)(2,1)S(1)}, bf16[64,3072]{1,0:T(8,128)(2,1)S(1)}, u32[]{:S(2)}, u32[]{:S(2)}) collective-permute-start(bf16[64,3072]{1,0:T(8,128)(2,1)S(1)} %get-tuple-element.37.refs_1_), channel_id=1, source_target_pairs={{0,4},{1,5},{2,6},{3,7},{4,0},{5,1},{6,2},{7,3},{8,12},{9,13},{10,... | collective-permute-start | bytes 1179656 | tf_op jit(solution)/shard_map/ppermute | solution.py:94
  6.7 1.5 %collective-permute-start.2 = (bf16[64,3072]{1,0:T(8,128)(2,1)S(1)}, bf16[64,3072]{1,0:T(8,128)(2,1)S(1)}, u32[]{:S(2)}, u32[]{:S(2)}) collective-permute-start(bf16[64,3072]{1,0:T(8,128)(2,1)S(1)} %get-tuple-element.37.refs_1_), channel_id=1, source_target_pairs={{0,1},{1,0},{2,3},{3,2},{4,5},{5,4},{6,7},{7,6},{8,9},{9,8},{10,11... | collective-permute-start | bytes 1179656 | tf_op jit(solution)/shard_map/ppermute | solution.py:94
  8.3 1.5 %collective-permute-start = (bf16[64,3072]{1,0:T(8,128)(2,1)S(1)}, bf16[64,3072]{1,0:T(8,128)(2,1)S(1)}, u32[]{:S(2)}, u32[]{:S(2)}) collective-permute-start(bf16[64,3072]{1,0:T(8,128)(2,1)S(1)} %get-tuple-element.35), channel_id=1, source_target_pairs={{0,16},{1,17},{2,18},{3,19},{4,20},{5,21},{6,22},{7,23},{8,24},{9,... | collective-permute-start | bytes 1179656 | tf_op jit(solution)/shard_map/ppermute | solution.py:94
  9.8 0.9 %copy-done.1 = bf16[512,128]{1,0:T(8,128)(2,1)S(1)} copy-done((bf16[512,128]{1,0:T(8,128)(2,1)S(1)}, bf16[512,128]{1,0:T(8,128)(2,1)}, u32[]{:S(2)}) %copy-start.1) | copy-done | bytes 131096
  10.8 0.9 %forward.1 = (f32[2,256,256]{2,1,0:T(8,128)S(1)}, bf16[256,128]{1,0:T(8,128)(2,1)S(1)}, bf16[256,128]{1,0:T(8,128)(2,1)S(1)}) custom-call(bf16[512,128]{1,0:T(8,128)(2,1)S(1)} %copy-done.1, bf16[512,128]{1,0:T(8,128)(2,1)S(1)} %copy-done.2, bf16[512,128]{1,0:T(8,128)(2,1)S(1)} %copy-done.3), custom_call_target="tpu_custom_call" | custom-call | flops 1 | bytes 1048576 | tf_op jit(solution)/shard_map/forward/pallas_call | solution.py:107
  11.8 6.7 %collective-permute-done.refs_5_ = bf16[64,3072]{1,0:T(8,128)(2,1)S(1)} collective-permute-done((bf16[64,3072]{1,0:T(8,128)(2,1)S(1)}, bf16[64,3072]{1,0:T(8,128)(2,1)S(1)}, u32[]{:S(2)}, u32[]{:S(2)}) %collective-permute-start) | collective-permute-done | bytes 393248 | tf_op jit(solution)/shard_map/ppermute | solution.py:94
  18.6 1.6 %collective-permute-start.3 = (bf16[256,128]{1,0:T(8,128)(2,1)S(1)}, bf16[256,128]{1,0:T(8,128)(2,1)S(1)}, u32[]{:S(2)}, u32[]{:S(2)}) collective-permute-start(bf16[256,128]{1,0:T(8,128)(2,1)S(1)} %get-tuple-element.40), channel_id=1, source_target_pairs={{0,2},{1,3},{2,0},{3,1},{4,6},{5,7},{6,4},{7,5},{8,10},{9,11},{10,... | collective-permute-start | bytes 196616 | tf_op jit(solution)/shard_map/ppermute | solution.py:94
  21.5 8.5 %collective-permute-done.1.refs_3_ = bf16[64,3072]{1,0:T(8,128)(2,1)S(1)} collective-permute-done((bf16[64,3072]{1,0:T(8,128)(2,1)S(1)}, bf16[64,3072]{1,0:T(8,128)(2,1)S(1)}, u32[]{:S(2)}, u32[]{:S(2)}) %collective-permute-start.1) | collective-permute-done | bytes 393248 | tf_op jit(solution)/shard_map/ppermute | solution.py:94
  30.0 1.9 %collective-permute-start.6 = (bf16[64,3072]{1,0:T(8,128)(2,1)S(1)}, bf16[64,3072]{1,0:T(8,128)(2,1)S(1)}, u32[]{:S(2)}, u32[]{:S(2)}) collective-permute-start(bf16[64,3072]{1,0:T(8,128)(2,1)S(1)} %collective-permute-done.1.refs_3_), channel_id=1, source_target_pairs={{0,1},{1,0},{2,3},{3,2},{4,5},{5,4},{6,7},{7,6},{8,9},{9,8},{10,11... | collective-permute-start | bytes 1179656 | tf_op jit(solution)/shard_map/ppermute | solution.py:94
  32.0 1.6 %collective-permute-start.4 = (bf16[512,128]{1,0:T(8,128)(2,1)S(1)}, bf16[512,128]{1,0:T(8,128)(2,1)S(1)}, u32[]{:S(2)}, u32[]{:S(2)}) collective-permute-start(bf16[512,128]{1,0:T(8,128)(2,1)S(1)} %constant_dynamic-update-slice_fusion.refs_11_), channel_id=1, source_target_pairs={{0,16},{1,17},{2,18},{3,19},{4,20},{5,21},{6,22},{7,23},{8,24},{9,... | collective-permute-start | bytes 393224 | tf_op jit(solution)/shard_map/ppermute | solution.py:94
  33.6 3.5 %collective-permute-done.4.refs_12_ = bf16[512,128]{1,0:T(8,128)(2,1)S(1)} collective-permute-done((bf16[512,128]{1,0:T(8,128)(2,1)S(1)}, bf16[512,128]{1,0:T(8,128)(2,1)S(1)}, u32[]{:S(2)}, u32[]{:S(2)}) %collective-permute-start.4) | collective-permute-done | bytes 131104 | tf_op jit(solution)/shard_map/ppermute | solution.py:94
  37.2 3.6 %collective-permute-done.10 = bf16[128,1536]{1,0:T(8,128)(2,1)S(1)} collective-permute-done((bf16[128,1536]{1,0:T(8,128)(2,1)S(1)}, bf16[128,1536]{1,0:T(8,128)(2,1)S(1)}, u32[]{:S(2)}, u32[]{:S(2)}) %collective-permute-start.10) | collective-permute-done | bytes 393248 | tf_op jit(solution)/shard_map/ppermute | solution.py:94
  40.9 3.7 %collective-permute-done.5.refs_7_ = bf16[64,1280]{1,0:T(8,128)(2,1)S(1)} collective-permute-done((bf16[64,1280]{1,0:T(8,128)(2,1)S(1)}, bf16[64,1280]{1,0:T(8,128)(2,1)S(1)}, u32[]{:S(2)}, u32[]{:S(2)}) %collective-permute-start.5) | collective-permute-done | bytes 163872 | tf_op jit(solution)/shard_map/ppermute | solution.py:94
  45.1 2.2 %products.2 = (f32[256,896]{1,0:T(8,128)S(1)}, bf16[256,896]{1,0:T(8,128)(2,1)S(1)}, f32[512,256]{1,0:T(8,128)S(1)}) custom-call(f32[8,128]{1,0:T(8,128)S(1)} %get-tuple-element.34.token.refs_0_, bf16[64,3072]{1,0:T(8,128)(2,1)S(1)} %get-tuple-element.37.refs_1_, bf16[64,3072]{1,0:T(8,128)(2,1)S(1)} %collective-permute-done.2.refs_2_, ...), custom_call_target="tpu_custom_call" | custom-call | flops 10000000000 | bytes 1048576 | tf_op jit(solution)/shard_map/products/pallas_call | solution.py:107
  47.3 2.6 %collective-permute-done.13.refs_8_ = bf16[64,1280]{1,0:T(8,128)(2,1)S(1)} collective-permute-done((bf16[64,1280]{1,0:T(8,128)(2,1)S(1)}, bf16[64,1280]{1,0:T(8,128)(2,1)S(1)}, u32[]{:S(2)}, u32[]{:S(2)}) %collective-permute-start.13) | collective-permute-done | bytes 163872 | tf_op jit(solution)/shard_map/ppermute | solution.py:94
  49.9 1.6 %products.3 = (f32[256,640]{1,0:T(8,128)S(1)}, bf16[256,640]{1,0:T(8,128)(2,1)S(1)}, f32[256,128]{1,0:T(8,128)S(1)}, bf16[256,128]{1,0:T(8,128)(2,1)S(1)}, bf16[...) custom-call(f32[8,128]{1,0:T(8,128)S(1)} %get-tuple-element.34.token.refs_0_, ...), custom_call_target="tpu_custom_call" | custom-call | flops 10000000000 | bytes 1048576 | tf_op jit(solution)/shard_map/products/pallas_call | solution.py:107
  51.6 1.6 %collective-permute-start.16 = (bf16[256,128]{1,0:T(8,128)(2,1)S(1)}, bf16[256,128]{1,0:T(8,128)(2,1)S(1)}, u32[]{:S(2)}, u32[]{:S(2)}) collective-permute-start(bf16[256,128]{1,0:T(8,128)(2,1)S(1)} %get-tuple-element.57), channel_id=1, source_target_pairs={{0,16},{1,17},{2,18},{3,19},{4,20},{5,21},{6,22},{7,23},{8,24},{9,... | collective-permute-start | bytes 196616 | tf_op jit(solution)/shard_map/ppermute | solution.py:94
  53.1 2.0 %collective-permute-start.18 = (bf16[256,128]{1,0:T(8,128)(2,1)S(1)}, bf16[256,128]{1,0:T(8,128)(2,1)S(1)}, u32[]{:S(2)}, u32[]{:S(2)}) collective-permute-start(bf16[256,128]{1,0:T(8,128)(2,1)S(1)} %get-tuple-element.59), channel_id=1, source_target_pairs={{0,18},{1,19},{2,16},{3,17},{4,22},{5,23},{6,20},{7,21},{8,26},{9,... | collective-permute-start | bytes 196616 | tf_op jit(solution)/shard_map/ppermute | solution.py:94
  55.4 2.1 %collective-permute-start.15 = (bf16[128,896]{1,0:T(8,128)(2,1)S(1)}, bf16[128,896]{1,0:T(8,128)(2,1)S(1)}, u32[]{:S(2)}, u32[]{:S(2)}) collective-permute-start(bf16[128,896]{1,0:T(8,128)(2,1)S(1)} %slice.50), channel_id=1, source_target_pairs={{0,2},{1,3},{2,0},{3,1},{4,6},{5,7},{6,4},{7,5},{8,10},{9,11},{10,... | collective-permute-start | bytes 688136 | tf_op jit(solution)/shard_map/ppermute | solution.py:94
  57.5 5.5 %collective-permute-done.19 = bf16[128,640]{1,0:T(8,128)(2,1)S(1)} collective-permute-done((bf16[128,640]{1,0:T(8,128)(2,1)S(1)}, bf16[128,640]{1,0:T(8,128)(2,1)S(1)}, u32[]{:S(2)}, u32[]{:S(2)}) %collective-permute-start.19) | collective-permute-done | bytes 163872 | tf_op jit(solution)/shard_map/ppermute | solution.py:94
  63.0 4.1 %collective-permute-done.15 = bf16[128,896]{1,0:T(8,128)(2,1)S(1)} collective-permute-done((bf16[128,896]{1,0:T(8,128)(2,1)S(1)}, bf16[128,896]{1,0:T(8,128)(2,1)S(1)}, u32[]{:S(2)}, u32[]{:S(2)}) %collective-permute-start.15) | collective-permute-done | bytes 229408 | tf_op jit(solution)/shard_map/ppermute | solution.py:94
  68.0 1.5 %backward.1 = (bf16[512,128]{1,0:T(8,128)(2,1)}, bf16[512,128]{1,0:T(8,128)(2,1)}, bf16[512,128]{1,0:T(8,128)(2,1)}) custom-call(f32[8,128]{1,0:T(8,128)S(1)} %fence.11.at, bf16[512,128]{1,0:T(8,128)(2,1)S(1)} %copy-done.1, bf16[512,128]{1,0:T(8,128)(2,1)S(1)} %copy-done.2, bf16[512,128]{1,0:T(8,128)(2,1)S(1)} %copy-done.3, ...), custom_call_target="tpu_custom_call" | custom-call | flops 10000000000 | bytes 1048576 | tf_op jit(solution)/shard_map/backward/pallas_call | solution.py:107
  (52 shorter events, 3.7 us)
Async XLA Ops:
  0.6 1.1 %copy-start = (bf16[64,6144]{1,0:T(8,128)(2,1)S(1)}, bf16[64,6144]{1,0:T(8,128)(2,1)}, u32[]{:S(2)}) copy-start(bf16[64,6144]{1,0:T(8,128)(2,1)} %cot.1) | copy-start | bytes 2359300
  2.7 27.3 %collective-permute-start.1 = (bf16[64,3072]{1,0:T(8,128)(2,1)S(1)}, bf16[64,3072]{1,0:T(8,128)(2,1)S(1)}, u32[]{:S(2)}, u32[]{:S(2)}) collective-permute-start(bf16[64,3072]{1,0:T(8,128)(2,1)S(1)} %get-tuple-element.37.refs_1_), channel_id=1, source_target_pairs={{0,4},{1,5},{2,6},{3,7},{4,0},{5,1},{6,2},{7,3},{8,12},{9,13},{10,... | collective-permute-start | bytes 1179656 | tf_op jit(solution)/shard_map/ppermute | solution.py:94
  6.7 11.8 %collective-permute-start.2 = (bf16[64,3072]{1,0:T(8,128)(2,1)S(1)}, bf16[64,3072]{1,0:T(8,128)(2,1)S(1)}, u32[]{:S(2)}, u32[]{:S(2)}) collective-permute-start(bf16[64,3072]{1,0:T(8,128)(2,1)S(1)} %get-tuple-element.37.refs_1_), channel_id=1, source_target_pairs={{0,1},{1,0},{2,3},{3,2},{4,5},{5,4},{6,7},{7,6},{8,9},{9,8},{10,11... | collective-permute-start | bytes 1179656 | tf_op jit(solution)/shard_map/ppermute | solution.py:94
  8.3 10.3 %collective-permute-start = (bf16[64,3072]{1,0:T(8,128)(2,1)S(1)}, bf16[64,3072]{1,0:T(8,128)(2,1)S(1)}, u32[]{:S(2)}, u32[]{:S(2)}) collective-permute-start(bf16[64,3072]{1,0:T(8,128)(2,1)S(1)} %get-tuple-element.35), channel_id=1, source_target_pairs={{0,16},{1,17},{2,18},{3,19},{4,20},{5,21},{6,22},{7,23},{8,24},{9,... | collective-permute-start | bytes 1179656 | tf_op jit(solution)/shard_map/ppermute | solution.py:94
  9.7 1.0 %copy-start.2 = (bf16[512,128]{1,0:T(8,128)(2,1)S(1)}, bf16[512,128]{1,0:T(8,128)(2,1)}, u32[]{:S(2)}) copy-start(bf16[512,128]{1,0:T(8,128)(2,1)} %k.3) | copy-start | bytes 393220
  9.7 1.0 %copy-start.3 = (bf16[512,128]{1,0:T(8,128)(2,1)S(1)}, bf16[512,128]{1,0:T(8,128)(2,1)}, u32[]{:S(2)}) copy-start(bf16[512,128]{1,0:T(8,128)(2,1)} %v.3) | copy-start | bytes 393220
  10.8 1.0 %copy-start.4 = (bf16[128,1536]{1,0:T(8,128)(2,1)S(1)}, bf16[128,1536]{1,0:T(8,128)(2,1)}, u32[]{:S(2)}) copy-start(bf16[128,1536]{1,0:T(8,128)(2,1)} %param.8) | copy-start | bytes 1179652
  18.6 13.4 %collective-permute-start.3 = (bf16[256,128]{1,0:T(8,128)(2,1)S(1)}, bf16[256,128]{1,0:T(8,128)(2,1)S(1)}, u32[]{:S(2)}, u32[]{:S(2)}) collective-permute-start(bf16[256,128]{1,0:T(8,128)(2,1)S(1)} %get-tuple-element.40), channel_id=1, source_target_pairs={{0,2},{1,3},{2,0},{3,1},{4,6},{5,7},{6,4},{7,5},{8,10},{9,11},{10,... | collective-permute-start | bytes 196616 | tf_op jit(solution)/shard_map/ppermute | solution.py:94
  20.1 24.9 %collective-permute-start.7 = (bf16[64,3072]{1,0:T(8,128)(2,1)S(1)}, bf16[64,3072]{1,0:T(8,128)(2,1)S(1)}, u32[]{:S(2)}, u32[]{:S(2)}) collective-permute-start(bf16[64,3072]{1,0:T(8,128)(2,1)S(1)} %collective-permute-done.refs_5_), channel_id=1, source_target_pairs={{0,1},{1,0},{2,3},{3,2},{4,5},{5,4},{6,7},{7,6},{8,9},{9,8},{10,11... | collective-permute-start | bytes 1179656 | tf_op jit(solution)/shard_map/ppermute | solution.py:94
  20.7 16.3 %collective-permute-start.8 = (bf16[64,1792]{1,0:T(8,128)(2,1)S(1)}, bf16[64,1792]{1,0:T(8,128)(2,1)S(1)}, u32[]{:S(2)}, u32[]{:S(2)}) collective-permute-start(bf16[64,1792]{1,0:T(8,128)(2,1)S(1)} %pad_maximum_fusion.1), channel_id=1, source_target_pairs={{0,4},{1,5},{2,6},{3,7},{4,0},{5,1},{6,2},{7,3},{8,12},{9,13},{10,... | collective-permute-start | bytes 688136 | tf_op jit(solution)/shard_map/ppermute | solution.py:94
  21.1 19.7 %collective-permute-start.10 = (bf16[128,1536]{1,0:T(8,128)(2,1)S(1)}, bf16[128,1536]{1,0:T(8,128)(2,1)S(1)}, u32[]{:S(2)}, u32[]{:S(2)}) collective-permute-start(bf16[128,1536]{1,0:T(8,128)(2,1)S(1)} %copy-done.4), channel_id=1, source_target_pairs={{0,2},{1,3},{2,0},{3,1},{4,6},{5,7},{6,4},{7,5},{8,10},{9,11},{10,... | collective-permute-start | bytes 1179656 | tf_op jit(solution)/shard_map/ppermute | solution.py:94
  30.0 15.0 %collective-permute-start.6 = (bf16[64,3072]{1,0:T(8,128)(2,1)S(1)}, bf16[64,3072]{1,0:T(8,128)(2,1)S(1)}, u32[]{:S(2)}, u32[]{:S(2)}) collective-permute-start(bf16[64,3072]{1,0:T(8,128)(2,1)S(1)} %collective-permute-done.1.refs_3_), channel_id=1, source_target_pairs={{0,1},{1,0},{2,3},{3,2},{4,5},{5,4},{6,7},{7,6},{8,9},{9,8},{10,11... | collective-permute-start | bytes 1179656 | tf_op jit(solution)/shard_map/ppermute | solution.py:94
  32.0 5.0 %collective-permute-start.4 = (bf16[512,128]{1,0:T(8,128)(2,1)S(1)}, bf16[512,128]{1,0:T(8,128)(2,1)S(1)}, u32[]{:S(2)}, u32[]{:S(2)}) collective-permute-start(bf16[512,128]{1,0:T(8,128)(2,1)S(1)} %constant_dynamic-update-slice_fusion.refs_11_), channel_id=1, source_target_pairs={{0,16},{1,17},{2,18},{3,19},{4,20},{5,21},{6,22},{7,23},{8,24},{9,... | collective-permute-start | bytes 393224 | tf_op jit(solution)/shard_map/ppermute | solution.py:94
  37.0 7.6 %collective-permute-start.5 = (bf16[64,1280]{1,0:T(8,128)(2,1)S(1)}, bf16[64,1280]{1,0:T(8,128)(2,1)S(1)}, u32[]{:S(2)}, u32[]{:S(2)}) collective-permute-start(bf16[64,1280]{1,0:T(8,128)(2,1)S(1)} %pad_maximum_fusion.2), channel_id=1, source_target_pairs={{0,4},{1,5},{2,6},{3,7},{4,0},{5,1},{6,2},{7,3},{8,12},{9,13},{10,... | collective-permute-start | bytes 491528 | tf_op jit(solution)/shard_map/ppermute | solution.py:94
  37.0 8.1 %collective-permute-start.9 = (bf16[64,1792]{1,0:T(8,128)(2,1)S(1)}, bf16[64,1792]{1,0:T(8,128)(2,1)S(1)}, u32[]{:S(2)}, u32[]{:S(2)}) collective-permute-start(bf16[64,1792]{1,0:T(8,128)(2,1)S(1)} %collective-permute-done.8.refs_7_), channel_id=1, source_target_pairs={{0,1},{1,0},{2,3},{3,2},{4,5},{5,4},{6,7},{7,6},{8,9},{9,8},{10,11... | collective-permute-start | bytes 688136 | tf_op jit(solution)/shard_map/ppermute | solution.py:94
  40.8 4.3 %collective-permute-start.11 = (bf16[256,1536]{1,0:T(8,128)(2,1)S(1)}, bf16[256,1536]{1,0:T(8,128)(2,1)S(1)}, u32[]{:S(2)}, u32[]{:S(2)}) collective-permute-start(bf16[256,1536]{1,0:T(8,128)(2,1)S(1)} %constant_dynamic-update-slice_fusion.2.refs_9_), channel_id=1, source_target_pairs={{0,8},{1,9},{2,10},{3,11},{4,12},{5,13},{6,14},{7,15},{8,0},{9,1},... | collective-permute-start | bytes 2359304 | tf_op jit(solution)/shard_map/ppermute | solution.py:94
  44.6 5.3 %collective-permute-start.13 = (bf16[64,1280]{1,0:T(8,128)(2,1)S(1)}, bf16[64,1280]{1,0:T(8,128)(2,1)S(1)}, u32[]{:S(2)}, u32[]{:S(2)}) collective-permute-start(bf16[64,1280]{1,0:T(8,128)(2,1)S(1)} %collective-permute-done.5.refs_7_), channel_id=1, source_target_pairs={{0,1},{1,0},{2,3},{3,2},{4,5},{5,4},{6,7},{7,6},{8,9},{9,8},{10,11... | collective-permute-start | bytes 491528 | tf_op jit(solution)/shard_map/ppermute | solution.py:94
  47.3 8.1 %collective-permute-start.12 = (bf16[256,896]{1,0:T(8,128)(2,1)S(1)}, bf16[256,896]{1,0:T(8,128)(2,1)S(1)}, u32[]{:S(2)}, u32[]{:S(2)}) collective-permute-start(bf16[256,896]{1,0:T(8,128)(2,1)S(1)} %get-tuple-element.47), channel_id=1, source_target_pairs={{0,8},{1,9},{2,10},{3,11},{4,12},{5,13},{6,14},{7,15},{8,0},{9,1},... | collective-permute-start | bytes 1376264 | tf_op jit(solution)/shard_map/ppermute | solution.py:94
  51.5 3.6 %collective-permute-start.14 = (bf16[256,640]{1,0:T(8,128)(2,1)S(1)}, bf16[256,640]{1,0:T(8,128)(2,1)S(1)}, u32[]{:S(2)}, u32[]{:S(2)}) collective-permute-start(bf16[256,640]{1,0:T(8,128)(2,1)S(1)} %get-tuple-element.51), channel_id=1, source_target_pairs={{0,8},{1,9},{2,10},{3,11},{4,12},{5,13},{6,14},{7,15},{8,0},{9,1},... | collective-permute-start | bytes 983048 | tf_op jit(solution)/shard_map/ppermute | solution.py:94
  51.6 16.4 %collective-permute-start.16 = (bf16[256,128]{1,0:T(8,128)(2,1)S(1)}, bf16[256,128]{1,0:T(8,128)(2,1)S(1)}, u32[]{:S(2)}, u32[]{:S(2)}) collective-permute-start(bf16[256,128]{1,0:T(8,128)(2,1)S(1)} %get-tuple-element.57), channel_id=1, source_target_pairs={{0,16},{1,17},{2,18},{3,19},{4,20},{5,21},{6,22},{7,23},{8,24},{9,... | collective-permute-start | bytes 196616 | tf_op jit(solution)/shard_map/ppermute | solution.py:94
  53.1 14.8 %collective-permute-start.17 = (bf16[256,128]{1,0:T(8,128)(2,1)S(1)}, bf16[256,128]{1,0:T(8,128)(2,1)S(1)}, u32[]{:S(2)}, u32[]{:S(2)}) collective-permute-start(bf16[256,128]{1,0:T(8,128)(2,1)S(1)} %get-tuple-element.58), channel_id=1, source_target_pairs={{0,2},{1,3},{2,0},{3,1},{4,6},{5,7},{6,4},{7,5},{8,10},{9,11},{10,... | collective-permute-start | bytes 196616 | tf_op jit(solution)/shard_map/ppermute | solution.py:94
  53.1 14.8 %collective-permute-start.18 = (bf16[256,128]{1,0:T(8,128)(2,1)S(1)}, bf16[256,128]{1,0:T(8,128)(2,1)S(1)}, u32[]{:S(2)}, u32[]{:S(2)}) collective-permute-start(bf16[256,128]{1,0:T(8,128)(2,1)S(1)} %get-tuple-element.59), channel_id=1, source_target_pairs={{0,18},{1,19},{2,16},{3,17},{4,22},{5,23},{6,20},{7,21},{8,26},{9,... | collective-permute-start | bytes 196616 | tf_op jit(solution)/shard_map/ppermute | solution.py:94
  55.2 7.8 %collective-permute-start.19 = (bf16[128,640]{1,0:T(8,128)(2,1)S(1)}, bf16[128,640]{1,0:T(8,128)(2,1)S(1)}, u32[]{:S(2)}, u32[]{:S(2)}) collective-permute-start(bf16[128,640]{1,0:T(8,128)(2,1)S(1)} %slice.51), channel_id=1, source_target_pairs={{0,2},{1,3},{2,0},{3,1},{4,6},{5,7},{6,4},{7,5},{8,10},{9,11},{10,... | collective-permute-start | bytes 491528 | tf_op jit(solution)/shard_map/ppermute | solution.py:94
  55.4 11.7 %collective-permute-start.15 = (bf16[128,896]{1,0:T(8,128)(2,1)S(1)}, bf16[128,896]{1,0:T(8,128)(2,1)S(1)}, u32[]{:S(2)}, u32[]{:S(2)}) collective-permute-start(bf16[128,896]{1,0:T(8,128)(2,1)S(1)} %slice.50), channel_id=1, source_target_pairs={{0,2},{1,3},{2,0},{3,1},{4,6},{5,7},{6,4},{7,5},{8,10},{9,11},{10,... | collective-permute-start | bytes 688136 | tf_op jit(solution)/shard_map/ppermute | solution.py:94
  (1 other events, 0.9 us)

commit v7 on v6

--- a/solution.py
+++ b/solution.py
@@ -13,7 +13,7 @@
 ANY = pl.BlockSpec(memory_space=pl.ANY)
 VMEM = pl.BlockSpec(memory_space=pltpu.VMEM)
 F32 = jnp.float32
-SMALL, LARGE = 1, 10000000000
+SMALL, LARGE, LAST = 50000000000, 1000000000, 1000000000
 BF16 = jnp.bfloat16
 
 
@@ -188,7 +188,7 @@
     images = q.shape[0] // PATCH
     ins = [at, q, k, v, probs, own, from_x, from_z, from_xz]
     scratch = [pltpu.VMEM((images, PATCH, HD), BF16)]
-    return call("backward", backward_kernel, [(q.shape, BF16)] * 3, ins, LARGE, scratch)
+    return call("backward", backward_kernel, [(q.shape, BF16)] * 3, ins, LAST, scratch)
 
 
 def products_kernel(low, high, first, last, places, *refs):
@@ -202,7 +202,7 @@
     d_refs = refs
     at = place()
     width = high - low
-    tile = next(size for size in (512, 384, 256, 128) if width % size == 0)
+    tiles = [(start, min(512, width - start)) for start in range(0, width, 512)]
     rows = []
     for n in range(4):
         z1 = 1 - at["z1"] if n // 2 else at["z1"]
@@ -220,7 +220,7 @@
     d = None if first else before[...]
     for other in (1, 0):
         c = 1 - at["c"] if other else at["c"]
-        for start in range(0, width, tile):
+        for start, tile in tiles:
             cot = jnp.concatenate(
                 [
                     block[row : row + 64, pl.ds(pl.multiple_of(c * half + start + skip, 128), tile)]
@@ -299,58 +299,59 @@
 
 
 def on_device_4x8(queries, keys, values, w_out, cotangent):
-    m, o, m1, _, m2, _, token = pack(cotangent, ((0, CUTS[-1][1]), *CUTS))
+    m, o, token = pack(cotangent, ((0, CUTS[-1][1]),))
     at0 = fence(token, cost=1)
     at1 = fence(at0, cost=10**10)
-    x = send(o, x=1)
-    at2 = fence(at1, x, cost=10**10)
     za = send(m, z1=1)
     probs, mine, others = forward(queries, keys, values)
     ya = send(m, y=1)
-    att_z = send(after(others, at0, ya), z0=1)
+    att_z = send(after(others, ya), z0=1)
     att = two(mine, att_z)
-    att_x = send(att, x=1)
-    at3 = fence(at2, za, att_x, cost=10**10)
-    at4 = fence(at3, cost=10**10)
+    att_x = send(after(att, ya), x=1)
+    x = send(o, x=1)
+    at2 = fence(at1, za, att_x, x, cost=10**10)
+    at3 = fence(at2, cost=10**10)
+    w_z = send(after(w_out, x, ya), z0=1)
+    w_c = send(after(two(w_out, w_z), w_z), c=1)
+    at4 = fence(at3, w_c, cost=2 * 10**10)
+    att_all = [att, att_x]
+    own_x = after(att_all[0], za)
+    sa = send(after(za, att_x, ya), y=1)
+    yx = send(x, y=1)
     x1, x2 = cut(x, CUTS)
-    zb2 = send(after(x2, at3), z1=1)
-    at5 = fence(at4, zb2, cost=10**10)
-    att_all = [att, att_x]
-    own_x = att_all[0]
-    sa = send(za, y=1)
-    yx = send(after(x, at2), y=1)
     zb1 = send(x1, z1=1)
     sb1 = send(zb1, y=1)
-    w_z = send(after(w_out, x), z0=1)
     w_own = two(w_out, w_z)
-    w_c = send(two(w_out, w_z), c=1)
     w_all = [w_own, w_c]
     blocks = [(m, 0), (ya, 0), (za, 0), (sa, 0), (x, 0), (yx, 0), (zb1, 0), (sb1, 0)]
     keep1, give1, d = products(
         CUTS[0], blocks, w_all, [own_x, att_all[1]], token, None, False
     )
-    got1 = send(give1, c=1)
-    total1 = keep1 + got1.astype(F32)
-    to_pair1 = total1[HD:].astype(BF16)
-    own_x = after(att_all[0], at4, at2)
-    sb2 = send(after(zb2, at4), y=1)
+    got1 = send(after(give1, give1, att_z), c=1)
+    at5 = fence(at4, att_x, got1, cost=10**10)
+    own_x = after(att_all[0], give1)
+    zb2 = send(after(x2, at2, za, att_z), z1=1)
+    sb2 = send(after(zb2, at3), y=1)
     blocks = [(m, 0), (ya, 0), (za, 0), (sa, 0), (x, 0), (yx, 0), (zb2, 0), (sb2, 0)]
     keep2, give2, own, to_x, to_z, to_xz = products(
         CUTS[1], blocks, w_all, [own_x, att_all[1]], token, d, True
     )
     got2 = send(give2, c=1)
-    pair1 = send(after(to_pair1, got2), z0=1)
-    queries = after(queries, pair1, at1)
-    from_x = send(after(to_x, at0), x=1)
-    from_z = send(to_z, z0=1)
+    total2 = keep2 + got2.astype(F32)
+    to_pair2 = total2[HD:].astype(BF16)
+    pair2 = send(after(to_pair2, at2), z0=1)
+    queries = after(queries, pair2, at3)
+    from_x = send(after(to_x, at0, got1), x=1)
+    from_z = send(after(to_z, at1), z0=1)
     from_xz = send(to_xz, x=1, z0=1)
     grads = backward(at5, queries, keys, values, probs, own, from_x, from_z, from_xz)
+    total1 = keep1 + got1.astype(F32)
     rest1 = total1[:HD]
+    rest2 = total2[:HD]
+    rest2 = after(rest2, grads[0])
+    to_pair1 = total1[HD:].astype(BF16)
+    pair1 = send(after(to_pair1, at1), z0=1)
     part1 = (rest1 + pair1.astype(F32)).astype(BF16)
-    total2 = keep2 + got2.astype(F32)
-    rest2 = total2[:HD]
-    to_pair2 = total2[HD:].astype(BF16)
-    pair2 = send(to_pair2, z0=1)
     part2 = (rest2 + pair2.astype(F32)).astype(BF16)
     return *grads, jnp.concatenate([part1, part2], axis=1)
 

time: 69.7 us -> 67 us (0.961)
  the two profiles are of different devices: /device:TPU:0 before, /device:TPU:20 now
where the time goes in v7:
time: 67 us; the launch traced here: 66.8 us
  waiting for transfers between devices  33.6 us (50%)
  starting transfers between devices  23.5 us (35%)
  Pallas kernels  4.81 us (7%)
  local copies, waits for them, and re-layouts  3.07 us (5%)
  other arithmetic  1.07 us (2%)
  between operations  0.82 us (1%)
    ppermute x20, waiting for transfers between devices, send(): return lax.ppermute(value, AXES, flip(**bits))  33.6 us
    ppermute x20, starting transfers between devices, send(): return lax.ppermute(value, AXES, flip(**bits))  23.5 us
    pallas_call x11, Pallas kernels, call(): pl.pallas_call(kernel, out_shape=[jax.ShapeDtypeStruct(shape, kind) for s...  4.81 us
    unnamed x14, local copies, waits for them, and re-layouts  2.94 us
  transfers between devices with their start and end apart: 20, of which 8 were waited for; matrix products, arithmetic and copies ran while one was open for 1% of the time, Pallas kernels for 7%

profile of v7, /device:TPU:20, one launch (start us, length us, event | category | flops | bytes accessed | tf_op | source)
XLA Modules:
  0.0 66.8 jit_solution(17430839956481631898)
XLA Ops:
  0.6 1.1 %copy-done = bf16[64,6144]{1,0:T(8,128)(2,1)S(1)} copy-done((bf16[64,6144]{1,0:T(8,128)(2,1)S(1)}, bf16[64,6144]{1,0:T(8,128)(2,1)}, u32[]{:S(2)}) %copy-start) | copy-done | bytes 786456
  2.4 1.8 %collective-permute-start.4 = (bf16[64,3072]{1,0:T(8,128)(2,1)S(1)}, bf16[64,3072]{1,0:T(8,128)(2,1)S(1)}, u32[]{:S(2)}, u32[]{:S(2)}) collective-permute-start(bf16[64,3072]{1,0:T(8,128)(2,1)S(1)} %get-tuple-element.47), channel_id=1, source_target_pairs={{0,16},{1,17},{2,18},{3,19},{4,20},{5,21},{6,22},{7,23},{8,24},{9,... | collective-permute-start | bytes 1179656 | tf_op jit(solution)/shard_map/ppermute | solution.py:94
  4.2 0.9 %forward.1 = (f32[2,256,256]{2,1,0:T(8,128)S(1)}, bf16[256,128]{1,0:T(8,128)(2,1)S(1)}, bf16[256,128]{1,0:T(8,128)(2,1)S(1)}) custom-call(bf16[512,128]{1,0:T(8,128)(2,1)S(1)} %copy-done.1, bf16[512,128]{1,0:T(8,128)(2,1)S(1)} %copy-done.2, bf16[512,128]{1,0:T(8,128)(2,1)S(1)} %copy-done.3), custom_call_target="tpu_custom_call" | custom-call | flops 49999998976 | bytes 1048576 | tf_op jit(solution)/shard_map/forward/pallas_call | solution.py:107
  5.2 1.0 %copy-done.5 = bf16[128,1536]{1,0:T(8,128)(2,1)S(1)} copy-done((bf16[128,1536]{1,0:T(8,128)(2,1)S(1)}, bf16[128,1536]{1,0:T(8,128)(2,1)}, u32[]{:S(2)}) %copy-start.5) | copy-done | bytes 393240
  6.2 6.6 %collective-permute-done.1.refs_2_ = bf16[64,3072]{1,0:T(8,128)(2,1)S(1)} collective-permute-done((bf16[64,3072]{1,0:T(8,128)(2,1)S(1)}, bf16[64,3072]{1,0:T(8,128)(2,1)S(1)}, u32[]{:S(2)}, u32[]{:S(2)}) %collective-permute-start.1) | collective-permute-done | bytes 393248 | tf_op jit(solution)/shard_map/ppermute | solution.py:94
  12.7 1.6 %collective-permute-start.2 = (bf16[256,128]{1,0:T(8,128)(2,1)S(1)}, bf16[256,128]{1,0:T(8,128)(2,1)S(1)}, u32[]{:S(2)}, u32[]{:S(2)}) collective-permute-start(bf16[256,128]{1,0:T(8,128)(2,1)S(1)} %get-tuple-element.45), channel_id=1, source_target_pairs={{0,2},{1,3},{2,0},{3,1},{4,6},{5,7},{6,4},{7,5},{8,10},{9,11},{10,... | collective-permute-start | bytes 196616 | tf_op jit(solution)/shard_map/ppermute | solution.py:94
  14.8 2.5 %collective-permute-start.9 = (bf16[64,1792]{1,0:T(8,128)(2,1)S(1)}, bf16[64,1792]{1,0:T(8,128)(2,1)S(1)}, u32[]{:S(2)}, u32[]{:S(2)}) collective-permute-start(bf16[64,1792]{1,0:T(8,128)(2,1)S(1)} %pad_maximum_fusion.1), channel_id=1, source_target_pairs={{0,4},{1,5},{2,6},{3,7},{4,0},{5,1},{6,2},{7,3},{8,12},{9,13},{10,... | collective-permute-start | bytes 688136 | tf_op jit(solution)/shard_map/ppermute | solution.py:94
  17.3 1.5 %collective-permute-start.8 = (bf16[64,3072]{1,0:T(8,128)(2,1)S(1)}, bf16[64,3072]{1,0:T(8,128)(2,1)S(1)}, u32[]{:S(2)}, u32[]{:S(2)}) collective-permute-start(bf16[64,3072]{1,0:T(8,128)(2,1)S(1)} %collective-permute-done.4.refs_5_), channel_id=1, source_target_pairs={{0,1},{1,0},{2,3},{3,2},{4,5},{5,4},{6,7},{7,6},{8,9},{9,8},{10,11... | collective-permute-start | bytes 1179656 | tf_op jit(solution)/shard_map/ppermute | solution.py:94
  18.9 6.0 %collective-permute-done.2 = bf16[256,128]{1,0:T(8,128)(2,1)S(1)} collective-permute-done((bf16[256,128]{1,0:T(8,128)(2,1)S(1)}, bf16[256,128]{1,0:T(8,128)(2,1)S(1)}, u32[]{:S(2)}, u32[]{:S(2)}) %collective-permute-start.2) | collective-permute-done | bytes 65568 | tf_op jit(solution)/shard_map/ppermute | solution.py:94
  24.8 1.6 %collective-permute-start.3 = (bf16[512,128]{1,0:T(8,128)(2,1)S(1)}, bf16[512,128]{1,0:T(8,128)(2,1)S(1)}, u32[]{:S(2)}, u32[]{:S(2)}) collective-permute-start(bf16[512,128]{1,0:T(8,128)(2,1)S(1)} %constant_dynamic-update-slice_fusion.refs_11_), channel_id=1, source_target_pairs={{0,16},{1,17},{2,18},{3,19},{4,20},{5,21},{6,22},{7,23},{8,24},{9,... | collective-permute-start | bytes 393224 | tf_op jit(solution)/shard_map/ppermute | solution.py:94
  26.4 3.5 %collective-permute-done.3.refs_12_ = bf16[512,128]{1,0:T(8,128)(2,1)S(1)} collective-permute-done((bf16[512,128]{1,0:T(8,128)(2,1)S(1)}, bf16[512,128]{1,0:T(8,128)(2,1)S(1)}, u32[]{:S(2)}, u32[]{:S(2)}) %collective-permute-start.3) | collective-permute-done | bytes 131104 | tf_op jit(solution)/shard_map/ppermute | solution.py:94
  30.0 3.6 %collective-permute-start.12 = (bf16[64,1280]{1,0:T(8,128)(2,1)S(1)}, bf16[64,1280]{1,0:T(8,128)(2,1)S(1)}, u32[]{:S(2)}, u32[]{:S(2)}) collective-permute-start(bf16[64,1280]{1,0:T(8,128)(2,1)S(1)} %pad_maximum_fusion.2), channel_id=1, source_target_pairs={{0,4},{1,5},{2,6},{3,7},{4,0},{5,1},{6,2},{7,3},{8,12},{9,13},{10,... | collective-permute-start | bytes 491528 | tf_op jit(solution)/shard_map/ppermute | solution.py:94
  33.5 1.8 %collective-permute-start.10 = (bf16[64,1792]{1,0:T(8,128)(2,1)S(1)}, bf16[64,1792]{1,0:T(8,128)(2,1)S(1)}, u32[]{:S(2)}, u32[]{:S(2)}) collective-permute-start(bf16[64,1792]{1,0:T(8,128)(2,1)S(1)} %collective-permute-done.9.refs_7_), channel_id=1, source_target_pairs={{0,1},{1,0},{2,3},{3,2},{4,5},{5,4},{6,7},{7,6},{8,9},{9,8},{10,11... | collective-permute-start | bytes 688136 | tf_op jit(solution)/shard_map/ppermute | solution.py:94
  35.3 4.3 %collective-permute-done.5 = bf16[128,1536]{1,0:T(8,128)(2,1)S(1)} collective-permute-done((bf16[128,1536]{1,0:T(8,128)(2,1)S(1)}, bf16[128,1536]{1,0:T(8,128)(2,1)S(1)}, u32[]{:S(2)}, u32[]{:S(2)}) %collective-permute-start.5) | collective-permute-done | bytes 393248 | tf_op jit(solution)/shard_map/ppermute | solution.py:94
  39.7 1.0 %collective-permute-start.13 = (bf16[64,1280]{1,0:T(8,128)(2,1)S(1)}, bf16[64,1280]{1,0:T(8,128)(2,1)S(1)}, u32[]{:S(2)}, u32[]{:S(2)}) collective-permute-start(bf16[64,1280]{1,0:T(8,128)(2,1)S(1)} %collective-permute-done.12.refs_7_), channel_id=1, source_target_pairs={{0,1},{1,0},{2,3},{3,2},{4,5},{5,4},{6,7},{7,6},{8,9},{9,8},{10,11... | collective-permute-start | bytes 491528 | tf_op jit(solution)/shard_map/ppermute | solution.py:94
  40.7 5.5 %collective-permute-done.10.refs_8_ = bf16[64,1792]{1,0:T(8,128)(2,1)S(1)} collective-permute-done((bf16[64,1792]{1,0:T(8,128)(2,1)S(1)}, bf16[64,1792]{1,0:T(8,128)(2,1)S(1)}, u32[]{:S(2)}, u32[]{:S(2)}) %collective-permute-start.10) | collective-permute-done | bytes 229408 | tf_op jit(solution)/shard_map/ppermute | solution.py:94
  46.2 1.3 %products.2 = (f32[256,896]{1,0:T(8,128)S(1)}, bf16[256,896]{1,0:T(8,128)(2,1)S(1)}, f32[512,256]{1,0:T(8,128)S(1)}) custom-call(f32[8,128]{1,0:T(8,128)S(1)} %get-tuple-element.41.token.refs_0_, bf16[64,3072]{1,0:T(8,128)(2,1)S(1)} %get-tuple-element.42.refs_1_, bf16[64,3072]{1,0:T(8,128)(2,1)S(1)} %collective-permute-done.1.refs_2_, ...), custom_call_target="tpu_custom_call" | custom-call | flops 1000000000 | bytes 1048576 | tf_op jit(solution)/shard_map/products/pallas_call | solution.py:107
  48.0 1.0 %products.3 = (f32[256,640]{1,0:T(8,128)S(1)}, bf16[256,640]{1,0:T(8,128)(2,1)S(1)}, f32[256,128]{1,0:T(8,128)S(1)}, bf16[256,128]{1,0:T(8,128)(2,1)S(1)}, bf16[...) custom-call(f32[8,128]{1,0:T(8,128)S(1)} %get-tuple-element.41.token.refs_0_, ...), custom_call_target="tpu_custom_call" | custom-call | flops 1000000000 | bytes 1048576 | tf_op jit(solution)/shard_map/products/pallas_call | solution.py:107
  49.2 3.2 %collective-permute-start.17 = (bf16[256,128]{1,0:T(8,128)(2,1)S(1)}, bf16[256,128]{1,0:T(8,128)(2,1)S(1)}, u32[]{:S(2)}, u32[]{:S(2)}) collective-permute-start(bf16[256,128]{1,0:T(8,128)(2,1)S(1)} %get-tuple-element.70), channel_id=1, source_target_pairs={{0,2},{1,3},{2,0},{3,1},{4,6},{5,7},{6,4},{7,5},{8,10},{9,11},{10,... | collective-permute-start | bytes 196616 | tf_op jit(solution)/shard_map/ppermute | solution.py:94
  52.4 0.9 %collective-permute-start.18 = (bf16[256,128]{1,0:T(8,128)(2,1)S(1)}, bf16[256,128]{1,0:T(8,128)(2,1)S(1)}, u32[]{:S(2)}, u32[]{:S(2)}) collective-permute-start(bf16[256,128]{1,0:T(8,128)(2,1)S(1)} %get-tuple-element.71), channel_id=1, source_target_pairs={{0,18},{1,19},{2,16},{3,17},{4,22},{5,23},{6,20},{7,21},{8,26},{9,... | collective-permute-start | bytes 196616 | tf_op jit(solution)/shard_map/ppermute | solution.py:94
  54.2 2.0 %collective-permute-start.15 = (bf16[128,640]{1,0:T(8,128)(2,1)S(1)}, bf16[128,640]{1,0:T(8,128)(2,1)S(1)}, u32[]{:S(2)}, u32[]{:S(2)}) collective-permute-start(bf16[128,640]{1,0:T(8,128)(2,1)S(1)} %slice.48), channel_id=1, source_target_pairs={{0,2},{1,3},{2,0},{3,1},{4,6},{5,7},{6,4},{7,5},{8,10},{9,11},{10,... | collective-permute-start | bytes 491528 | tf_op jit(solution)/shard_map/ppermute | solution.py:94
  57.1 4.7 %collective-permute-done.15 = bf16[128,640]{1,0:T(8,128)(2,1)S(1)} collective-permute-done((bf16[128,640]{1,0:T(8,128)(2,1)S(1)}, bf16[128,640]{1,0:T(8,128)(2,1)S(1)}, u32[]{:S(2)}, u32[]{:S(2)}) %collective-permute-start.15) | collective-permute-done | bytes 163872 | tf_op jit(solution)/shard_map/ppermute | solution.py:94
  61.8 1.5 %backward.1 = (bf16[512,128]{1,0:T(8,128)(2,1)}, bf16[512,128]{1,0:T(8,128)(2,1)}, bf16[512,128]{1,0:T(8,128)(2,1)}) custom-call(f32[8,128]{1,0:T(8,128)S(1)} %fence.11.at, bf16[512,128]{1,0:T(8,128)(2,1)S(1)} %copy-done.1, bf16[512,128]{1,0:T(8,128)(2,1)S(1)} %copy-done.2, bf16[512,128]{1,0:T(8,128)(2,1)S(1)} %copy-done.3, ...), custom_call_target="tpu_custom_call" | custom-call | flops 1000000000 | bytes 1048576 | tf_op jit(solution)/shard_map/backward/pallas_call | solution.py:107
  63.3 2.7 %collective-permute-done.19 = bf16[128,896]{1,0:T(8,128)(2,1)S(1)} collective-permute-done((bf16[128,896]{1,0:T(8,128)(2,1)S(1)}, bf16[128,896]{1,0:T(8,128)(2,1)S(1)}, u32[]{:S(2)}, u32[]{:S(2)}) %collective-permute-start.19) | collective-permute-done | bytes 229408 | tf_op jit(solution)/shard_map/ppermute | solution.py:94
  (56 shorter events, 4.6 us)
Async XLA Ops:
  1.8 2.5 %copy-start.1 = (bf16[512,128]{1,0:T(8,128)(2,1)S(1)}, bf16[512,128]{1,0:T(8,128)(2,1)}, u32[]{:S(2)}) copy-start(bf16[512,128]{1,0:T(8,128)(2,1)} %q.2) | copy-start | bytes 393220
  1.8 2.5 %copy-start.2 = (bf16[512,128]{1,0:T(8,128)(2,1)S(1)}, bf16[512,128]{1,0:T(8,128)(2,1)}, u32[]{:S(2)}) copy-start(bf16[512,128]{1,0:T(8,128)(2,1)} %k.3) | copy-start | bytes 393220
  1.8 2.5 %copy-start.3 = (bf16[512,128]{1,0:T(8,128)(2,1)S(1)}, bf16[512,128]{1,0:T(8,128)(2,1)}, u32[]{:S(2)}) copy-start(bf16[512,128]{1,0:T(8,128)(2,1)} %v.3) | copy-start | bytes 393220
  1.8 10.9 %collective-permute-start.1 = (bf16[64,3072]{1,0:T(8,128)(2,1)S(1)}, bf16[64,3072]{1,0:T(8,128)(2,1)S(1)}, u32[]{:S(2)}, u32[]{:S(2)}) collective-permute-start(bf16[64,3072]{1,0:T(8,128)(2,1)S(1)} %get-tuple-element.42.refs_1_), channel_id=1, source_target_pairs={{0,1},{1,0},{2,3},{3,2},{4,5},{5,4},{6,7},{7,6},{8,9},{9,8},{10,11... | collective-permute-start | bytes 1179656 | tf_op jit(solution)/shard_map/ppermute | solution.py:94
  2.4 24.0 %collective-permute-start = (bf16[64,3072]{1,0:T(8,128)(2,1)S(1)}, bf16[64,3072]{1,0:T(8,128)(2,1)S(1)}, u32[]{:S(2)}, u32[]{:S(2)}) collective-permute-start(bf16[64,3072]{1,0:T(8,128)(2,1)S(1)} %get-tuple-element.42.refs_1_), channel_id=1, source_target_pairs={{0,4},{1,5},{2,6},{3,7},{4,0},{5,1},{6,2},{7,3},{8,12},{9,13},{10,... | collective-permute-start | bytes 1179656 | tf_op jit(solution)/shard_map/ppermute | solution.py:94
  2.4 11.9 %collective-permute-start.4 = (bf16[64,3072]{1,0:T(8,128)(2,1)S(1)}, bf16[64,3072]{1,0:T(8,128)(2,1)S(1)}, u32[]{:S(2)}, u32[]{:S(2)}) collective-permute-start(bf16[64,3072]{1,0:T(8,128)(2,1)S(1)} %get-tuple-element.47), channel_id=1, source_target_pairs={{0,16},{1,17},{2,18},{3,19},{4,20},{5,21},{6,22},{7,23},{8,24},{9,... | collective-permute-start | bytes 1179656 | tf_op jit(solution)/shard_map/ppermute | solution.py:94
  12.7 12.1 %collective-permute-start.2 = (bf16[256,128]{1,0:T(8,128)(2,1)S(1)}, bf16[256,128]{1,0:T(8,128)(2,1)S(1)}, u32[]{:S(2)}, u32[]{:S(2)}) collective-permute-start(bf16[256,128]{1,0:T(8,128)(2,1)S(1)} %get-tuple-element.45), channel_id=1, source_target_pairs={{0,2},{1,3},{2,0},{3,1},{4,6},{5,7},{6,4},{7,5},{8,10},{9,11},{10,... | collective-permute-start | bytes 196616 | tf_op jit(solution)/shard_map/ppermute | solution.py:94
  14.3 25.2 %collective-permute-start.5 = (bf16[128,1536]{1,0:T(8,128)(2,1)S(1)}, bf16[128,1536]{1,0:T(8,128)(2,1)S(1)}, u32[]{:S(2)}, u32[]{:S(2)}) collective-permute-start(bf16[128,1536]{1,0:T(8,128)(2,1)S(1)} %copy-done.5), channel_id=1, source_target_pairs={{0,2},{1,3},{2,0},{3,1},{4,6},{5,7},{6,4},{7,5},{8,10},{9,11},{10,... | collective-permute-start | bytes 1179656 | tf_op jit(solution)/shard_map/ppermute | solution.py:94
  14.8 18.7 %collective-permute-start.9 = (bf16[64,1792]{1,0:T(8,128)(2,1)S(1)}, bf16[64,1792]{1,0:T(8,128)(2,1)S(1)}, u32[]{:S(2)}, u32[]{:S(2)}) collective-permute-start(bf16[64,1792]{1,0:T(8,128)(2,1)S(1)} %pad_maximum_fusion.1), channel_id=1, source_target_pairs={{0,4},{1,5},{2,6},{3,7},{4,0},{5,1},{6,2},{7,3},{8,12},{9,13},{10,... | collective-permute-start | bytes 688136 | tf_op jit(solution)/shard_map/ppermute | solution.py:94
  17.3 23.4 %collective-permute-start.8 = (bf16[64,3072]{1,0:T(8,128)(2,1)S(1)}, bf16[64,3072]{1,0:T(8,128)(2,1)S(1)}, u32[]{:S(2)}, u32[]{:S(2)}) collective-permute-start(bf16[64,3072]{1,0:T(8,128)(2,1)S(1)} %collective-permute-done.4.refs_5_), channel_id=1, source_target_pairs={{0,1},{1,0},{2,3},{3,2},{4,5},{5,4},{6,7},{7,6},{8,9},{9,8},{10,11... | collective-permute-start | bytes 1179656 | tf_op jit(solution)/shard_map/ppermute | solution.py:94
  24.8 5.0 %collective-permute-start.3 = (bf16[512,128]{1,0:T(8,128)(2,1)S(1)}, bf16[512,128]{1,0:T(8,128)(2,1)S(1)}, u32[]{:S(2)}, u32[]{:S(2)}) collective-permute-start(bf16[512,128]{1,0:T(8,128)(2,1)S(1)} %constant_dynamic-update-slice_fusion.refs_11_), channel_id=1, source_target_pairs={{0,16},{1,17},{2,18},{3,19},{4,20},{5,21},{6,22},{7,23},{8,24},{9,... | collective-permute-start | bytes 393224 | tf_op jit(solution)/shard_map/ppermute | solution.py:94
  29.9 16.3 %collective-permute-start.7 = (bf16[64,3072]{1,0:T(8,128)(2,1)S(1)}, bf16[64,3072]{1,0:T(8,128)(2,1)S(1)}, u32[]{:S(2)}, u32[]{:S(2)}) collective-permute-start(bf16[64,3072]{1,0:T(8,128)(2,1)S(1)} %collective-permute-done.refs_3_), channel_id=1, source_target_pairs={{0,1},{1,0},{2,3},{3,2},{4,5},{5,4},{6,7},{7,6},{8,9},{9,8},{10,11... | collective-permute-start | bytes 1179656 | tf_op jit(solution)/shard_map/ppermute | solution.py:94
  30.0 9.7 %collective-permute-start.12 = (bf16[64,1280]{1,0:T(8,128)(2,1)S(1)}, bf16[64,1280]{1,0:T(8,128)(2,1)S(1)}, u32[]{:S(2)}, u32[]{:S(2)}) collective-permute-start(bf16[64,1280]{1,0:T(8,128)(2,1)S(1)} %pad_maximum_fusion.2), channel_id=1, source_target_pairs={{0,4},{1,5},{2,6},{3,7},{4,0},{5,1},{6,2},{7,3},{8,12},{9,13},{10,... | collective-permute-start | bytes 491528 | tf_op jit(solution)/shard_map/ppermute | solution.py:94
  33.5 12.7 %collective-permute-start.10 = (bf16[64,1792]{1,0:T(8,128)(2,1)S(1)}, bf16[64,1792]{1,0:T(8,128)(2,1)S(1)}, u32[]{:S(2)}, u32[]{:S(2)}) collective-permute-start(bf16[64,1792]{1,0:T(8,128)(2,1)S(1)} %collective-permute-done.9.refs_7_), channel_id=1, source_target_pairs={{0,1},{1,0},{2,3},{3,2},{4,5},{5,4},{6,7},{7,6},{8,9},{9,8},{10,11... | collective-permute-start | bytes 688136 | tf_op jit(solution)/shard_map/ppermute | solution.py:94
  39.6 6.6 %collective-permute-start.6 = (bf16[256,1536]{1,0:T(8,128)(2,1)S(1)}, bf16[256,1536]{1,0:T(8,128)(2,1)S(1)}, u32[]{:S(2)}, u32[]{:S(2)}) collective-permute-start(bf16[256,1536]{1,0:T(8,128)(2,1)S(1)} %constant_dynamic-update-slice_fusion.2.refs_9_), channel_id=1, source_target_pairs={{0,8},{1,9},{2,10},{3,11},{4,12},{5,13},{6,14},{7,15},{8,0},{9,1},... | collective-permute-start | bytes 2359304 | tf_op jit(solution)/shard_map/ppermute | solution.py:94
  39.7 8.4 %collective-permute-start.13 = (bf16[64,1280]{1,0:T(8,128)(2,1)S(1)}, bf16[64,1280]{1,0:T(8,128)(2,1)S(1)}, u32[]{:S(2)}, u32[]{:S(2)}) collective-permute-start(bf16[64,1280]{1,0:T(8,128)(2,1)S(1)} %collective-permute-done.12.refs_7_), channel_id=1, source_target_pairs={{0,1},{1,0},{2,3},{3,2},{4,5},{5,4},{6,7},{7,6},{8,9},{9,8},{10,11... | collective-permute-start | bytes 491528 | tf_op jit(solution)/shard_map/ppermute | solution.py:94
  47.5 8.7 %collective-permute-start.11 = (bf16[256,896]{1,0:T(8,128)(2,1)S(1)}, bf16[256,896]{1,0:T(8,128)(2,1)S(1)}, u32[]{:S(2)}, u32[]{:S(2)}) collective-permute-start(bf16[256,896]{1,0:T(8,128)(2,1)S(1)} %get-tuple-element.55), channel_id=1, source_target_pairs={{0,8},{1,9},{2,10},{3,11},{4,12},{5,13},{6,14},{7,15},{8,0},{9,1},... | collective-permute-start | bytes 1376264 | tf_op jit(solution)/shard_map/ppermute | solution.py:94
  49.1 4.3 %collective-permute-start.14 = (bf16[256,640]{1,0:T(8,128)(2,1)S(1)}, bf16[256,640]{1,0:T(8,128)(2,1)S(1)}, u32[]{:S(2)}, u32[]{:S(2)}) collective-permute-start(bf16[256,640]{1,0:T(8,128)(2,1)S(1)} %get-tuple-element.62), channel_id=1, source_target_pairs={{0,8},{1,9},{2,10},{3,11},{4,12},{5,13},{6,14},{7,15},{8,0},{9,1},... | collective-permute-start | bytes 983048 | tf_op jit(solution)/shard_map/ppermute | solution.py:94
  49.2 12.6 %collective-permute-start.17 = (bf16[256,128]{1,0:T(8,128)(2,1)S(1)}, bf16[256,128]{1,0:T(8,128)(2,1)S(1)}, u32[]{:S(2)}, u32[]{:S(2)}) collective-permute-start(bf16[256,128]{1,0:T(8,128)(2,1)S(1)} %get-tuple-element.70), channel_id=1, source_target_pairs={{0,2},{1,3},{2,0},{3,1},{4,6},{5,7},{6,4},{7,5},{8,10},{9,11},{10,... | collective-permute-start | bytes 196616 | tf_op jit(solution)/shard_map/ppermute | solution.py:94
  52.4 9.4 %collective-permute-start.18 = (bf16[256,128]{1,0:T(8,128)(2,1)S(1)}, bf16[256,128]{1,0:T(8,128)(2,1)S(1)}, u32[]{:S(2)}, u32[]{:S(2)}) collective-permute-start(bf16[256,128]{1,0:T(8,128)(2,1)S(1)} %get-tuple-element.71), channel_id=1, source_target_pairs={{0,18},{1,19},{2,16},{3,17},{4,22},{5,23},{6,20},{7,21},{8,26},{9,... | collective-permute-start | bytes 196616 | tf_op jit(solution)/shard_map/ppermute | solution.py:94
  54.2 7.5 %collective-permute-start.15 = (bf16[128,640]{1,0:T(8,128)(2,1)S(1)}, bf16[128,640]{1,0:T(8,128)(2,1)S(1)}, u32[]{:S(2)}, u32[]{:S(2)}) collective-permute-start(bf16[128,640]{1,0:T(8,128)(2,1)S(1)} %slice.48), channel_id=1, source_target_pairs={{0,2},{1,3},{2,0},{3,1},{4,6},{5,7},{6,4},{7,5},{8,10},{9,11},{10,... | collective-permute-start | bytes 491528 | tf_op jit(solution)/shard_map/ppermute | solution.py:94
  56.4 9.6 %collective-permute-start.19 = (bf16[128,896]{1,0:T(8,128)(2,1)S(1)}, bf16[128,896]{1,0:T(8,128)(2,1)S(1)}, u32[]{:S(2)}, u32[]{:S(2)}) collective-permute-start(bf16[128,896]{1,0:T(8,128)(2,1)S(1)} %slice.47), channel_id=1, source_target_pairs={{0,2},{1,3},{2,0},{3,1},{4,6},{5,7},{6,4},{7,5},{8,10},{9,11},{10,... | collective-permute-start | bytes 688136 | tf_op jit(solution)/shard_map/ppermute | solution.py:94
  56.5 5.3 %collective-permute-start.16 = (bf16[256,128]{1,0:T(8,128)(2,1)S(1)}, bf16[256,128]{1,0:T(8,128)(2,1)S(1)}, u32[]{:S(2)}, u32[]{:S(2)}) collective-permute-start(bf16[256,128]{1,0:T(8,128)(2,1)S(1)} %get-tuple-element.68), channel_id=1, source_target_pairs={{0,16},{1,17},{2,18},{3,19},{4,20},{5,21},{6,22},{7,23},{8,24},{9,... | collective-permute-start | bytes 196616 | tf_op jit(solution)/shard_map/ppermute | solution.py:94
  61.8 1.5 %slice-start = ((f32[256,640]{1,0:T(8,128)}), f32[128,640]{1,0:T(8,128)S(1)}, s32[]{:S(2)}) async-start(f32[256,640]{1,0:T(8,128)} %copy-done.4), calls=%async_computation | async-start | bytes 655360 | tf_op jit(solution)/shard_map/slice | solution.py:350
  (3 other events, 3.0 us)

commit v8 on v7

--- a/solution.py
+++ b/solution.py
@@ -13,7 +13,7 @@
 ANY = pl.BlockSpec(memory_space=pl.ANY)
 VMEM = pl.BlockSpec(memory_space=pltpu.VMEM)
 F32 = jnp.float32
-SMALL, LARGE, LAST = 50000000000, 1000000000, 1000000000
+SMALL, LARGE, LAST = 1, 50000000000, 20000000000
 BF16 = jnp.bfloat16
 
 
@@ -142,8 +142,9 @@
     return lax.dot_general(a, b, ((over[0], over[1]), ((), ())), preferred_element_type=F32)
 
 
-def forward_kernel(q, k, v, probs, mine, others, held):
+def forward_kernel(q, k, v, w, probs, mine, bundle, held):
     z0 = place()["z0"]
+    bundle[:, : w.shape[1]] = w[...]
     half = PATCH // 2
     for i in range(q.shape[0] // PATCH):
         rows = pl.ds(i * PATCH, PATCH)
@@ -154,18 +155,21 @@
         probs[i] = attention
         held[...] = dot(attention.astype(BF16), v[rows], ((0,), (0,))).astype(BF16)
         mine[pl.ds(i * half, half)] = held[pl.ds(aligned(z0, half), half)]
-        others[pl.ds(i * half, half)] = held[pl.ds(aligned(1 - z0, half), half)]
-
-
-def forward(q, k, v):
+        bundle[:, w.shape[1] + i * HD : w.shape[1] + (i + 1) * HD] = held[
+            pl.ds(aligned(1 - z0, half), half)
+        ]
+
+
+def forward(q, k, v, w):
     images = q.shape[0] // PATCH
-    half = ((q.shape[0] // 2, HD), BF16)
-    outs = [((images, PATCH, PATCH), F32), half, half]
-    return call("forward", forward_kernel, outs, [q, k, v], SMALL, [pltpu.VMEM((PATCH, HD), BF16)])
-
-
-def backward_kernel(at, q, k, v, probs, own, from_x, from_z, from_xz, gq, gk, gv, held):
-    del at
+    outs = [((images, PATCH, PATCH), F32), ((q.shape[0] // 2, HD), BF16)]
+    outs.append(((HD, w.shape[1] + images * HD), BF16))
+    scratch = [pltpu.VMEM((PATCH, HD), BF16)]
+    return call("forward", forward_kernel, outs, [q, k, v, w], SMALL, scratch)
+
+
+def backward_kernel(at, q, k, v, probs, own, from_x, from_z, from_xz, gq, gk, gv, end, held):
+    end[...] = at[...]
     z0 = place()["z0"]
     half = PATCH // 2
     mine = (own[...] + from_x[...].astype(F32)).astype(BF16)
@@ -188,34 +192,34 @@
     images = q.shape[0] // PATCH
     ins = [at, q, k, v, probs, own, from_x, from_z, from_xz]
     scratch = [pltpu.VMEM((images, PATCH, HD), BF16)]
-    return call("backward", backward_kernel, [(q.shape, BF16)] * 3, ins, LAST, scratch)
+    outs = [(q.shape, BF16)] * 3 + [(at.shape, at.dtype)]
+    return call("backward", backward_kernel, outs, ins, LAST, scratch)
 
 
 def products_kernel(low, high, first, last, places, *refs):
     refs = list(refs[1:])
     arrays = [refs.pop(0) for _ in range(1 + max(array for array, _ in places))]
     blocks = [(arrays[array], row) for array, row in places]
-    w_refs = [refs.pop(0) for _ in range(2)]
-    att = [refs.pop(0) for _ in range(2)]
+    w_refs = [refs.pop(0) for _ in range(4)]
+    mine, att_x = refs.pop(0), refs.pop(0)
+    pairs = w_refs[1]
     before = None if first else refs.pop(0)
     keep, give = refs.pop(0), refs.pop(0)
     d_refs = refs
     at = place()
+    whole = w_refs[0].shape[1]
     width = high - low
     tiles = [(start, min(512, width - start)) for start in range(0, width, 512)]
-    rows = []
+    rows, parts = [], []
     for n in range(4):
         z1 = 1 - at["z1"] if n // 2 else at["z1"]
         y = 1 - at["y"] if n % 2 else at["y"]
         rows.append(pl.multiple_of(z1 * 128 + y * 64, 64))
-    attended = jnp.concatenate(
-        [
-            jnp.concatenate([att[g][pl.ds(row, 64)], att[g][pl.ds(256 + row, 64)]], axis=1)
-            for g in range(2)
-            for row in rows
-        ],
-        axis=0,
-    )
+        spot = pl.ds(aligned(y, 64), 64), pl.ds(pl.multiple_of(whole + z1 * HD, HD), HD)
+        parts.append([mine[pl.ds(rows[n], 64)], pairs[spot]])
+    for row in rows:
+        parts.append([att_x[pl.ds(row, 64)], att_x[pl.ds(256 + row, 64)]])
+    attended = jnp.concatenate([jnp.concatenate(both, axis=1) for both in parts], axis=0)
     turned = attended.T
     d = None if first else before[...]
     for other in (1, 0):
@@ -235,7 +239,10 @@
                 give[:, start : start + tile] = share.astype(BF16)
             else:
                 keep[:, start : start + tile] = share
-            part = dot(cot, w_refs[other][:, low + start : low + start + tile], ((1,), (1,)))
+            w = jnp.concatenate(
+                [ref[:, low + start : low + start + tile] for ref in w_refs[2 * other :][:2]], axis=0
+            )
+            part = dot(cot, w, ((1,), (1,)))
             d = part if d is None else d + part
     if not last:
         d_refs[0][...] = d
@@ -275,6 +282,19 @@
     return call("fence", fence_kernel, [(token.shape, token.dtype)], [token], cost)[0]
 
 
+def finish_kernel(limits, *refs):
+    out = refs[-1]
+    for n, (low, high) in enumerate(limits):
+        total, pair = refs[1 + 2 * n], refs[2 + 2 * n]
+        out[:, low:high] = (total[:HD] + pair[...].astype(F32)).astype(BF16)
+
+
+def finish(token, limits, totals, pairs):
+    ins = [token, *(ref for both in zip(totals, pairs) for ref in both)]
+    outs = [((HD, limits[-1][1]), BF16)]
+    return call("finish", functools.partial(finish_kernel, limits), outs, ins, LAST)[0]
+
+
 def after(value, *others):
     return lax.optimization_barrier((value, *others))[0]
 
@@ -295,65 +315,58 @@
     return lax.optimization_barrier((value, *others))[0]
 
 
-CUTS = ((0, 896), (896, 1536))
+CUTS = ((0, 1024), (1024, 1536))
 
 
 def on_device_4x8(queries, keys, values, w_out, cotangent):
     m, o, token = pack(cotangent, ((0, CUTS[-1][1]),))
-    at0 = fence(token, cost=1)
-    at1 = fence(at0, cost=10**10)
     za = send(m, z1=1)
-    probs, mine, others = forward(queries, keys, values)
     ya = send(m, y=1)
-    att_z = send(after(others, ya), z0=1)
-    att = two(mine, att_z)
-    att_x = send(after(att, ya), x=1)
+    sa = send(after(za, ya), y=1)
+    at0 = fence(token, sa, cost=20000000000)
+    probs, mine, bundle = forward(queries, keys, values, w_out)
+    pair_w = send(after(bundle, ya), z0=1)
+    core_w = send(after(w_out, pair_w), c=1)
     x = send(o, x=1)
-    at2 = fence(at1, za, att_x, x, cost=10**10)
-    at3 = fence(at2, cost=10**10)
-    w_z = send(after(w_out, x, ya), z0=1)
-    w_c = send(after(two(w_out, w_z), w_z), c=1)
-    at4 = fence(at3, w_c, cost=2 * 10**10)
-    att_all = [att, att_x]
-    own_x = after(att_all[0], za)
-    sa = send(after(za, att_x, ya), y=1)
-    yx = send(x, y=1)
     x1, x2 = cut(x, CUTS)
     zb1 = send(x1, z1=1)
-    sb1 = send(zb1, y=1)
-    w_own = two(w_out, w_z)
-    w_all = [w_own, w_c]
+    sb1 = send(after(zb1, zb1), y=1)
+    at1 = fence(at0, core_w, sb1, cost=1)
+    whole = w_out.shape[1]
+    att = jnp.concatenate([mine, pair_w[:, whole : whole + HD], pair_w[:, whole + HD :]])
+    att_x = send(att, x=1)
+    own = mine
+    yx = send(x, y=1)
+    core_pair_w = send(after(pair_w, za), c=1)
+    w_all = [w_out, pair_w, core_w, core_pair_w]
     blocks = [(m, 0), (ya, 0), (za, 0), (sa, 0), (x, 0), (yx, 0), (zb1, 0), (sb1, 0)]
     keep1, give1, d = products(
-        CUTS[0], blocks, w_all, [own_x, att_all[1]], token, None, False
-    )
-    got1 = send(after(give1, give1, att_z), c=1)
-    at5 = fence(at4, att_x, got1, cost=10**10)
-    own_x = after(att_all[0], give1)
-    zb2 = send(after(x2, at2, za, att_z), z1=1)
-    sb2 = send(after(zb2, at3), y=1)
+        CUTS[0], blocks, w_all, [own, att_x], token, None, False
+    )
+    got1 = send(after(give1, att_x, zb1), c=1)
+    total1 = keep1 + got1.astype(F32)
+    to_pair1 = total1[HD:].astype(BF16)
+    pair1 = send(to_pair1, z0=1)
+    queries = after(queries, at1, pair1)
+    own = mine
+    zb2 = send(after(x2, yx), z1=1)
+    sb2 = send(zb2, y=1)
     blocks = [(m, 0), (ya, 0), (za, 0), (sa, 0), (x, 0), (yx, 0), (zb2, 0), (sb2, 0)]
-    keep2, give2, own, to_x, to_z, to_xz = products(
-        CUTS[1], blocks, w_all, [own_x, att_all[1]], token, d, True
-    )
-    got2 = send(give2, c=1)
+    keep2, give2, d, to_x, to_z, to_xz = products(
+        CUTS[1], blocks, w_all, [own, att_x], token, d, True
+    )
+    from_x = send(after(to_x, at1), x=1)
+    from_z = send(after(to_z, give1), z0=1)
+    from_xz = send(to_xz, x=1, z0=1)
+    *grads, end = backward(
+        at1, queries, keys, values, probs, d, from_x, from_z, from_xz
+    )
+    got2 = send(after(give2, to_pair1), c=1)
     total2 = keep2 + got2.astype(F32)
     to_pair2 = total2[HD:].astype(BF16)
-    pair2 = send(after(to_pair2, at2), z0=1)
-    queries = after(queries, pair2, at3)
-    from_x = send(after(to_x, at0, got1), x=1)
-    from_z = send(after(to_z, at1), z0=1)
-    from_xz = send(to_xz, x=1, z0=1)
-    grads = backward(at5, queries, keys, values, probs, own, from_x, from_z, from_xz)
-    total1 = keep1 + got1.astype(F32)
-    rest1 = total1[:HD]
-    rest2 = total2[:HD]
-    rest2 = after(rest2, grads[0])
-    to_pair1 = total1[HD:].astype(BF16)
-    pair1 = send(after(to_pair1, at1), z0=1)
-    part1 = (rest1 + pair1.astype(F32)).astype(BF16)
-    part2 = (rest2 + pair2.astype(F32)).astype(BF16)
-    return *grads, jnp.concatenate([part1, part2], axis=1)
+    pair2 = send(to_pair2, z0=1)
+    totals, pairs = [total1, total2], [pair1, pair2]
+    return *grads, finish(token, CUTS, totals, pairs)
 
 
 def solution(mesh):

time: 67 us -> 66.3 us (0.990)
  the two profiles are of different devices: /device:TPU:20 before, /device:TPU:0 now
where the time goes in v8:
time: 66.3 us; the launch traced here: 66.1 us
  waiting for transfers between devices  34.6 us (52%)
  starting transfers between devices  23.9 us (36%)
  Pallas kernels  5.38 us (8%)
  local copies, waits for them, and re-layouts  1.23 us (2%)
  between operations  0.82 us (1%)
    ppermute x20, waiting for transfers between devices, send(): return lax.ppermute(value, AXES, flip(**bits))  34.6 us
    ppermute x20, starting transfers between devices, send(): return lax.ppermute(value, AXES, flip(**bits))  23.9 us
    pallas_call x8, Pallas kernels, call(): pl.pallas_call(kernel, out_shape=[jax.ShapeDtypeStruct(shape, kind) for s...  5.38 us
  transfers between devices with their start and end apart: 20, of which 9 were waited for; matrix products, arithmetic and copies ran while one was open for 0% of the time, Pallas kernels for 7%

profile of v8, /device:TPU:0, one launch (start us, length us, event | category | flops | bytes accessed | tf_op | source)
XLA Modules:
  0.0 66.1 jit_solution(987774147661042430)
XLA Ops:
  0.6 1.1 %copy-done = bf16[64,6144]{1,0:T(8,128)(2,1)S(1)} copy-done((bf16[64,6144]{1,0:T(8,128)(2,1)S(1)}, bf16[64,6144]{1,0:T(8,128)(2,1)}, u32[]{:S(2)}) %copy-start) | copy-done | bytes 786456
  1.9 3.0 %collective-permute-start.1 = (bf16[64,3072]{1,0:T(8,128)(2,1)S(1)}, bf16[64,3072]{1,0:T(8,128)(2,1)S(1)}, u32[]{:S(2)}, u32[]{:S(2)}) collective-permute-start(bf16[64,3072]{1,0:T(8,128)(2,1)S(1)} %get-tuple-element.36.refs_1_), channel_id=1, source_target_pairs={{0,1},{1,0},{2,3},{3,2},{4,5},{5,4},{6,7},{7,6},{8,9},{9,8},{10,11... | collective-permute-start | bytes 1179656 | tf_op jit(solution)/shard_map/ppermute | solution.py:94
  4.9 1.5 %collective-permute-start.5 = (bf16[64,3072]{1,0:T(8,128)(2,1)S(1)}, bf16[64,3072]{1,0:T(8,128)(2,1)S(1)}, u32[]{:S(2)}, u32[]{:S(2)}) collective-permute-start(bf16[64,3072]{1,0:T(8,128)(2,1)S(1)} %get-tuple-element.42), channel_id=1, source_target_pairs={{0,16},{1,17},{2,18},{3,19},{4,20},{5,21},{6,22},{7,23},{8,24},{9,... | collective-permute-start | bytes 1179656 | tf_op jit(solution)/shard_map/ppermute | solution.py:94
  6.4 2.6 %collective-permute-start = (bf16[64,3072]{1,0:T(8,128)(2,1)S(1)}, bf16[64,3072]{1,0:T(8,128)(2,1)S(1)}, u32[]{:S(2)}, u32[]{:S(2)}) collective-permute-start(bf16[64,3072]{1,0:T(8,128)(2,1)S(1)} %get-tuple-element.36.refs_1_), channel_id=1, source_target_pairs={{0,4},{1,5},{2,6},{3,7},{4,0},{5,1},{6,2},{7,3},{8,12},{9,13},{10,... | collective-permute-start | bytes 1179656 | tf_op jit(solution)/shard_map/ppermute | solution.py:94
  9.0 0.9 %forward.1 = (f32[2,256,256]{2,1,0:T(8,128)S(1)}, bf16[256,128]{1,0:T(8,128)(2,1)S(1)}, bf16[128,1792]{1,0:T(8,128)(2,1)S(1)}) custom-call(bf16[512,128]{1,0:T(8,128)(2,1)S(1)} %copy-done.2, bf16[512,128]{1,0:T(8,128)(2,1)S(1)} %copy-done.3, bf16[512,128]{1,0:T(8,128)(2,1)S(1)} %copy-done.4, bf16[128,1536]{1,0:T(8,128)(2,1)S(1)} %copy-done.1), custom_call_target="tpu_custom_call" | custom-call | flops 1 | bytes 1048576 | tf_op jit(solution)/shard_map/forward/pallas_call | solution.py:107
  9.9 4.1 %collective-permute-done.1.refs_2_ = bf16[64,3072]{1,0:T(8,128)(2,1)S(1)} collective-permute-done((bf16[64,3072]{1,0:T(8,128)(2,1)S(1)}, bf16[64,3072]{1,0:T(8,128)(2,1)S(1)}, u32[]{:S(2)}, u32[]{:S(2)}) %collective-permute-start.1) | collective-permute-done | bytes 393248 | tf_op jit(solution)/shard_map/ppermute | solution.py:94
  14.0 1.8 %collective-permute-start.3 = (bf16[128,1792]{1,0:T(8,128)(2,1)S(1)}, bf16[128,1792]{1,0:T(8,128)(2,1)S(1)}, u32[]{:S(2)}, u32[]{:S(2)}) collective-permute-start(bf16[128,1792]{1,0:T(8,128)(2,1)S(1)} %get-tuple-element.40), channel_id=1, source_target_pairs={{0,2},{1,3},{2,0},{3,1},{4,6},{5,7},{6,4},{7,5},{8,10},{9,11},{10,... | collective-permute-start | bytes 1376264 | tf_op jit(solution)/shard_map/ppermute | solution.py:94
  15.8 1.5 %collective-permute-start.8 = (bf16[64,3072]{1,0:T(8,128)(2,1)S(1)}, bf16[64,3072]{1,0:T(8,128)(2,1)S(1)}, u32[]{:S(2)}, u32[]{:S(2)}) collective-permute-start(bf16[64,3072]{1,0:T(8,128)(2,1)S(1)} %collective-permute-done.5.refs_5_), channel_id=1, source_target_pairs={{0,1},{1,0},{2,3},{3,2},{4,5},{5,4},{6,7},{7,6},{8,9},{9,8},{10,11... | collective-permute-start | bytes 1179656 | tf_op jit(solution)/shard_map/ppermute | solution.py:94
  17.4 2.7 %collective-permute-start.6 = (bf16[64,2048]{1,0:T(8,128)(2,1)S(1)}, bf16[64,2048]{1,0:T(8,128)(2,1)S(1)}, u32[]{:S(2)}, u32[]{:S(2)}) collective-permute-start(bf16[64,2048]{1,0:T(8,128)(2,1)S(1)} %pad_maximum_fusion), channel_id=1, source_target_pairs={{0,4},{1,5},{2,6},{3,7},{4,0},{5,1},{6,2},{7,3},{8,12},{9,13},{10,... | collective-permute-start | bytes 786440 | tf_op jit(solution)/shard_map/ppermute | solution.py:94
  20.0 7.2 %collective-permute-done.refs_3_ = bf16[64,3072]{1,0:T(8,128)(2,1)S(1)} collective-permute-done((bf16[64,3072]{1,0:T(8,128)(2,1)S(1)}, bf16[64,3072]{1,0:T(8,128)(2,1)S(1)}, u32[]{:S(2)}, u32[]{:S(2)}) %collective-permute-start) | collective-permute-done | bytes 393248 | tf_op jit(solution)/shard_map/ppermute | solution.py:94
  27.3 1.1 %collective-permute-start.2 = (bf16[64,3072]{1,0:T(8,128)(2,1)S(1)}, bf16[64,3072]{1,0:T(8,128)(2,1)S(1)}, u32[]{:S(2)}, u32[]{:S(2)}) collective-permute-start(bf16[64,3072]{1,0:T(8,128)(2,1)S(1)} %collective-permute-done.refs_3_), channel_id=1, source_target_pairs={{0,1},{1,0},{2,3},{3,2},{4,5},{5,4},{6,7},{7,6},{8,9},{9,8},{10,11... | collective-permute-start | bytes 1179656 | tf_op jit(solution)/shard_map/ppermute | solution.py:94
  28.4 9.0 %collective-permute-done.6.refs_7_ = bf16[64,2048]{1,0:T(8,128)(2,1)S(1)} collective-permute-done((bf16[64,2048]{1,0:T(8,128)(2,1)S(1)}, bf16[64,2048]{1,0:T(8,128)(2,1)S(1)}, u32[]{:S(2)}, u32[]{:S(2)}) %collective-permute-start.6) | collective-permute-done | bytes 262176 | tf_op jit(solution)/shard_map/ppermute | solution.py:94
  39.2 1.5 %collective-permute-start.10 = (bf16[512,128]{1,0:T(8,128)(2,1)S(1)}, bf16[512,128]{1,0:T(8,128)(2,1)S(1)}, u32[]{:S(2)}, u32[]{:S(2)}) collective-permute-start(bf16[512,128]{1,0:T(8,128)(2,1)S(1)} %pad_maximum_fusion.1), channel_id=1, source_target_pairs={{0,16},{1,17},{2,18},{3,19},{4,20},{5,21},{6,22},{7,23},{8,24},{9,... | collective-permute-start | bytes 393224 | tf_op jit(solution)/shard_map/ppermute | solution.py:94
  40.6 5.5 %collective-permute-done.13.refs_7_ = bf16[64,1024]{1,0:T(8,128)(2,1)S(1)} collective-permute-done((bf16[64,1024]{1,0:T(8,128)(2,1)S(1)}, bf16[64,1024]{1,0:T(8,128)(2,1)S(1)}, u32[]{:S(2)}, u32[]{:S(2)}) %collective-permute-start.13) | collective-permute-done | bytes 131104 | tf_op jit(solution)/shard_map/ppermute | solution.py:94
  46.1 1.5 %collective-permute-start.14 = (bf16[64,1024]{1,0:T(8,128)(2,1)S(1)}, bf16[64,1024]{1,0:T(8,128)(2,1)S(1)}, u32[]{:S(2)}, u32[]{:S(2)}) collective-permute-start(bf16[64,1024]{1,0:T(8,128)(2,1)S(1)} %collective-permute-done.13.refs_7_), channel_id=1, source_target_pairs={{0,1},{1,0},{2,3},{3,2},{4,5},{5,4},{6,7},{7,6},{8,9},{9,8},{10,11... | collective-permute-start | bytes 393224 | tf_op jit(solution)/shard_map/ppermute | solution.py:94
  47.7 1.3 %products.2 = (f32[256,1024]{1,0:T(8,128)S(1)}, bf16[256,1024]{1,0:T(8,128)(2,1)S(1)}, f32[512,256]{1,0:T(8,128)S(1)}) custom-call(f32[8,128]{1,0:T(8,128)S(1)} %get-tuple-element.38.token.refs_0_, bf16[64,3072]{1,0:T(8,128)(2,1)S(1)} %get-tuple-element.36.refs_1_, bf16[64,3072]{1,0:T(8,128)(2,1)S(1)} %collective-permute-done.1.refs_2_, ...), custom_call_target="tpu_custom_call" | custom-call | flops 49999998976 | bytes 1048576 | tf_op jit(solution)/shard_map/products/pallas_call | solution.py:107
  49.1 2.0 %collective-permute-done.14.refs_8_ = bf16[64,1024]{1,0:T(8,128)(2,1)S(1)} collective-permute-done((bf16[64,1024]{1,0:T(8,128)(2,1)S(1)}, bf16[64,1024]{1,0:T(8,128)(2,1)S(1)}, u32[]{:S(2)}, u32[]{:S(2)}) %collective-permute-start.14) | collective-permute-done | bytes 131104 | tf_op jit(solution)/shard_map/ppermute | solution.py:94
  52.3 1.9 %collective-permute-start.16 = (bf16[256,128]{1,0:T(8,128)(2,1)S(1)}, bf16[256,128]{1,0:T(8,128)(2,1)S(1)}, u32[]{:S(2)}, u32[]{:S(2)}) collective-permute-start(bf16[256,128]{1,0:T(8,128)(2,1)S(1)} %get-tuple-element.58), channel_id=1, source_target_pairs={{0,2},{1,3},{2,0},{3,1},{4,6},{5,7},{6,4},{7,5},{8,10},{9,11},{10,... | collective-permute-start | bytes 196616 | tf_op jit(solution)/shard_map/ppermute | solution.py:94
  54.7 1.1 %collective-permute-start.17 = (bf16[256,128]{1,0:T(8,128)(2,1)S(1)}, bf16[256,128]{1,0:T(8,128)(2,1)S(1)}, u32[]{:S(2)}, u32[]{:S(2)}) collective-permute-start(bf16[256,128]{1,0:T(8,128)(2,1)S(1)} %get-tuple-element.59), channel_id=1, source_target_pairs={{0,18},{1,19},{2,16},{3,17},{4,22},{5,23},{6,20},{7,21},{8,26},{9,... | collective-permute-start | bytes 196616 | tf_op jit(solution)/shard_map/ppermute | solution.py:94
  55.9 1.9 %collective-permute-start.19 = (bf16[128,512]{1,0:T(8,128)(2,1)S(1)}, bf16[128,512]{1,0:T(8,128)(2,1)S(1)}, u32[]{:S(2)}, u32[]{:S(2)}) collective-permute-start(bf16[128,512]{1,0:T(8,128)(2,1)S(1)} %slice.45), channel_id=1, source_target_pairs={{0,2},{1,3},{2,0},{3,1},{4,6},{5,7},{6,4},{7,5},{8,10},{9,11},{10,... | collective-permute-start | bytes 393224 | tf_op jit(solution)/shard_map/ppermute | solution.py:94
  57.8 3.5 %collective-permute-done.12.refs_2_ = bf16[128,1024]{1,0:T(8,128)(2,1)S(1)} collective-permute-done((bf16[128,1024]{1,0:T(8,128)(2,1)S(1)}, bf16[128,1024]{1,0:T(8,128)(2,1)S(1)}, u32[]{:S(2)}, u32[]{:S(2)}) %collective-permute-start.12) | collective-permute-done | bytes 262176 | tf_op jit(solution)/shard_map/ppermute | solution.py:94
  61.4 1.4 %collective-permute-done.16.from_z = bf16[256,128]{1,0:T(8,128)(2,1)S(1)} collective-permute-done((bf16[256,128]{1,0:T(8,128)(2,1)S(1)}, bf16[256,128]{1,0:T(8,128)(2,1)S(1)}, u32[]{:S(2)}, u32[]{:S(2)}) %collective-permute-start.16) | collective-permute-done | bytes 65568 | tf_op jit(solution)/shard_map/ppermute | solution.py:94
  62.8 1.0 %collective-permute-done.17.from_xz = bf16[256,128]{1,0:T(8,128)(2,1)S(1)} collective-permute-done((bf16[256,128]{1,0:T(8,128)(2,1)S(1)}, bf16[256,128]{1,0:T(8,128)(2,1)S(1)}, u32[]{:S(2)}, u32[]{:S(2)}) %collective-permute-start.17) | collective-permute-done | bytes 65568 | tf_op jit(solution)/shard_map/ppermute | solution.py:94
  63.8 1.5 %backward.1 = (bf16[512,128]{1,0:T(8,128)(2,1)}, bf16[512,128]{1,0:T(8,128)(2,1)}, bf16[512,128]{1,0:T(8,128)(2,1)}, f32[8,128]{1,0:T(8,128)}) custom-call(f32[8,128]{1,0:T(8,128)S(1)} %fence.3.at, bf16[512,128]{1,0:T(8,128)(2,1)S(1)} %copy-done.2, bf16[512,128]{1,0:T(8,128)(2,1)S(1)} %copy-done.3, bf16[512,128]{1,0:T(8,128)(2,1)S(1)} %copy-done.4, ...), custom_call_target="tpu_custom_call" | custom-call | flops 20000000000 | bytes 1048576 | tf_op jit(solution)/shard_map/backward/pallas_call | solution.py:107
  (44 shorter events, 4.6 us)
Async XLA Ops:
  1.8 7.2 %copy-start.1 = (bf16[128,1536]{1,0:T(8,128)(2,1)S(1)}, bf16[128,1536]{1,0:T(8,128)(2,1)}, u32[]{:S(2)}) copy-start(bf16[128,1536]{1,0:T(8,128)(2,1)} %refs_9_.3) | copy-start | bytes 1179652
  1.8 7.2 %copy-start.2 = (bf16[512,128]{1,0:T(8,128)(2,1)S(1)}, bf16[512,128]{1,0:T(8,128)(2,1)}, u32[]{:S(2)}) copy-start(bf16[512,128]{1,0:T(8,128)(2,1)} %q.2) | copy-start | bytes 393220
  1.8 7.2 %copy-start.3 = (bf16[512,128]{1,0:T(8,128)(2,1)S(1)}, bf16[512,128]{1,0:T(8,128)(2,1)}, u32[]{:S(2)}) copy-start(bf16[512,128]{1,0:T(8,128)(2,1)} %k.3) | copy-start | bytes 393220
  1.8 7.2 %copy-start.4 = (bf16[512,128]{1,0:T(8,128)(2,1)S(1)}, bf16[512,128]{1,0:T(8,128)(2,1)}, u32[]{:S(2)}) copy-start(bf16[512,128]{1,0:T(8,128)(2,1)} %v.3) | copy-start | bytes 393220
  1.9 12.1 %collective-permute-start.1 = (bf16[64,3072]{1,0:T(8,128)(2,1)S(1)}, bf16[64,3072]{1,0:T(8,128)(2,1)S(1)}, u32[]{:S(2)}, u32[]{:S(2)}) collective-permute-start(bf16[64,3072]{1,0:T(8,128)(2,1)S(1)} %get-tuple-element.36.refs_1_), channel_id=1, source_target_pairs={{0,1},{1,0},{2,3},{3,2},{4,5},{5,4},{6,7},{7,6},{8,9},{9,8},{10,11... | collective-permute-start | bytes 1179656 | tf_op jit(solution)/shard_map/ppermute | solution.py:94
  4.9 10.9 %collective-permute-start.5 = (bf16[64,3072]{1,0:T(8,128)(2,1)S(1)}, bf16[64,3072]{1,0:T(8,128)(2,1)S(1)}, u32[]{:S(2)}, u32[]{:S(2)}) collective-permute-start(bf16[64,3072]{1,0:T(8,128)(2,1)S(1)} %get-tuple-element.42), channel_id=1, source_target_pairs={{0,16},{1,17},{2,18},{3,19},{4,20},{5,21},{6,22},{7,23},{8,24},{9,... | collective-permute-start | bytes 1179656 | tf_op jit(solution)/shard_map/ppermute | solution.py:94
  6.4 20.9 %collective-permute-start = (bf16[64,3072]{1,0:T(8,128)(2,1)S(1)}, bf16[64,3072]{1,0:T(8,128)(2,1)S(1)}, u32[]{:S(2)}, u32[]{:S(2)}) collective-permute-start(bf16[64,3072]{1,0:T(8,128)(2,1)S(1)} %get-tuple-element.36.refs_1_), channel_id=1, source_target_pairs={{0,4},{1,5},{2,6},{3,7},{4,0},{5,1},{6,2},{7,3},{8,12},{9,13},{10,... | collective-permute-start | bytes 1179656 | tf_op jit(solution)/shard_map/ppermute | solution.py:94
  14.0 24.6 %collective-permute-start.3 = (bf16[128,1792]{1,0:T(8,128)(2,1)S(1)}, bf16[128,1792]{1,0:T(8,128)(2,1)S(1)}, u32[]{:S(2)}, u32[]{:S(2)}) collective-permute-start(bf16[128,1792]{1,0:T(8,128)(2,1)S(1)} %get-tuple-element.40), channel_id=1, source_target_pairs={{0,2},{1,3},{2,0},{3,1},{4,6},{5,7},{6,4},{7,5},{8,10},{9,11},{10,... | collective-permute-start | bytes 1376264 | tf_op jit(solution)/shard_map/ppermute | solution.py:94
  15.8 22.1 %collective-permute-start.8 = (bf16[64,3072]{1,0:T(8,128)(2,1)S(1)}, bf16[64,3072]{1,0:T(8,128)(2,1)S(1)}, u32[]{:S(2)}, u32[]{:S(2)}) collective-permute-start(bf16[64,3072]{1,0:T(8,128)(2,1)S(1)} %collective-permute-done.5.refs_5_), channel_id=1, source_target_pairs={{0,1},{1,0},{2,3},{3,2},{4,5},{5,4},{6,7},{7,6},{8,9},{9,8},{10,11... | collective-permute-start | bytes 1179656 | tf_op jit(solution)/shard_map/ppermute | solution.py:94
  17.4 20.0 %collective-permute-start.6 = (bf16[64,2048]{1,0:T(8,128)(2,1)S(1)}, bf16[64,2048]{1,0:T(8,128)(2,1)S(1)}, u32[]{:S(2)}, u32[]{:S(2)}) collective-permute-start(bf16[64,2048]{1,0:T(8,128)(2,1)S(1)} %pad_maximum_fusion), channel_id=1, source_target_pairs={{0,4},{1,5},{2,6},{3,7},{4,0},{5,1},{6,2},{7,3},{8,12},{9,13},{10,... | collective-permute-start | bytes 786440 | tf_op jit(solution)/shard_map/ppermute | solution.py:94
  27.3 11.9 %collective-permute-start.2 = (bf16[64,3072]{1,0:T(8,128)(2,1)S(1)}, bf16[64,3072]{1,0:T(8,128)(2,1)S(1)}, u32[]{:S(2)}, u32[]{:S(2)}) collective-permute-start(bf16[64,3072]{1,0:T(8,128)(2,1)S(1)} %collective-permute-done.refs_3_), channel_id=1, source_target_pairs={{0,1},{1,0},{2,3},{3,2},{4,5},{5,4},{6,7},{7,6},{8,9},{9,8},{10,11... | collective-permute-start | bytes 1179656 | tf_op jit(solution)/shard_map/ppermute | solution.py:94
  37.4 10.3 %collective-permute-start.7 = (bf16[64,2048]{1,0:T(8,128)(2,1)S(1)}, bf16[64,2048]{1,0:T(8,128)(2,1)S(1)}, u32[]{:S(2)}, u32[]{:S(2)}) collective-permute-start(bf16[64,2048]{1,0:T(8,128)(2,1)S(1)} %collective-permute-done.6.refs_7_), channel_id=1, source_target_pairs={{0,1},{1,0},{2,3},{3,2},{4,5},{5,4},{6,7},{7,6},{8,9},{9,8},{10,11... | collective-permute-start | bytes 786440 | tf_op jit(solution)/shard_map/ppermute | solution.py:94
  37.9 8.2 %collective-permute-start.13 = (bf16[64,1024]{1,0:T(8,128)(2,1)S(1)}, bf16[64,1024]{1,0:T(8,128)(2,1)S(1)}, u32[]{:S(2)}, u32[]{:S(2)}) collective-permute-start(bf16[64,1024]{1,0:T(8,128)(2,1)S(1)} %pad_maximum_fusion.2), channel_id=1, source_target_pairs={{0,4},{1,5},{2,6},{3,7},{4,0},{5,1},{6,2},{7,3},{8,12},{9,13},{10,... | collective-permute-start | bytes 393224 | tf_op jit(solution)/shard_map/ppermute | solution.py:94
  38.6 9.0 %collective-permute-start.4 = (bf16[128,1536]{1,0:T(8,128)(2,1)S(1)}, bf16[128,1536]{1,0:T(8,128)(2,1)S(1)}, u32[]{:S(2)}, u32[]{:S(2)}) collective-permute-start(bf16[128,1536]{1,0:T(8,128)(2,1)S(1)} %copy-done.1), channel_id=1, source_target_pairs={{0,8},{1,9},{2,10},{3,11},{4,12},{5,13},{6,14},{7,15},{8,0},{9,1},... | collective-permute-start | bytes 1179656 | tf_op jit(solution)/shard_map/ppermute | solution.py:94
  38.6 9.0 %collective-permute-start.9 = (bf16[128,1792]{1,0:T(8,128)(2,1)S(1)}, bf16[128,1792]{1,0:T(8,128)(2,1)S(1)}, u32[]{:S(2)}, u32[]{:S(2)}) collective-permute-start(bf16[128,1792]{1,0:T(8,128)(2,1)S(1)} %collective-permute-done.3.refs_10_), channel_id=1, source_target_pairs={{0,8},{1,9},{2,10},{3,11},{4,12},{5,13},{6,14},{7,15},{8,0},{9,1},... | collective-permute-start | bytes 1376264 | tf_op jit(solution)/shard_map/ppermute | solution.py:94
  39.2 8.5 %collective-permute-start.10 = (bf16[512,128]{1,0:T(8,128)(2,1)S(1)}, bf16[512,128]{1,0:T(8,128)(2,1)S(1)}, u32[]{:S(2)}, u32[]{:S(2)}) collective-permute-start(bf16[512,128]{1,0:T(8,128)(2,1)S(1)} %pad_maximum_fusion.1), channel_id=1, source_target_pairs={{0,16},{1,17},{2,18},{3,19},{4,20},{5,21},{6,22},{7,23},{8,24},{9,... | collective-permute-start | bytes 393224 | tf_op jit(solution)/shard_map/ppermute | solution.py:94
  46.1 5.0 %collective-permute-start.14 = (bf16[64,1024]{1,0:T(8,128)(2,1)S(1)}, bf16[64,1024]{1,0:T(8,128)(2,1)S(1)}, u32[]{:S(2)}, u32[]{:S(2)}) collective-permute-start(bf16[64,1024]{1,0:T(8,128)(2,1)S(1)} %collective-permute-done.13.refs_7_), channel_id=1, source_target_pairs={{0,1},{1,0},{2,3},{3,2},{4,5},{5,4},{6,7},{7,6},{8,9},{9,8},{10,11... | collective-permute-start | bytes 393224 | tf_op jit(solution)/shard_map/ppermute | solution.py:94
  49.0 2.9 %collective-permute-start.11 = (bf16[256,1024]{1,0:T(8,128)(2,1)S(1)}, bf16[256,1024]{1,0:T(8,128)(2,1)S(1)}, u32[]{:S(2)}, u32[]{:S(2)}) collective-permute-start(bf16[256,1024]{1,0:T(8,128)(2,1)S(1)} %get-tuple-element.49), channel_id=1, source_target_pairs={{0,8},{1,9},{2,10},{3,11},{4,12},{5,13},{6,14},{7,15},{8,0},{9,1},... | collective-permute-start | bytes 1572872 | tf_op jit(solution)/shard_map/ppermute | solution.py:94
  52.1 9.3 %collective-permute-start.12 = (bf16[128,1024]{1,0:T(8,128)(2,1)S(1)}, bf16[128,1024]{1,0:T(8,128)(2,1)S(1)}, u32[]{:S(2)}, u32[]{:S(2)}) collective-permute-start(bf16[128,1024]{1,0:T(8,128)(2,1)S(1)} %slice.44), channel_id=1, source_target_pairs={{0,2},{1,3},{2,0},{3,1},{4,6},{5,7},{6,4},{7,5},{8,10},{9,11},{10,... | collective-permute-start | bytes 786440 | tf_op jit(solution)/shard_map/ppermute | solution.py:94
  52.2 3.7 %collective-permute-start.18 = (bf16[256,512]{1,0:T(8,128)(2,1)S(1)}, bf16[256,512]{1,0:T(8,128)(2,1)S(1)}, u32[]{:S(2)}, u32[]{:S(2)}) collective-permute-start(bf16[256,512]{1,0:T(8,128)(2,1)S(1)} %get-tuple-element.65), channel_id=1, source_target_pairs={{0,8},{1,9},{2,10},{3,11},{4,12},{5,13},{6,14},{7,15},{8,0},{9,1},... | collective-permute-start | bytes 786440 | tf_op jit(solution)/shard_map/ppermute | solution.py:94
  52.3 10.5 %collective-permute-start.16 = (bf16[256,128]{1,0:T(8,128)(2,1)S(1)}, bf16[256,128]{1,0:T(8,128)(2,1)S(1)}, u32[]{:S(2)}, u32[]{:S(2)}) collective-permute-start(bf16[256,128]{1,0:T(8,128)(2,1)S(1)} %get-tuple-element.58), channel_id=1, source_target_pairs={{0,2},{1,3},{2,0},{3,1},{4,6},{5,7},{6,4},{7,5},{8,10},{9,11},{10,... | collective-permute-start | bytes 196616 | tf_op jit(solution)/shard_map/ppermute | solution.py:94
  54.2 8.6 %collective-permute-start.15 = (bf16[256,128]{1,0:T(8,128)(2,1)S(1)}, bf16[256,128]{1,0:T(8,128)(2,1)S(1)}, u32[]{:S(2)}, u32[]{:S(2)}) collective-permute-start(bf16[256,128]{1,0:T(8,128)(2,1)S(1)} %get-tuple-element.56), channel_id=1, source_target_pairs={{0,16},{1,17},{2,18},{3,19},{4,20},{5,21},{6,22},{7,23},{8,24},{9,... | collective-permute-start | bytes 196616 | tf_op jit(solution)/shard_map/ppermute | solution.py:94
  54.7 9.1 %collective-permute-start.17 = (bf16[256,128]{1,0:T(8,128)(2,1)S(1)}, bf16[256,128]{1,0:T(8,128)(2,1)S(1)}, u32[]{:S(2)}, u32[]{:S(2)}) collective-permute-start(bf16[256,128]{1,0:T(8,128)(2,1)S(1)} %get-tuple-element.59), channel_id=1, source_target_pairs={{0,18},{1,19},{2,16},{3,17},{4,22},{5,23},{6,20},{7,21},{8,26},{9,... | collective-permute-start | bytes 196616 | tf_op jit(solution)/shard_map/ppermute | solution.py:94
  55.9 9.4 %collective-permute-start.19 = (bf16[128,512]{1,0:T(8,128)(2,1)S(1)}, bf16[128,512]{1,0:T(8,128)(2,1)S(1)}, u32[]{:S(2)}, u32[]{:S(2)}) collective-permute-start(bf16[128,512]{1,0:T(8,128)(2,1)S(1)} %slice.45), channel_id=1, source_target_pairs={{0,2},{1,3},{2,0},{3,1},{4,6},{5,7},{6,4},{7,5},{8,10},{9,11},{10,... | collective-permute-start | bytes 393224 | tf_op jit(solution)/shard_map/ppermute | solution.py:94
  (1 other events, 1.1 us)

commit v9 on v8

--- a/solution.py
+++ b/solution.py
@@ -13,7 +13,7 @@
 ANY = pl.BlockSpec(memory_space=pl.ANY)
 VMEM = pl.BlockSpec(memory_space=pltpu.VMEM)
 F32 = jnp.float32
-SMALL, LARGE, LAST = 1, 50000000000, 20000000000
+SMALL, LARGE, LAST = 10000000000, 10000000000, 20000000000
 BF16 = jnp.bfloat16
 
 
@@ -315,53 +315,54 @@
     return lax.optimization_barrier((value, *others))[0]
 
 
-CUTS = ((0, 1024), (1024, 1536))
+CUTS = ((0, 768), (768, 1536))
 
 
 def on_device_4x8(queries, keys, values, w_out, cotangent):
     m, o, token = pack(cotangent, ((0, CUTS[-1][1]),))
-    za = send(m, z1=1)
+    probs, mine, bundle = forward(queries, keys, values, w_out)
     ya = send(m, y=1)
-    sa = send(after(za, ya), y=1)
-    at0 = fence(token, sa, cost=20000000000)
-    probs, mine, bundle = forward(queries, keys, values, w_out)
     pair_w = send(after(bundle, ya), z0=1)
-    core_w = send(after(w_out, pair_w), c=1)
     x = send(o, x=1)
+    yx = send(after(x, x), y=1)
+    core_pair_w = send(after(pair_w, yx), c=1)
+    at0 = fence(token, core_pair_w, cost=20000000000)
     x1, x2 = cut(x, CUTS)
     zb1 = send(x1, z1=1)
     sb1 = send(after(zb1, zb1), y=1)
-    at1 = fence(at0, core_w, sb1, cost=1)
     whole = w_out.shape[1]
     att = jnp.concatenate([mine, pair_w[:, whole : whole + HD], pair_w[:, whole + HD :]])
-    att_x = send(att, x=1)
+    att_x = send(after(att, ya), x=1)
     own = mine
-    yx = send(x, y=1)
-    core_pair_w = send(after(pair_w, za), c=1)
+    za = send(m, z1=1)
+    sa = send(za, y=1)
+    zb2 = send(after(x2, yx), z1=1)
+    sb2 = send(zb2, y=1)
+    core_w = send(after(w_out, pair_w), c=1)
     w_all = [w_out, pair_w, core_w, core_pair_w]
+    own = after(mine, yx, sa, core_pair_w)
     blocks = [(m, 0), (ya, 0), (za, 0), (sa, 0), (x, 0), (yx, 0), (zb1, 0), (sb1, 0)]
     keep1, give1, d = products(
         CUTS[0], blocks, w_all, [own, att_x], token, None, False
     )
-    got1 = send(after(give1, att_x, zb1), c=1)
-    total1 = keep1 + got1.astype(F32)
-    to_pair1 = total1[HD:].astype(BF16)
-    pair1 = send(to_pair1, z0=1)
-    queries = after(queries, at1, pair1)
-    own = mine
-    zb2 = send(after(x2, yx), z1=1)
-    sb2 = send(zb2, y=1)
     blocks = [(m, 0), (ya, 0), (za, 0), (sa, 0), (x, 0), (yx, 0), (zb2, 0), (sb2, 0)]
     keep2, give2, d, to_x, to_z, to_xz = products(
         CUTS[1], blocks, w_all, [own, att_x], token, d, True
     )
-    from_x = send(after(to_x, at1), x=1)
+    got1 = send(after(give1, att_x, zb1, give1), c=1)
+    total1 = keep1 + got1.astype(F32)
+    to_pair1 = total1[HD:].astype(BF16)
+    got2 = send(after(give2, to_pair1, sb1), c=1)
+    at1 = fence(at0, sb1, got2, cost=1)
+    at2 = fence(at1, zb1, to_pair1, cost=20000000000)
+    pair1 = send(after(to_pair1, to_pair1), z0=1)
+    queries = after(queries, pair1)
+    from_x = send(to_x, x=1)
     from_z = send(after(to_z, give1), z0=1)
     from_xz = send(to_xz, x=1, z0=1)
     *grads, end = backward(
-        at1, queries, keys, values, probs, d, from_x, from_z, from_xz
-    )
-    got2 = send(after(give2, to_pair1), c=1)
+        at2, queries, keys, values, probs, d, from_x, from_z, from_xz
+    )
     total2 = keep2 + got2.astype(F32)
     to_pair2 = total2[HD:].astype(BF16)
     pair2 = send(to_pair2, z0=1)

time: 66.3 us -> 63.9 us (0.964)
  waiting for transfers between devices: 34.6 us -> 29.6 us
  starting transfers between devices: 23.9 us -> 26.6 us
    ppermute x20, waiting for transfers between devices: 34.6 us -> 29.6 us  [send(): return lax.ppermute(value, AXES, flip(**bits))]
    ppermute x20, starting transfers between devices: 23.9 us -> 26.6 us  [send(): return lax.ppermute(value, AXES, flip(**bits))]
    pallas_call x8 -> x9, Pallas kernels: 5.38 us -> 5.4 us  [call(): pl.pallas_call(kernel, out_shape=[jax.ShapeDtypeStruct(shape, kind) for s...]
  transfers between devices with their start and end apart: 20 -> 20, of which waited for: 9 -> 10; matrix products, arithmetic and copies ran while one was open for 0% -> 0% of each run, Pallas kernels for 7% -> 7%
where the time goes in v9:
time: 63.9 us; the launch traced here: 63.8 us
  waiting for transfers between devices  29.6 us (46%)
  starting transfers between devices  26.6 us (42%)
  Pallas kernels  5.4 us (8%)
  local copies, waits for them, and re-layouts  1.22 us (2%)
  between operations  0.77 us (1%)
    ppermute x20, waiting for transfers between devices, send(): return lax.ppermute(value, AXES, flip(**bits))  29.6 us
    ppermute x20, starting transfers between devices, send(): return lax.ppermute(value, AXES, flip(**bits))  26.6 us
    pallas_call x9, Pallas kernels, call(): pl.pallas_call(kernel, out_shape=[jax.ShapeDtypeStruct(shape, kind) for s...  5.4 us
  transfers between devices with their start and end apart: 20, of which 10 were waited for; matrix products, arithmetic and copies ran while one was open for 0% of the time, Pallas kernels for 7%

profile of v9, /device:TPU:0, one launch (start us, length us, event | category | flops | bytes accessed | tf_op | source)
XLA Modules:
  0.0 63.8 jit_solution(10382822197741597)
XLA Ops:
  0.6 1.1 %copy-done = bf16[64,6144]{1,0:T(8,128)(2,1)S(1)} copy-done((bf16[64,6144]{1,0:T(8,128)(2,1)S(1)}, bf16[64,6144]{1,0:T(8,128)(2,1)}, u32[]{:S(2)}) %copy-start) | copy-done | bytes 786456
  1.9 4.1 %collective-permute-start.7 = (bf16[64,3072]{1,0:T(8,128)(2,1)S(1)}, bf16[64,3072]{1,0:T(8,128)(2,1)S(1)}, u32[]{:S(2)}, u32[]{:S(2)}) collective-permute-start(bf16[64,3072]{1,0:T(8,128)(2,1)S(1)} %get-tuple-element.40.refs_1_), channel_id=1, source_target_pairs={{0,4},{1,5},{2,6},{3,7},{4,0},{5,1},{6,2},{7,3},{8,12},{9,13},{10,... | collective-permute-start | bytes 1179656 | tf_op jit(solution)/shard_map/ppermute | solution.py:94
  6.0 1.5 %collective-permute-start = (bf16[64,3072]{1,0:T(8,128)(2,1)S(1)}, bf16[64,3072]{1,0:T(8,128)(2,1)S(1)}, u32[]{:S(2)}, u32[]{:S(2)}) collective-permute-start(bf16[64,3072]{1,0:T(8,128)(2,1)S(1)} %get-tuple-element.40.refs_1_), channel_id=1, source_target_pairs={{0,1},{1,0},{2,3},{3,2},{4,5},{5,4},{6,7},{7,6},{8,9},{9,8},{10,11... | collective-permute-start | bytes 1179656 | tf_op jit(solution)/shard_map/ppermute | solution.py:94
  7.5 1.5 %collective-permute-start.2 = (bf16[64,3072]{1,0:T(8,128)(2,1)S(1)}, bf16[64,3072]{1,0:T(8,128)(2,1)S(1)}, u32[]{:S(2)}, u32[]{:S(2)}) collective-permute-start(bf16[64,3072]{1,0:T(8,128)(2,1)S(1)} %get-tuple-element.42), channel_id=1, source_target_pairs={{0,16},{1,17},{2,18},{3,19},{4,20},{5,21},{6,22},{7,23},{8,24},{9,... | collective-permute-start | bytes 1179656 | tf_op jit(solution)/shard_map/ppermute | solution.py:94
  9.9 7.9 %collective-permute-done.2.refs_5_ = bf16[64,3072]{1,0:T(8,128)(2,1)S(1)} collective-permute-done((bf16[64,3072]{1,0:T(8,128)(2,1)S(1)}, bf16[64,3072]{1,0:T(8,128)(2,1)S(1)}, u32[]{:S(2)}, u32[]{:S(2)}) %collective-permute-start.2) | collective-permute-done | bytes 393248 | tf_op jit(solution)/shard_map/ppermute | solution.py:94
  18.3 1.6 %collective-permute-start.1 = (bf16[128,1792]{1,0:T(8,128)(2,1)S(1)}, bf16[128,1792]{1,0:T(8,128)(2,1)S(1)}, u32[]{:S(2)}, u32[]{:S(2)}) collective-permute-start(bf16[128,1792]{1,0:T(8,128)(2,1)S(1)} %get-tuple-element.41), channel_id=1, source_target_pairs={{0,2},{1,3},{2,0},{3,1},{4,6},{5,7},{6,4},{7,5},{8,10},{9,11},{10,... | collective-permute-start | bytes 1376264 | tf_op jit(solution)/shard_map/ppermute | solution.py:94
  20.3 4.1 %collective-permute-done.7.refs_3_ = bf16[64,3072]{1,0:T(8,128)(2,1)S(1)} collective-permute-done((bf16[64,3072]{1,0:T(8,128)(2,1)S(1)}, bf16[64,3072]{1,0:T(8,128)(2,1)S(1)}, u32[]{:S(2)}, u32[]{:S(2)}) %collective-permute-start.7) | collective-permute-done | bytes 393248 | tf_op jit(solution)/shard_map/ppermute | solution.py:94
  24.4 1.9 %collective-permute-start.8 = (bf16[64,3072]{1,0:T(8,128)(2,1)S(1)}, bf16[64,3072]{1,0:T(8,128)(2,1)S(1)}, u32[]{:S(2)}, u32[]{:S(2)}) collective-permute-start(bf16[64,3072]{1,0:T(8,128)(2,1)S(1)} %collective-permute-done.7.refs_3_), channel_id=1, source_target_pairs={{0,1},{1,0},{2,3},{3,2},{4,5},{5,4},{6,7},{7,6},{8,9},{9,8},{10,11... | collective-permute-start | bytes 1179656 | tf_op jit(solution)/shard_map/ppermute | solution.py:94
  26.3 5.8 %collective-permute-done.5.refs_7_ = bf16[64,1536]{1,0:T(8,128)(2,1)S(1)} collective-permute-done((bf16[64,1536]{1,0:T(8,128)(2,1)S(1)}, bf16[64,1536]{1,0:T(8,128)(2,1)S(1)}, u32[]{:S(2)}, u32[]{:S(2)}) %collective-permute-start.5) | collective-permute-done | bytes 196640 | tf_op jit(solution)/shard_map/ppermute | solution.py:94
  32.1 1.5 %collective-permute-start.6 = (bf16[64,1536]{1,0:T(8,128)(2,1)S(1)}, bf16[64,1536]{1,0:T(8,128)(2,1)S(1)}, u32[]{:S(2)}, u32[]{:S(2)}) collective-permute-start(bf16[64,1536]{1,0:T(8,128)(2,1)S(1)} %collective-permute-done.5.refs_7_), channel_id=1, source_target_pairs={{0,1},{1,0},{2,3},{3,2},{4,5},{5,4},{6,7},{7,6},{8,9},{9,8},{10,11... | collective-permute-start | bytes 589832 | tf_op jit(solution)/shard_map/ppermute | solution.py:94
  33.6 3.4 %collective-permute-start.9 = (bf16[64,1536]{1,0:T(8,128)(2,1)S(1)}, bf16[64,1536]{1,0:T(8,128)(2,1)S(1)}, u32[]{:S(2)}, u32[]{:S(2)}) collective-permute-start(bf16[64,1536]{1,0:T(8,128)(2,1)S(1)} %pad_maximum_fusion.1), channel_id=1, source_target_pairs={{0,4},{1,5},{2,6},{3,7},{4,0},{5,1},{6,2},{7,3},{8,12},{9,13},{10,... | collective-permute-start | bytes 589832 | tf_op jit(solution)/shard_map/ppermute | solution.py:94
  37.0 2.9 %collective-permute-done.1.refs_10_ = bf16[128,1792]{1,0:T(8,128)(2,1)S(1)} collective-permute-done((bf16[128,1792]{1,0:T(8,128)(2,1)S(1)}, bf16[128,1792]{1,0:T(8,128)(2,1)S(1)}, u32[]{:S(2)}, u32[]{:S(2)}) %collective-permute-start.1) | collective-permute-done | bytes 458784 | tf_op jit(solution)/shard_map/ppermute | solution.py:94
  40.4 1.6 %collective-permute-start.12 = (bf16[512,128]{1,0:T(8,128)(2,1)S(1)}, bf16[512,128]{1,0:T(8,128)(2,1)S(1)}, u32[]{:S(2)}, u32[]{:S(2)}) collective-permute-start(bf16[512,128]{1,0:T(8,128)(2,1)S(1)} %pad_maximum_fusion.2), channel_id=1, source_target_pairs={{0,16},{1,17},{2,18},{3,19},{4,20},{5,21},{6,22},{7,23},{8,24},{9,... | collective-permute-start | bytes 393224 | tf_op jit(solution)/shard_map/ppermute | solution.py:94
  43.5 2.3 %collective-permute-done.12.refs_14_ = bf16[512,128]{1,0:T(8,128)(2,1)S(1)} collective-permute-done((bf16[512,128]{1,0:T(8,128)(2,1)S(1)}, bf16[512,128]{1,0:T(8,128)(2,1)S(1)}, u32[]{:S(2)}, u32[]{:S(2)}) %collective-permute-start.12) | collective-permute-done | bytes 131104 | tf_op jit(solution)/shard_map/ppermute | solution.py:94
  45.9 1.0 %products.2 = (f32[256,768]{1,0:T(8,128)S(1)}, bf16[256,768]{1,0:T(8,128)(2,1)S(1)}, f32[512,256]{1,0:T(8,128)S(1)}) custom-call(f32[8,128]{1,0:T(8,128)S(1)} %get-tuple-element.45.token.refs_0_, bf16[64,3072]{1,0:T(8,128)(2,1)S(1)} %get-tuple-element.40.refs_1_, bf16[64,3072]{1,0:T(8,128)(2,1)S(1)} %collective-permute-done.refs_2_, ...), custom_call_target="tpu_custom_call" | custom-call | flops 10000000000 | bytes 1048576 | tf_op jit(solution)/shard_map/products/pallas_call | solution.py:107
  47.0 1.6 %collective-permute-done.10.refs_8_ = bf16[64,1536]{1,0:T(8,128)(2,1)S(1)} collective-permute-done((bf16[64,1536]{1,0:T(8,128)(2,1)S(1)}, bf16[64,1536]{1,0:T(8,128)(2,1)S(1)}, u32[]{:S(2)}, u32[]{:S(2)}) %collective-permute-start.10) | collective-permute-done | bytes 196640 | tf_op jit(solution)/shard_map/ppermute | solution.py:94
  48.6 1.0 %products.3 = (f32[256,768]{1,0:T(8,128)S(1)}, bf16[256,768]{1,0:T(8,128)(2,1)S(1)}, f32[256,128]{1,0:T(8,128)S(1)}, bf16[256,128]{1,0:T(8,128)(2,1)S(1)}, bf16[...) custom-call(f32[8,128]{1,0:T(8,128)S(1)} %get-tuple-element.45.token.refs_0_, ...), custom_call_target="tpu_custom_call" | custom-call | flops 10000000000 | bytes 1048576 | tf_op jit(solution)/shard_map/products/pallas_call | solution.py:107
  49.7 1.9 %collective-permute-start.15 = (bf16[128,768]{1,0:T(8,128)(2,1)S(1)}, bf16[128,768]{1,0:T(8,128)(2,1)S(1)}, u32[]{:S(2)}, u32[]{:S(2)}) collective-permute-start(bf16[128,768]{1,0:T(8,128)(2,1)S(1)} %slice.45), channel_id=1, source_target_pairs={{0,2},{1,3},{2,0},{3,1},{4,6},{5,7},{6,4},{7,5},{8,10},{9,11},{10,... | collective-permute-start | bytes 589832 | tf_op jit(solution)/shard_map/ppermute | solution.py:94
  51.8 1.5 %collective-permute-start.16 = (bf16[256,128]{1,0:T(8,128)(2,1)S(1)}, bf16[256,128]{1,0:T(8,128)(2,1)S(1)}, u32[]{:S(2)}, u32[]{:S(2)}) collective-permute-start(bf16[256,128]{1,0:T(8,128)(2,1)S(1)} %get-tuple-element.64), channel_id=1, source_target_pairs={{0,16},{1,17},{2,18},{3,19},{4,20},{5,21},{6,22},{7,23},{8,24},{9,... | collective-permute-start | bytes 196616 | tf_op jit(solution)/shard_map/ppermute | solution.py:94
  53.3 1.8 %collective-permute-start.18 = (bf16[256,128]{1,0:T(8,128)(2,1)S(1)}, bf16[256,128]{1,0:T(8,128)(2,1)S(1)}, u32[]{:S(2)}, u32[]{:S(2)}) collective-permute-start(bf16[256,128]{1,0:T(8,128)(2,1)S(1)} %get-tuple-element.67), channel_id=1, source_target_pairs={{0,18},{1,19},{2,16},{3,17},{4,22},{5,23},{6,20},{7,21},{8,26},{9,... | collective-permute-start | bytes 196616 | tf_op jit(solution)/shard_map/ppermute | solution.py:94
  55.1 1.8 %collective-permute-done.15.refs_2_ = bf16[128,768]{1,0:T(8,128)(2,1)S(1)} collective-permute-done((bf16[128,768]{1,0:T(8,128)(2,1)S(1)}, bf16[128,768]{1,0:T(8,128)(2,1)S(1)}, u32[]{:S(2)}, u32[]{:S(2)}) %collective-permute-start.15) | collective-permute-done | bytes 196640 | tf_op jit(solution)/shard_map/ppermute | solution.py:94
  57.1 2.0 %collective-permute-start.19 = (bf16[128,768]{1,0:T(8,128)(2,1)S(1)}, bf16[128,768]{1,0:T(8,128)(2,1)S(1)}, u32[]{:S(2)}, u32[]{:S(2)}) collective-permute-start(bf16[128,768]{1,0:T(8,128)(2,1)S(1)} %slice.44), channel_id=1, source_target_pairs={{0,2},{1,3},{2,0},{3,1},{4,6},{5,7},{6,4},{7,5},{8,10},{9,11},{10,... | collective-permute-start | bytes 589832 | tf_op jit(solution)/shard_map/ppermute | solution.py:94
  59.1 1.6 %collective-permute-done.18.from_xz = bf16[256,128]{1,0:T(8,128)(2,1)S(1)} collective-permute-done((bf16[256,128]{1,0:T(8,128)(2,1)S(1)}, bf16[256,128]{1,0:T(8,128)(2,1)S(1)}, u32[]{:S(2)}, u32[]{:S(2)}) %collective-permute-start.18) | collective-permute-done | bytes 65568 | tf_op jit(solution)/shard_map/ppermute | solution.py:94
  60.7 1.5 %backward.1 = (bf16[512,128]{1,0:T(8,128)(2,1)}, bf16[512,128]{1,0:T(8,128)(2,1)}, bf16[512,128]{1,0:T(8,128)(2,1)}, f32[8,128]{1,0:T(8,128)}) custom-call(f32[8,128]{1,0:T(8,128)S(1)} %fence.5.at, bf16[512,128]{1,0:T(8,128)(2,1)S(1)} %copy-done.2, bf16[512,128]{1,0:T(8,128)(2,1)S(1)} %copy-done.3, bf16[512,128]{1,0:T(8,128)(2,1)S(1)} %copy-done.4, ...), custom_call_target="tpu_custom_call" | custom-call | flops 20000000000 | bytes 1048576 | tf_op jit(solution)/shard_map/backward/pallas_call | solution.py:107
  (44 shorter events, 6.0 us)
Async XLA Ops:
  1.8 7.2 %copy-start.1 = (bf16[128,1536]{1,0:T(8,128)(2,1)S(1)}, bf16[128,1536]{1,0:T(8,128)(2,1)}, u32[]{:S(2)}) copy-start(bf16[128,1536]{1,0:T(8,128)(2,1)} %refs_9_.3) | copy-start | bytes 1179652
  1.8 7.2 %copy-start.2 = (bf16[512,128]{1,0:T(8,128)(2,1)S(1)}, bf16[512,128]{1,0:T(8,128)(2,1)}, u32[]{:S(2)}) copy-start(bf16[512,128]{1,0:T(8,128)(2,1)} %q.2) | copy-start | bytes 393220
  1.8 7.2 %copy-start.3 = (bf16[512,128]{1,0:T(8,128)(2,1)S(1)}, bf16[512,128]{1,0:T(8,128)(2,1)}, u32[]{:S(2)}) copy-start(bf16[512,128]{1,0:T(8,128)(2,1)} %k.3) | copy-start | bytes 393220
  1.8 7.2 %copy-start.4 = (bf16[512,128]{1,0:T(8,128)(2,1)S(1)}, bf16[512,128]{1,0:T(8,128)(2,1)}, u32[]{:S(2)}) copy-start(bf16[512,128]{1,0:T(8,128)(2,1)} %v.3) | copy-start | bytes 393220
  1.9 22.6 %collective-permute-start.7 = (bf16[64,3072]{1,0:T(8,128)(2,1)S(1)}, bf16[64,3072]{1,0:T(8,128)(2,1)S(1)}, u32[]{:S(2)}, u32[]{:S(2)}) collective-permute-start(bf16[64,3072]{1,0:T(8,128)(2,1)S(1)} %get-tuple-element.40.refs_1_), channel_id=1, source_target_pairs={{0,4},{1,5},{2,6},{3,7},{4,0},{5,1},{6,2},{7,3},{8,12},{9,13},{10,... | collective-permute-start | bytes 1179656 | tf_op jit(solution)/shard_map/ppermute | solution.py:94
  6.0 12.3 %collective-permute-start = (bf16[64,3072]{1,0:T(8,128)(2,1)S(1)}, bf16[64,3072]{1,0:T(8,128)(2,1)S(1)}, u32[]{:S(2)}, u32[]{:S(2)}) collective-permute-start(bf16[64,3072]{1,0:T(8,128)(2,1)S(1)} %get-tuple-element.40.refs_1_), channel_id=1, source_target_pairs={{0,1},{1,0},{2,3},{3,2},{4,5},{5,4},{6,7},{7,6},{8,9},{9,8},{10,11... | collective-permute-start | bytes 1179656 | tf_op jit(solution)/shard_map/ppermute | solution.py:94
  7.5 10.3 %collective-permute-start.2 = (bf16[64,3072]{1,0:T(8,128)(2,1)S(1)}, bf16[64,3072]{1,0:T(8,128)(2,1)S(1)}, u32[]{:S(2)}, u32[]{:S(2)}) collective-permute-start(bf16[64,3072]{1,0:T(8,128)(2,1)S(1)} %get-tuple-element.42), channel_id=1, source_target_pairs={{0,16},{1,17},{2,18},{3,19},{4,20},{5,21},{6,22},{7,23},{8,24},{9,... | collective-permute-start | bytes 1179656 | tf_op jit(solution)/shard_map/ppermute | solution.py:94
  17.8 15.8 %collective-permute-start.3 = (bf16[64,3072]{1,0:T(8,128)(2,1)S(1)}, bf16[64,3072]{1,0:T(8,128)(2,1)S(1)}, u32[]{:S(2)}, u32[]{:S(2)}) collective-permute-start(bf16[64,3072]{1,0:T(8,128)(2,1)S(1)} %collective-permute-done.2.refs_5_), channel_id=1, source_target_pairs={{0,1},{1,0},{2,3},{3,2},{4,5},{5,4},{6,7},{7,6},{8,9},{9,8},{10,11... | collective-permute-start | bytes 1179656 | tf_op jit(solution)/shard_map/ppermute | solution.py:94
  18.3 21.6 %collective-permute-start.1 = (bf16[128,1792]{1,0:T(8,128)(2,1)S(1)}, bf16[128,1792]{1,0:T(8,128)(2,1)S(1)}, u32[]{:S(2)}, u32[]{:S(2)}) collective-permute-start(bf16[128,1792]{1,0:T(8,128)(2,1)S(1)} %get-tuple-element.41), channel_id=1, source_target_pairs={{0,2},{1,3},{2,0},{3,1},{4,6},{5,7},{6,4},{7,5},{8,10},{9,11},{10,... | collective-permute-start | bytes 1376264 | tf_op jit(solution)/shard_map/ppermute | solution.py:94
  19.9 12.2 %collective-permute-start.5 = (bf16[64,1536]{1,0:T(8,128)(2,1)S(1)}, bf16[64,1536]{1,0:T(8,128)(2,1)S(1)}, u32[]{:S(2)}, u32[]{:S(2)}) collective-permute-start(bf16[64,1536]{1,0:T(8,128)(2,1)S(1)} %pad_maximum_fusion), channel_id=1, source_target_pairs={{0,4},{1,5},{2,6},{3,7},{4,0},{5,1},{6,2},{7,3},{8,12},{9,13},{10,... | collective-permute-start | bytes 589832 | tf_op jit(solution)/shard_map/ppermute | solution.py:94
  24.4 16.0 %collective-permute-start.8 = (bf16[64,3072]{1,0:T(8,128)(2,1)S(1)}, bf16[64,3072]{1,0:T(8,128)(2,1)S(1)}, u32[]{:S(2)}, u32[]{:S(2)}) collective-permute-start(bf16[64,3072]{1,0:T(8,128)(2,1)S(1)} %collective-permute-done.7.refs_3_), channel_id=1, source_target_pairs={{0,1},{1,0},{2,3},{3,2},{4,5},{5,4},{6,7},{7,6},{8,9},{9,8},{10,11... | collective-permute-start | bytes 1179656 | tf_op jit(solution)/shard_map/ppermute | solution.py:94
  32.1 11.4 %collective-permute-start.6 = (bf16[64,1536]{1,0:T(8,128)(2,1)S(1)}, bf16[64,1536]{1,0:T(8,128)(2,1)S(1)}, u32[]{:S(2)}, u32[]{:S(2)}) collective-permute-start(bf16[64,1536]{1,0:T(8,128)(2,1)S(1)} %collective-permute-done.5.refs_7_), channel_id=1, source_target_pairs={{0,1},{1,0},{2,3},{3,2},{4,5},{5,4},{6,7},{7,6},{8,9},{9,8},{10,11... | collective-permute-start | bytes 589832 | tf_op jit(solution)/shard_map/ppermute | solution.py:94
  33.6 9.3 %collective-permute-start.9 = (bf16[64,1536]{1,0:T(8,128)(2,1)S(1)}, bf16[64,1536]{1,0:T(8,128)(2,1)S(1)}, u32[]{:S(2)}, u32[]{:S(2)}) collective-permute-start(bf16[64,1536]{1,0:T(8,128)(2,1)S(1)} %pad_maximum_fusion.1), channel_id=1, source_target_pairs={{0,4},{1,5},{2,6},{3,7},{4,0},{5,1},{6,2},{7,3},{8,12},{9,13},{10,... | collective-permute-start | bytes 589832 | tf_op jit(solution)/shard_map/ppermute | solution.py:94
  39.9 6.0 %collective-permute-start.11 = (bf16[128,1536]{1,0:T(8,128)(2,1)S(1)}, bf16[128,1536]{1,0:T(8,128)(2,1)S(1)}, u32[]{:S(2)}, u32[]{:S(2)}) collective-permute-start(bf16[128,1536]{1,0:T(8,128)(2,1)S(1)} %copy-done.1), channel_id=1, source_target_pairs={{0,8},{1,9},{2,10},{3,11},{4,12},{5,13},{6,14},{7,15},{8,0},{9,1},... | collective-permute-start | bytes 1179656 | tf_op jit(solution)/shard_map/ppermute | solution.py:94
  39.9 3.7 %collective-permute-start.4 = (bf16[128,1792]{1,0:T(8,128)(2,1)S(1)}, bf16[128,1792]{1,0:T(8,128)(2,1)S(1)}, u32[]{:S(2)}, u32[]{:S(2)}) collective-permute-start(bf16[128,1792]{1,0:T(8,128)(2,1)S(1)} %collective-permute-done.1.refs_10_), channel_id=1, source_target_pairs={{0,8},{1,9},{2,10},{3,11},{4,12},{5,13},{6,14},{7,15},{8,0},{9,1},... | collective-permute-start | bytes 1376264 | tf_op jit(solution)/shard_map/ppermute | solution.py:94
  40.4 5.5 %collective-permute-start.12 = (bf16[512,128]{1,0:T(8,128)(2,1)S(1)}, bf16[512,128]{1,0:T(8,128)(2,1)S(1)}, u32[]{:S(2)}, u32[]{:S(2)}) collective-permute-start(bf16[512,128]{1,0:T(8,128)(2,1)S(1)} %pad_maximum_fusion.2), channel_id=1, source_target_pairs={{0,16},{1,17},{2,18},{3,19},{4,20},{5,21},{6,22},{7,23},{8,24},{9,... | collective-permute-start | bytes 393224 | tf_op jit(solution)/shard_map/ppermute | solution.py:94
  42.9 5.7 %collective-permute-start.10 = (bf16[64,1536]{1,0:T(8,128)(2,1)S(1)}, bf16[64,1536]{1,0:T(8,128)(2,1)S(1)}, u32[]{:S(2)}, u32[]{:S(2)}) collective-permute-start(bf16[64,1536]{1,0:T(8,128)(2,1)S(1)} %collective-permute-done.9.refs_7_), channel_id=1, source_target_pairs={{0,1},{1,0},{2,3},{3,2},{4,5},{5,4},{6,7},{7,6},{8,9},{9,8},{10,11... | collective-permute-start | bytes 589832 | tf_op jit(solution)/shard_map/ppermute | solution.py:94
  46.9 2.7 %collective-permute-start.13 = (bf16[256,768]{1,0:T(8,128)(2,1)S(1)}, bf16[256,768]{1,0:T(8,128)(2,1)S(1)}, u32[]{:S(2)}, u32[]{:S(2)}) collective-permute-start(bf16[256,768]{1,0:T(8,128)(2,1)S(1)} %get-tuple-element.56), channel_id=1, source_target_pairs={{0,8},{1,9},{2,10},{3,11},{4,12},{5,13},{6,14},{7,15},{8,0},{9,1},... | collective-permute-start | bytes 1179656 | tf_op jit(solution)/shard_map/ppermute | solution.py:94
  49.7 7.2 %collective-permute-start.15 = (bf16[128,768]{1,0:T(8,128)(2,1)S(1)}, bf16[128,768]{1,0:T(8,128)(2,1)S(1)}, u32[]{:S(2)}, u32[]{:S(2)}) collective-permute-start(bf16[128,768]{1,0:T(8,128)(2,1)S(1)} %slice.45), channel_id=1, source_target_pairs={{0,2},{1,3},{2,0},{3,1},{4,6},{5,7},{6,4},{7,5},{8,10},{9,11},{10,... | collective-permute-start | bytes 589832 | tf_op jit(solution)/shard_map/ppermute | solution.py:94
  51.6 5.3 %collective-permute-start.14 = (bf16[256,768]{1,0:T(8,128)(2,1)S(1)}, bf16[256,768]{1,0:T(8,128)(2,1)S(1)}, u32[]{:S(2)}, u32[]{:S(2)}) collective-permute-start(bf16[256,768]{1,0:T(8,128)(2,1)S(1)} %get-tuple-element.57), channel_id=1, source_target_pairs={{0,8},{1,9},{2,10},{3,11},{4,12},{5,13},{6,14},{7,15},{8,0},{9,1},... | collective-permute-start | bytes 1179656 | tf_op jit(solution)/shard_map/ppermute | solution.py:94
  51.7 7.4 %collective-permute-start.17 = (bf16[256,128]{1,0:T(8,128)(2,1)S(1)}, bf16[256,128]{1,0:T(8,128)(2,1)S(1)}, u32[]{:S(2)}, u32[]{:S(2)}) collective-permute-start(bf16[256,128]{1,0:T(8,128)(2,1)S(1)} %get-tuple-element.66), channel_id=1, source_target_pairs={{0,2},{1,3},{2,0},{3,1},{4,6},{5,7},{6,4},{7,5},{8,10},{9,11},{10,... | collective-permute-start | bytes 196616 | tf_op jit(solution)/shard_map/ppermute | solution.py:94
  51.8 7.3 %collective-permute-start.16 = (bf16[256,128]{1,0:T(8,128)(2,1)S(1)}, bf16[256,128]{1,0:T(8,128)(2,1)S(1)}, u32[]{:S(2)}, u32[]{:S(2)}) collective-permute-start(bf16[256,128]{1,0:T(8,128)(2,1)S(1)} %get-tuple-element.64), channel_id=1, source_target_pairs={{0,16},{1,17},{2,18},{3,19},{4,20},{5,21},{6,22},{7,23},{8,24},{9,... | collective-permute-start | bytes 196616 | tf_op jit(solution)/shard_map/ppermute | solution.py:94
  53.3 7.4 %collective-permute-start.18 = (bf16[256,128]{1,0:T(8,128)(2,1)S(1)}, bf16[256,128]{1,0:T(8,128)(2,1)S(1)}, u32[]{:S(2)}, u32[]{:S(2)}) collective-permute-start(bf16[256,128]{1,0:T(8,128)(2,1)S(1)} %get-tuple-element.67), channel_id=1, source_target_pairs={{0,18},{1,19},{2,16},{3,17},{4,22},{5,23},{6,20},{7,21},{8,26},{9,... | collective-permute-start | bytes 196616 | tf_op jit(solution)/shard_map/ppermute | solution.py:94
  57.1 5.8 %collective-permute-start.19 = (bf16[128,768]{1,0:T(8,128)(2,1)S(1)}, bf16[128,768]{1,0:T(8,128)(2,1)S(1)}, u32[]{:S(2)}, u32[]{:S(2)}) collective-permute-start(bf16[128,768]{1,0:T(8,128)(2,1)S(1)} %slice.44), channel_id=1, source_target_pairs={{0,2},{1,3},{2,0},{3,1},{4,6},{5,7},{6,4},{7,5},{8,10},{9,11},{10,... | collective-permute-start | bytes 589832 | tf_op jit(solution)/shard_map/ppermute | solution.py:94
  (1 other events, 1.1 us)

commit v10 on v9

--- a/solution.py
+++ b/solution.py
@@ -103,12 +103,12 @@
     return pl.multiple_of(index * unit, unit)
 
 
-def call(name, kernel, outs, ins, cost, scratch=()):
+def call(name, kernel, outs, ins, cost, scratch=(), out_space=VMEM):
     return pl.pallas_call(
         kernel,
         out_shape=[jax.ShapeDtypeStruct(shape, kind) for shape, kind in outs],
         in_specs=[VMEM] * len(ins),
-        out_specs=[VMEM] * len(outs),
+        out_specs=[out_space] * len(outs),
         scratch_shapes=list(scratch),
         cost_estimate=pl.CostEstimate(flops=cost, bytes_accessed=1 << 20, transcendentals=0),
         compiler_params=pltpu.CompilerParams(vmem_limit_bytes=16 << 20),
@@ -209,7 +209,7 @@
     at = place()
     whole = w_refs[0].shape[1]
     width = high - low
-    tiles = [(start, min(512, width - start)) for start in range(0, width, 512)]
+    tiles = [(start, min(768, width - start)) for start in range(0, width, 768)]
     rows, parts = [], []
     for n in range(4):
         z1 = 1 - at["z1"] if n // 2 else at["z1"]
@@ -283,16 +283,26 @@
 
 
 def finish_kernel(limits, *refs):
-    out = refs[-1]
+    out, held, sems = refs[-3:]
+    copies = []
     for n, (low, high) in enumerate(limits):
         total, pair = refs[1 + 2 * n], refs[2 + 2 * n]
-        out[:, low:high] = (total[:HD] + pair[...].astype(F32)).astype(BF16)
+        held[:, low:high] = (total[:HD] + pair[...].astype(F32)).astype(BF16)
+        columns = pl.ds(low, high - low)
+        copies.append(
+            pltpu.make_async_copy(held.at[:, columns], out.at[:, columns], sems.at[n])
+        )
+        copies[-1].start()
+    for copy in copies:
+        copy.wait()
 
 
 def finish(token, limits, totals, pairs):
     ins = [token, *(ref for both in zip(totals, pairs) for ref in both)]
-    outs = [((HD, limits[-1][1]), BF16)]
-    return call("finish", functools.partial(finish_kernel, limits), outs, ins, LAST)[0]
+    whole = (HD, limits[-1][1])
+    scratch = [pltpu.VMEM(whole, BF16), pltpu.SemaphoreType.DMA((len(limits),))]
+    kernel = functools.partial(finish_kernel, limits)
+    return call("finish", kernel, [(whole, BF16)], ins, LAST, scratch, ANY)[0]
 
 
 def after(value, *others):

time: 63.9 us -> 63.9 us (level)
  no operation moved by 1% of the time
where the time goes in v10:
time: 63.9 us; the launch traced here: 63.7 us
  waiting for transfers between devices  29.6 us (46%)
  starting transfers between devices  26.6 us (42%)
  Pallas kernels  5.38 us (8%)
  local copies, waits for them, and re-layouts  1.22 us (2%)
  between operations  0.77 us (1%)
    ppermute x20, waiting for transfers between devices, send(): return lax.ppermute(value, AXES, flip(**bits))  29.6 us
    ppermute x20, starting transfers between devices, send(): return lax.ppermute(value, AXES, flip(**bits))  26.6 us
    pallas_call x9, Pallas kernels, call(): pl.pallas_call(kernel, out_shape=[jax.ShapeDtypeStruct(shape, kind) for s...  5.38 us
  transfers between devices with their start and end apart: 20, of which 10 were waited for; matrix products, arithmetic and copies ran while one was open for 0% of the time, Pallas kernels for 7%

profile of v10, /device:TPU:0, one launch (start us, length us, event | category | flops | bytes accessed | tf_op | source)
XLA Modules:
  0.0 63.7 jit_solution(664749452124265421)
XLA Ops:
  0.6 1.1 %copy-done = bf16[64,6144]{1,0:T(8,128)(2,1)S(1)} copy-done((bf16[64,6144]{1,0:T(8,128)(2,1)S(1)}, bf16[64,6144]{1,0:T(8,128)(2,1)}, u32[]{:S(2)}) %copy-start) | copy-done | bytes 786456
  1.9 4.1 %collective-permute-start.7 = (bf16[64,3072]{1,0:T(8,128)(2,1)S(1)}, bf16[64,3072]{1,0:T(8,128)(2,1)S(1)}, u32[]{:S(2)}, u32[]{:S(2)}) collective-permute-start(bf16[64,3072]{1,0:T(8,128)(2,1)S(1)} %get-tuple-element.40.refs_1_), channel_id=1, source_target_pairs={{0,4},{1,5},{2,6},{3,7},{4,0},{5,1},{6,2},{7,3},{8,12},{9,13},{10,... | collective-permute-start | bytes 1179656 | tf_op jit(solution)/shard_map/ppermute | solution.py:94
  6.0 1.5 %collective-permute-start = (bf16[64,3072]{1,0:T(8,128)(2,1)S(1)}, bf16[64,3072]{1,0:T(8,128)(2,1)S(1)}, u32[]{:S(2)}, u32[]{:S(2)}) collective-permute-start(bf16[64,3072]{1,0:T(8,128)(2,1)S(1)} %get-tuple-element.40.refs_1_), channel_id=1, source_target_pairs={{0,1},{1,0},{2,3},{3,2},{4,5},{5,4},{6,7},{7,6},{8,9},{9,8},{10,11... | collective-permute-start | bytes 1179656 | tf_op jit(solution)/shard_map/ppermute | solution.py:94
  7.5 1.5 %collective-permute-start.2 = (bf16[64,3072]{1,0:T(8,128)(2,1)S(1)}, bf16[64,3072]{1,0:T(8,128)(2,1)S(1)}, u32[]{:S(2)}, u32[]{:S(2)}) collective-permute-start(bf16[64,3072]{1,0:T(8,128)(2,1)S(1)} %get-tuple-element.42), channel_id=1, source_target_pairs={{0,16},{1,17},{2,18},{3,19},{4,20},{5,21},{6,22},{7,23},{8,24},{9,... | collective-permute-start | bytes 1179656 | tf_op jit(solution)/shard_map/ppermute | solution.py:94
  9.9 7.9 %collective-permute-done.2.refs_5_ = bf16[64,3072]{1,0:T(8,128)(2,1)S(1)} collective-permute-done((bf16[64,3072]{1,0:T(8,128)(2,1)S(1)}, bf16[64,3072]{1,0:T(8,128)(2,1)S(1)}, u32[]{:S(2)}, u32[]{:S(2)}) %collective-permute-start.2) | collective-permute-done | bytes 393248 | tf_op jit(solution)/shard_map/ppermute | solution.py:94
  18.3 1.6 %collective-permute-start.1 = (bf16[128,1792]{1,0:T(8,128)(2,1)S(1)}, bf16[128,1792]{1,0:T(8,128)(2,1)S(1)}, u32[]{:S(2)}, u32[]{:S(2)}) collective-permute-start(bf16[128,1792]{1,0:T(8,128)(2,1)S(1)} %get-tuple-element.41), channel_id=1, source_target_pairs={{0,2},{1,3},{2,0},{3,1},{4,6},{5,7},{6,4},{7,5},{8,10},{9,11},{10,... | collective-permute-start | bytes 1376264 | tf_op jit(solution)/shard_map/ppermute | solution.py:94
  20.3 4.1 %collective-permute-done.7.refs_3_ = bf16[64,3072]{1,0:T(8,128)(2,1)S(1)} collective-permute-done((bf16[64,3072]{1,0:T(8,128)(2,1)S(1)}, bf16[64,3072]{1,0:T(8,128)(2,1)S(1)}, u32[]{:S(2)}, u32[]{:S(2)}) %collective-permute-start.7) | collective-permute-done | bytes 393248 | tf_op jit(solution)/shard_map/ppermute | solution.py:94
  24.4 1.9 %collective-permute-start.8 = (bf16[64,3072]{1,0:T(8,128)(2,1)S(1)}, bf16[64,3072]{1,0:T(8,128)(2,1)S(1)}, u32[]{:S(2)}, u32[]{:S(2)}) collective-permute-start(bf16[64,3072]{1,0:T(8,128)(2,1)S(1)} %collective-permute-done.7.refs_3_), channel_id=1, source_target_pairs={{0,1},{1,0},{2,3},{3,2},{4,5},{5,4},{6,7},{7,6},{8,9},{9,8},{10,11... | collective-permute-start | bytes 1179656 | tf_op jit(solution)/shard_map/ppermute | solution.py:94
  26.3 5.8 %collective-permute-done.5.refs_7_ = bf16[64,1536]{1,0:T(8,128)(2,1)S(1)} collective-permute-done((bf16[64,1536]{1,0:T(8,128)(2,1)S(1)}, bf16[64,1536]{1,0:T(8,128)(2,1)S(1)}, u32[]{:S(2)}, u32[]{:S(2)}) %collective-permute-start.5) | collective-permute-done | bytes 196640 | tf_op jit(solution)/shard_map/ppermute | solution.py:94
  32.1 1.5 %collective-permute-start.6 = (bf16[64,1536]{1,0:T(8,128)(2,1)S(1)}, bf16[64,1536]{1,0:T(8,128)(2,1)S(1)}, u32[]{:S(2)}, u32[]{:S(2)}) collective-permute-start(bf16[64,1536]{1,0:T(8,128)(2,1)S(1)} %collective-permute-done.5.refs_7_), channel_id=1, source_target_pairs={{0,1},{1,0},{2,3},{3,2},{4,5},{5,4},{6,7},{7,6},{8,9},{9,8},{10,11... | collective-permute-start | bytes 589832 | tf_op jit(solution)/shard_map/ppermute | solution.py:94
  33.6 3.4 %collective-permute-start.9 = (bf16[64,1536]{1,0:T(8,128)(2,1)S(1)}, bf16[64,1536]{1,0:T(8,128)(2,1)S(1)}, u32[]{:S(2)}, u32[]{:S(2)}) collective-permute-start(bf16[64,1536]{1,0:T(8,128)(2,1)S(1)} %pad_maximum_fusion.1), channel_id=1, source_target_pairs={{0,4},{1,5},{2,6},{3,7},{4,0},{5,1},{6,2},{7,3},{8,12},{9,13},{10,... | collective-permute-start | bytes 589832 | tf_op jit(solution)/shard_map/ppermute | solution.py:94
  37.0 2.9 %collective-permute-done.1.refs_10_ = bf16[128,1792]{1,0:T(8,128)(2,1)S(1)} collective-permute-done((bf16[128,1792]{1,0:T(8,128)(2,1)S(1)}, bf16[128,1792]{1,0:T(8,128)(2,1)S(1)}, u32[]{:S(2)}, u32[]{:S(2)}) %collective-permute-start.1) | collective-permute-done | bytes 458784 | tf_op jit(solution)/shard_map/ppermute | solution.py:94
  40.4 1.6 %collective-permute-start.12 = (bf16[512,128]{1,0:T(8,128)(2,1)S(1)}, bf16[512,128]{1,0:T(8,128)(2,1)S(1)}, u32[]{:S(2)}, u32[]{:S(2)}) collective-permute-start(bf16[512,128]{1,0:T(8,128)(2,1)S(1)} %pad_maximum_fusion.2), channel_id=1, source_target_pairs={{0,16},{1,17},{2,18},{3,19},{4,20},{5,21},{6,22},{7,23},{8,24},{9,... | collective-permute-start | bytes 393224 | tf_op jit(solution)/shard_map/ppermute | solution.py:94
  43.5 2.3 %collective-permute-done.12.refs_14_ = bf16[512,128]{1,0:T(8,128)(2,1)S(1)} collective-permute-done((bf16[512,128]{1,0:T(8,128)(2,1)S(1)}, bf16[512,128]{1,0:T(8,128)(2,1)S(1)}, u32[]{:S(2)}, u32[]{:S(2)}) %collective-permute-start.12) | collective-permute-done | bytes 131104 | tf_op jit(solution)/shard_map/ppermute | solution.py:94
  45.9 1.0 %products.2 = (f32[256,768]{1,0:T(8,128)S(1)}, bf16[256,768]{1,0:T(8,128)(2,1)S(1)}, f32[512,256]{1,0:T(8,128)S(1)}) custom-call(f32[8,128]{1,0:T(8,128)S(1)} %get-tuple-element.45.token.refs_0_, bf16[64,3072]{1,0:T(8,128)(2,1)S(1)} %get-tuple-element.40.refs_1_, bf16[64,3072]{1,0:T(8,128)(2,1)S(1)} %collective-permute-done.refs_2_, ...), custom_call_target="tpu_custom_call" | custom-call | flops 10000000000 | bytes 1048576 | tf_op jit(solution)/shard_map/products/pallas_call | solution.py:107
  47.0 1.6 %collective-permute-done.10.refs_8_ = bf16[64,1536]{1,0:T(8,128)(2,1)S(1)} collective-permute-done((bf16[64,1536]{1,0:T(8,128)(2,1)S(1)}, bf16[64,1536]{1,0:T(8,128)(2,1)S(1)}, u32[]{:S(2)}, u32[]{:S(2)}) %collective-permute-start.10) | collective-permute-done | bytes 196640 | tf_op jit(solution)/shard_map/ppermute | solution.py:94
  48.6 1.0 %products.3 = (f32[256,768]{1,0:T(8,128)S(1)}, bf16[256,768]{1,0:T(8,128)(2,1)S(1)}, f32[256,128]{1,0:T(8,128)S(1)}, bf16[256,128]{1,0:T(8,128)(2,1)S(1)}, bf16[...) custom-call(f32[8,128]{1,0:T(8,128)S(1)} %get-tuple-element.45.token.refs_0_, ...), custom_call_target="tpu_custom_call" | custom-call | flops 10000000000 | bytes 1048576 | tf_op jit(solution)/shard_map/products/pallas_call | solution.py:107
  49.7 1.9 %collective-permute-start.15 = (bf16[128,768]{1,0:T(8,128)(2,1)S(1)}, bf16[128,768]{1,0:T(8,128)(2,1)S(1)}, u32[]{:S(2)}, u32[]{:S(2)}) collective-permute-start(bf16[128,768]{1,0:T(8,128)(2,1)S(1)} %slice.45), channel_id=1, source_target_pairs={{0,2},{1,3},{2,0},{3,1},{4,6},{5,7},{6,4},{7,5},{8,10},{9,11},{10,... | collective-permute-start | bytes 589832 | tf_op jit(solution)/shard_map/ppermute | solution.py:94
  51.8 1.5 %collective-permute-start.16 = (bf16[256,128]{1,0:T(8,128)(2,1)S(1)}, bf16[256,128]{1,0:T(8,128)(2,1)S(1)}, u32[]{:S(2)}, u32[]{:S(2)}) collective-permute-start(bf16[256,128]{1,0:T(8,128)(2,1)S(1)} %get-tuple-element.64), channel_id=1, source_target_pairs={{0,16},{1,17},{2,18},{3,19},{4,20},{5,21},{6,22},{7,23},{8,24},{9,... | collective-permute-start | bytes 196616 | tf_op jit(solution)/shard_map/ppermute | solution.py:94
  53.3 1.8 %collective-permute-start.18 = (bf16[256,128]{1,0:T(8,128)(2,1)S(1)}, bf16[256,128]{1,0:T(8,128)(2,1)S(1)}, u32[]{:S(2)}, u32[]{:S(2)}) collective-permute-start(bf16[256,128]{1,0:T(8,128)(2,1)S(1)} %get-tuple-element.67), channel_id=1, source_target_pairs={{0,18},{1,19},{2,16},{3,17},{4,22},{5,23},{6,20},{7,21},{8,26},{9,... | collective-permute-start | bytes 196616 | tf_op jit(solution)/shard_map/ppermute | solution.py:94
  55.2 1.8 %collective-permute-done.15.refs_2_ = bf16[128,768]{1,0:T(8,128)(2,1)S(1)} collective-permute-done((bf16[128,768]{1,0:T(8,128)(2,1)S(1)}, bf16[128,768]{1,0:T(8,128)(2,1)S(1)}, u32[]{:S(2)}, u32[]{:S(2)}) %collective-permute-start.15) | collective-permute-done | bytes 196640 | tf_op jit(solution)/shard_map/ppermute | solution.py:94
  57.1 2.0 %collective-permute-start.19 = (bf16[128,768]{1,0:T(8,128)(2,1)S(1)}, bf16[128,768]{1,0:T(8,128)(2,1)S(1)}, u32[]{:S(2)}, u32[]{:S(2)}) collective-permute-start(bf16[128,768]{1,0:T(8,128)(2,1)S(1)} %slice.44), channel_id=1, source_target_pairs={{0,2},{1,3},{2,0},{3,1},{4,6},{5,7},{6,4},{7,5},{8,10},{9,11},{10,... | collective-permute-start | bytes 589832 | tf_op jit(solution)/shard_map/ppermute | solution.py:94
  59.1 1.6 %collective-permute-done.18.from_xz = bf16[256,128]{1,0:T(8,128)(2,1)S(1)} collective-permute-done((bf16[256,128]{1,0:T(8,128)(2,1)S(1)}, bf16[256,128]{1,0:T(8,128)(2,1)S(1)}, u32[]{:S(2)}, u32[]{:S(2)}) %collective-permute-start.18) | collective-permute-done | bytes 65568 | tf_op jit(solution)/shard_map/ppermute | solution.py:94
  60.7 1.5 %backward.1 = (bf16[512,128]{1,0:T(8,128)(2,1)}, bf16[512,128]{1,0:T(8,128)(2,1)}, bf16[512,128]{1,0:T(8,128)(2,1)}, f32[8,128]{1,0:T(8,128)}) custom-call(f32[8,128]{1,0:T(8,128)S(1)} %fence.5.at, bf16[512,128]{1,0:T(8,128)(2,1)S(1)} %copy-done.2, bf16[512,128]{1,0:T(8,128)(2,1)S(1)} %copy-done.3, bf16[512,128]{1,0:T(8,128)(2,1)S(1)} %copy-done.4, ...), custom_call_target="tpu_custom_call" | custom-call | flops 20000000000 | bytes 1048576 | tf_op jit(solution)/shard_map/backward/pallas_call | solution.py:107
  (44 shorter events, 6.0 us)
Async XLA Ops:
  1.8 7.2 %copy-start.1 = (bf16[128,1536]{1,0:T(8,128)(2,1)S(1)}, bf16[128,1536]{1,0:T(8,128)(2,1)}, u32[]{:S(2)}) copy-start(bf16[128,1536]{1,0:T(8,128)(2,1)} %refs_9_.3) | copy-start | bytes 1179652
  1.8 7.2 %copy-start.2 = (bf16[512,128]{1,0:T(8,128)(2,1)S(1)}, bf16[512,128]{1,0:T(8,128)(2,1)}, u32[]{:S(2)}) copy-start(bf16[512,128]{1,0:T(8,128)(2,1)} %q.2) | copy-start | bytes 393220
  1.8 7.2 %copy-start.3 = (bf16[512,128]{1,0:T(8,128)(2,1)S(1)}, bf16[512,128]{1,0:T(8,128)(2,1)}, u32[]{:S(2)}) copy-start(bf16[512,128]{1,0:T(8,128)(2,1)} %k.3) | copy-start | bytes 393220
  1.8 7.2 %copy-start.4 = (bf16[512,128]{1,0:T(8,128)(2,1)S(1)}, bf16[512,128]{1,0:T(8,128)(2,1)}, u32[]{:S(2)}) copy-start(bf16[512,128]{1,0:T(8,128)(2,1)} %v.3) | copy-start | bytes 393220
  1.9 22.6 %collective-permute-start.7 = (bf16[64,3072]{1,0:T(8,128)(2,1)S(1)}, bf16[64,3072]{1,0:T(8,128)(2,1)S(1)}, u32[]{:S(2)}, u32[]{:S(2)}) collective-permute-start(bf16[64,3072]{1,0:T(8,128)(2,1)S(1)} %get-tuple-element.40.refs_1_), channel_id=1, source_target_pairs={{0,4},{1,5},{2,6},{3,7},{4,0},{5,1},{6,2},{7,3},{8,12},{9,13},{10,... | collective-permute-start | bytes 1179656 | tf_op jit(solution)/shard_map/ppermute | solution.py:94
  6.0 12.3 %collective-permute-start = (bf16[64,3072]{1,0:T(8,128)(2,1)S(1)}, bf16[64,3072]{1,0:T(8,128)(2,1)S(1)}, u32[]{:S(2)}, u32[]{:S(2)}) collective-permute-start(bf16[64,3072]{1,0:T(8,128)(2,1)S(1)} %get-tuple-element.40.refs_1_), channel_id=1, source_target_pairs={{0,1},{1,0},{2,3},{3,2},{4,5},{5,4},{6,7},{7,6},{8,9},{9,8},{10,11... | collective-permute-start | bytes 1179656 | tf_op jit(solution)/shard_map/ppermute | solution.py:94
  7.5 10.3 %collective-permute-start.2 = (bf16[64,3072]{1,0:T(8,128)(2,1)S(1)}, bf16[64,3072]{1,0:T(8,128)(2,1)S(1)}, u32[]{:S(2)}, u32[]{:S(2)}) collective-permute-start(bf16[64,3072]{1,0:T(8,128)(2,1)S(1)} %get-tuple-element.42), channel_id=1, source_target_pairs={{0,16},{1,17},{2,18},{3,19},{4,20},{5,21},{6,22},{7,23},{8,24},{9,... | collective-permute-start | bytes 1179656 | tf_op jit(solution)/shard_map/ppermute | solution.py:94
  17.8 15.8 %collective-permute-start.3 = (bf16[64,3072]{1,0:T(8,128)(2,1)S(1)}, bf16[64,3072]{1,0:T(8,128)(2,1)S(1)}, u32[]{:S(2)}, u32[]{:S(2)}) collective-permute-start(bf16[64,3072]{1,0:T(8,128)(2,1)S(1)} %collective-permute-done.2.refs_5_), channel_id=1, source_target_pairs={{0,1},{1,0},{2,3},{3,2},{4,5},{5,4},{6,7},{7,6},{8,9},{9,8},{10,11... | collective-permute-start | bytes 1179656 | tf_op jit(solution)/shard_map/ppermute | solution.py:94
  18.3 21.6 %collective-permute-start.1 = (bf16[128,1792]{1,0:T(8,128)(2,1)S(1)}, bf16[128,1792]{1,0:T(8,128)(2,1)S(1)}, u32[]{:S(2)}, u32[]{:S(2)}) collective-permute-start(bf16[128,1792]{1,0:T(8,128)(2,1)S(1)} %get-tuple-element.41), channel_id=1, source_target_pairs={{0,2},{1,3},{2,0},{3,1},{4,6},{5,7},{6,4},{7,5},{8,10},{9,11},{10,... | collective-permute-start | bytes 1376264 | tf_op jit(solution)/shard_map/ppermute | solution.py:94
  19.9 12.2 %collective-permute-start.5 = (bf16[64,1536]{1,0:T(8,128)(2,1)S(1)}, bf16[64,1536]{1,0:T(8,128)(2,1)S(1)}, u32[]{:S(2)}, u32[]{:S(2)}) collective-permute-start(bf16[64,1536]{1,0:T(8,128)(2,1)S(1)} %pad_maximum_fusion), channel_id=1, source_target_pairs={{0,4},{1,5},{2,6},{3,7},{4,0},{5,1},{6,2},{7,3},{8,12},{9,13},{10,... | collective-permute-start | bytes 589832 | tf_op jit(solution)/shard_map/ppermute | solution.py:94
  24.4 16.0 %collective-permute-start.8 = (bf16[64,3072]{1,0:T(8,128)(2,1)S(1)}, bf16[64,3072]{1,0:T(8,128)(2,1)S(1)}, u32[]{:S(2)}, u32[]{:S(2)}) collective-permute-start(bf16[64,3072]{1,0:T(8,128)(2,1)S(1)} %collective-permute-done.7.refs_3_), channel_id=1, source_target_pairs={{0,1},{1,0},{2,3},{3,2},{4,5},{5,4},{6,7},{7,6},{8,9},{9,8},{10,11... | collective-permute-start | bytes 1179656 | tf_op jit(solution)/shard_map/ppermute | solution.py:94
  32.1 11.4 %collective-permute-start.6 = (bf16[64,1536]{1,0:T(8,128)(2,1)S(1)}, bf16[64,1536]{1,0:T(8,128)(2,1)S(1)}, u32[]{:S(2)}, u32[]{:S(2)}) collective-permute-start(bf16[64,1536]{1,0:T(8,128)(2,1)S(1)} %collective-permute-done.5.refs_7_), channel_id=1, source_target_pairs={{0,1},{1,0},{2,3},{3,2},{4,5},{5,4},{6,7},{7,6},{8,9},{9,8},{10,11... | collective-permute-start | bytes 589832 | tf_op jit(solution)/shard_map/ppermute | solution.py:94
  33.6 9.3 %collective-permute-start.9 = (bf16[64,1536]{1,0:T(8,128)(2,1)S(1)}, bf16[64,1536]{1,0:T(8,128)(2,1)S(1)}, u32[]{:S(2)}, u32[]{:S(2)}) collective-permute-start(bf16[64,1536]{1,0:T(8,128)(2,1)S(1)} %pad_maximum_fusion.1), channel_id=1, source_target_pairs={{0,4},{1,5},{2,6},{3,7},{4,0},{5,1},{6,2},{7,3},{8,12},{9,13},{10,... | collective-permute-start | bytes 589832 | tf_op jit(solution)/shard_map/ppermute | solution.py:94
  39.9 6.0 %collective-permute-start.11 = (bf16[128,1536]{1,0:T(8,128)(2,1)S(1)}, bf16[128,1536]{1,0:T(8,128)(2,1)S(1)}, u32[]{:S(2)}, u32[]{:S(2)}) collective-permute-start(bf16[128,1536]{1,0:T(8,128)(2,1)S(1)} %copy-done.1), channel_id=1, source_target_pairs={{0,8},{1,9},{2,10},{3,11},{4,12},{5,13},{6,14},{7,15},{8,0},{9,1},... | collective-permute-start | bytes 1179656 | tf_op jit(solution)/shard_map/ppermute | solution.py:94
  39.9 3.7 %collective-permute-start.4 = (bf16[128,1792]{1,0:T(8,128)(2,1)S(1)}, bf16[128,1792]{1,0:T(8,128)(2,1)S(1)}, u32[]{:S(2)}, u32[]{:S(2)}) collective-permute-start(bf16[128,1792]{1,0:T(8,128)(2,1)S(1)} %collective-permute-done.1.refs_10_), channel_id=1, source_target_pairs={{0,8},{1,9},{2,10},{3,11},{4,12},{5,13},{6,14},{7,15},{8,0},{9,1},... | collective-permute-start | bytes 1376264 | tf_op jit(solution)/shard_map/ppermute | solution.py:94
  40.4 5.5 %collective-permute-start.12 = (bf16[512,128]{1,0:T(8,128)(2,1)S(1)}, bf16[512,128]{1,0:T(8,128)(2,1)S(1)}, u32[]{:S(2)}, u32[]{:S(2)}) collective-permute-start(bf16[512,128]{1,0:T(8,128)(2,1)S(1)} %pad_maximum_fusion.2), channel_id=1, source_target_pairs={{0,16},{1,17},{2,18},{3,19},{4,20},{5,21},{6,22},{7,23},{8,24},{9,... | collective-permute-start | bytes 393224 | tf_op jit(solution)/shard_map/ppermute | solution.py:94
  42.9 5.7 %collective-permute-start.10 = (bf16[64,1536]{1,0:T(8,128)(2,1)S(1)}, bf16[64,1536]{1,0:T(8,128)(2,1)S(1)}, u32[]{:S(2)}, u32[]{:S(2)}) collective-permute-start(bf16[64,1536]{1,0:T(8,128)(2,1)S(1)} %collective-permute-done.9.refs_7_), channel_id=1, source_target_pairs={{0,1},{1,0},{2,3},{3,2},{4,5},{5,4},{6,7},{7,6},{8,9},{9,8},{10,11... | collective-permute-start | bytes 589832 | tf_op jit(solution)/shard_map/ppermute | solution.py:94
  46.9 2.7 %collective-permute-start.13 = (bf16[256,768]{1,0:T(8,128)(2,1)S(1)}, bf16[256,768]{1,0:T(8,128)(2,1)S(1)}, u32[]{:S(2)}, u32[]{:S(2)}) collective-permute-start(bf16[256,768]{1,0:T(8,128)(2,1)S(1)} %get-tuple-element.56), channel_id=1, source_target_pairs={{0,8},{1,9},{2,10},{3,11},{4,12},{5,13},{6,14},{7,15},{8,0},{9,1},... | collective-permute-start | bytes 1179656 | tf_op jit(solution)/shard_map/ppermute | solution.py:94
  49.7 7.2 %collective-permute-start.15 = (bf16[128,768]{1,0:T(8,128)(2,1)S(1)}, bf16[128,768]{1,0:T(8,128)(2,1)S(1)}, u32[]{:S(2)}, u32[]{:S(2)}) collective-permute-start(bf16[128,768]{1,0:T(8,128)(2,1)S(1)} %slice.45), channel_id=1, source_target_pairs={{0,2},{1,3},{2,0},{3,1},{4,6},{5,7},{6,4},{7,5},{8,10},{9,11},{10,... | collective-permute-start | bytes 589832 | tf_op jit(solution)/shard_map/ppermute | solution.py:94
  51.7 5.3 %collective-permute-start.14 = (bf16[256,768]{1,0:T(8,128)(2,1)S(1)}, bf16[256,768]{1,0:T(8,128)(2,1)S(1)}, u32[]{:S(2)}, u32[]{:S(2)}) collective-permute-start(bf16[256,768]{1,0:T(8,128)(2,1)S(1)} %get-tuple-element.57), channel_id=1, source_target_pairs={{0,8},{1,9},{2,10},{3,11},{4,12},{5,13},{6,14},{7,15},{8,0},{9,1},... | collective-permute-start | bytes 1179656 | tf_op jit(solution)/shard_map/ppermute | solution.py:94
  51.7 7.4 %collective-permute-start.17 = (bf16[256,128]{1,0:T(8,128)(2,1)S(1)}, bf16[256,128]{1,0:T(8,128)(2,1)S(1)}, u32[]{:S(2)}, u32[]{:S(2)}) collective-permute-start(bf16[256,128]{1,0:T(8,128)(2,1)S(1)} %get-tuple-element.66), channel_id=1, source_target_pairs={{0,2},{1,3},{2,0},{3,1},{4,6},{5,7},{6,4},{7,5},{8,10},{9,11},{10,... | collective-permute-start | bytes 196616 | tf_op jit(solution)/shard_map/ppermute | solution.py:94
  51.8 7.3 %collective-permute-start.16 = (bf16[256,128]{1,0:T(8,128)(2,1)S(1)}, bf16[256,128]{1,0:T(8,128)(2,1)S(1)}, u32[]{:S(2)}, u32[]{:S(2)}) collective-permute-start(bf16[256,128]{1,0:T(8,128)(2,1)S(1)} %get-tuple-element.64), channel_id=1, source_target_pairs={{0,16},{1,17},{2,18},{3,19},{4,20},{5,21},{6,22},{7,23},{8,24},{9,... | collective-permute-start | bytes 196616 | tf_op jit(solution)/shard_map/ppermute | solution.py:94
  53.3 7.4 %collective-permute-start.18 = (bf16[256,128]{1,0:T(8,128)(2,1)S(1)}, bf16[256,128]{1,0:T(8,128)(2,1)S(1)}, u32[]{:S(2)}, u32[]{:S(2)}) collective-permute-start(bf16[256,128]{1,0:T(8,128)(2,1)S(1)} %get-tuple-element.67), channel_id=1, source_target_pairs={{0,18},{1,19},{2,16},{3,17},{4,22},{5,23},{6,20},{7,21},{8,26},{9,... | collective-permute-start | bytes 196616 | tf_op jit(solution)/shard_map/ppermute | solution.py:94
  57.1 5.8 %collective-permute-start.19 = (bf16[128,768]{1,0:T(8,128)(2,1)S(1)}, bf16[128,768]{1,0:T(8,128)(2,1)S(1)}, u32[]{:S(2)}, u32[]{:S(2)}) collective-permute-start(bf16[128,768]{1,0:T(8,128)(2,1)S(1)} %slice.44), channel_id=1, source_target_pairs={{0,2},{1,3},{2,0},{3,1},{4,6},{5,7},{6,4},{7,5},{8,10},{9,11},{10,... | collective-permute-start | bytes 589832 | tf_op jit(solution)/shard_map/ppermute | solution.py:94
  (1 other events, 1.1 us)
